TPU v7x, 256 devices: a whole 4x4x8 slice. The times are simulated.
256 devices in a mesh: grp: 4 (over x_lo, core), blk: 64 (over x_hi, z, y).
Axes of the slice: x: 4 (x_hi: 2, x_lo: 2; x = x_hi * 2 + x_lo), y: 4, z: 8, core: 2. Of those that a mesh axis runs over, the one named last changes fastest.
Arguments:
- image_feat: bfloat16 [16384, 1152], P(('grp', 'blk')), may hold values from -6 to 6
- text_feat: bfloat16 [16384, 1152], P(('grp', 'blk')), may hold values from -6 to 6
- norm_gain: float32 [1152], replicated, may hold values from 0.1 to 1.9
- w_image: bfloat16 [1152, 1152], replicated, may hold values from -1 to 1
- w_text: bfloat16 [1152, 1152], replicated, may hold values from -1 to 1
- log_scale: float32 [1], replicated, may hold values from 2 to 2.7
- bias: float32 [1], replicated, may hold values from -4 to -1
Outputs:
- d_image: bfloat16 [16384, 1152], P(('grp', 'blk'))
- d_text: bfloat16 [16384, 1152], P(('grp', 'blk'))
All inputs are finite; a program needn't handle non-finite values.
Results may differ from a plain program's by a relative error of at most 0.0075.
Values may be sent and summed in bfloat16 or wider, within the bound.
No kernel may reach another device: no remote copies, remote signals or barrier semaphores. Data moves between devices by JAX's collectives and lax.ppermute only.
A program may use at most 128 MiB of HBM per device.

v0:
```python
import jax
import jax.numpy as jnp
from jax import lax
from jax.sharding import PartitionSpec as P


def unit_rows(project):
    length = jnp.sqrt(jnp.sum(project * project, axis=-1, keepdims=True) + 1e-06)
    unit = project / length
    return (unit.astype(jnp.bfloat16), unit, length)


def image_forward(features, norm_gain, weight):
    values = features.astype(jnp.float32)
    center = values - jnp.mean(values, axis=-1, keepdims=True)
    inv_std = lax.rsqrt(jnp.mean(center * center, axis=-1, keepdims=True) + 1e-06)
    normed = center * inv_std
    hidden = (normed * norm_gain).astype(jnp.bfloat16)
    project = jnp.dot(hidden, weight, preferred_element_type=jnp.float32)
    emb, unit, length = unit_rows(project)
    return (emb, unit, length, normed, inv_std)


def text_forward(features, weight):
    project = jnp.dot(features, weight, preferred_element_type=jnp.float32)
    return unit_rows(project)


def unit_backward(grad_unit, unit, length):
    return (grad_unit - unit * jnp.sum(unit * grad_unit, axis=-1, keepdims=True)) / length


def image_backward(grad_unit, unit, length, normed, inv_std, norm_gain, weight):
    grad_proj = unit_backward(grad_unit, unit, length).astype(jnp.bfloat16)
    grad_hidden = jnp.dot(grad_proj, weight.T, preferred_element_type=jnp.float32)
    grad_normed = grad_hidden * norm_gain
    grad_in = inv_std * (
        grad_normed
        - jnp.mean(grad_normed, axis=-1, keepdims=True)
        - normed * jnp.mean(grad_normed * normed, axis=-1, keepdims=True)
    )
    return grad_in.astype(jnp.bfloat16)


def text_backward(grad_unit, unit, length, weight):
    grad_proj = unit_backward(grad_unit, unit, length).astype(jnp.bfloat16)
    return jnp.dot(grad_proj, weight.T, preferred_element_type=jnp.float32).astype(jnp.bfloat16)


def sign_table(row_index, col_index):
    return jnp.where(row_index[:, None] == col_index[None, :], jnp.float32(1.0), jnp.float32(-1.0))


def pair_slope(logits, labels):
    return (-labels * jax.nn.sigmoid(-labels * logits)).astype(jnp.bfloat16)


def shards(image_feat, text_feat, norm_gain, w_image, w_text, log_scale, bias):
    image_emb, image_unit, image_len, normed, inv_std = image_forward(
        image_feat, norm_gain, w_image
    )
    text_emb, text_unit, text_len = text_forward(text_feat, w_text)
    logit_scale = jnp.exp(log_scale[0])
    logit_bias = bias[0]
    row_count = image_feat.shape[0]
    groups = lax.axis_size("grp")
    blocks = lax.axis_size("blk")
    group_here = lax.axis_index("grp")
    block_here = lax.axis_index("blk")
    near_local = jnp.arange(groups * row_count, dtype=jnp.int32)
    near_index = (
        near_local // row_count * blocks + block_here
    ) * row_count + near_local % row_count
    far_base = group_here * blocks * row_count
    near_all = lax.all_gather(image_emb, "grp", axis=0, tiled=True)
    piece_rows = lax.all_gather(text_emb, "blk", axis=0, tiled=True)
    far_index = far_base + jnp.arange(piece_rows.shape[0], dtype=jnp.int32)
    logits = (
        logit_scale * jnp.dot(piece_rows, near_all.T, preferred_element_type=jnp.float32)
        + logit_bias
    )
    make_grad_turned = pair_slope(logits, sign_table(far_index, near_index))
    near_grad = logit_scale * lax.dot_general(
        make_grad_turned, piece_rows, (((0,), (0,)), ((), ())), preferred_element_type=jnp.float32
    )
    image_gu = lax.psum_scatter(near_grad, "grp", scatter_dimension=0, tiled=True)
    text_gu = lax.psum_scatter(
        logit_scale * jnp.dot(make_grad_turned, near_all, preferred_element_type=jnp.float32),
        "blk",
        scatter_dimension=0,
        tiled=True,
    )
    d_image = image_backward(image_gu, image_unit, image_len, normed, inv_std, norm_gain, w_image)
    d_text = text_backward(text_gu, text_unit, text_len, w_text)
    return (d_image, d_text)


def solution(mesh):
    placed = (P(("grp", "blk"), None), P(("grp", "blk"), None), P(), P(), P(), P(), P())
    return jax.shard_map(
        shards,
        mesh=mesh,
        in_specs=placed,
        out_specs=(P(("grp", "blk"), None), P(("grp", "blk"), None)),
        check_vma=False,
    )
```

profile of v0, /device:TPU:32, one launch (start us, length us, event | category | flops | bytes accessed | tf_op | source)
XLA Modules:
  0.0 1093.8 jit_solution(18442994830120103590)
XLA Ops:
  7.2 0.0 copy-start
  7.2 0.0 all-gather.2.cloned.1.call-start
  7.2 2.7 multiply_reduce_fusion.3
  9.9 0.8 fusion.34
  10.7 0.0 all-gather.2.cloned.1.call-update
  10.7 0.0 reduce-scatter.3.cloned.1.call-start
  12.1 1.0 convert_reduce_fusion
  13.2 1.1 fusion.18
  14.3 0.0 copy-done
  14.3 1.6 multiply_reduce_fusion.2
  16.0 0.1 fusion.35
  16.1 8.0 all_gather.7
  24.1 147.3 %all-gather.2.cloned.1.call-done = bf16[4096,1152]{1,0:T(8,128)(2,1)} async-done(((bf16[64,1152]{1,0:T(8,128)(2,1)}), bf16[4096,1152]{1,0:T(8,128)(2,1)}) %all-gather.2.cloned.1.call-update) | async-done | bytes 9437200 | tf_op jit(solution)/shard_map/all_gather | solution.py:76
  171.4 0.0 copy-start.1
  171.4 7.3 fusion.7
  178.7 0.0 copy-start.2
  178.7 1.3 copy-done.2
  180.0 0.0 copy-done.1
  180.0 3.9 convolution_multiply_fusion.2
  183.9 0.0 reduce-scatter.3.cloned.1.call-update
  183.9 0.0 reduce-scatter.5.cloned.1.call-start
  184.0 11.1 %convolution_multiply_fusion = f32[4096,1152]{1,0:T(8,128)} fusion(bf16[4096,256]{1,0:T(8,128)(2,1)} %copy-done.2, bf16[256,1152]{1,0:T(8,128)(2,1)} %all_gather.7, f32[]{:T(128)} %bitcast), kind=kOutput, calls=%fused_computation | convolution fusion | flops 2420637696 | bytes 21561348 | tf_op jit(solution)/shard_map/dot_general | solution.py:88
  195.1 0.0 copy-start.3
  195.1 0.0 copy-start.4
  195.1 0.0 reduce-scatter.5.cloned.1.call-update
  195.1 9.6 reduce-scatter.3.cloned.1.call-done
  204.7 1.2 multiply_reduce_fusion.1
  205.9 0.0 copy-done.3
  205.9 0.0 copy-done.4
  205.9 2.0 fusion.36
  207.9 0.8 fusion.17
  208.7 873.9 %reduce-scatter.5.cloned.1.call-done = f32[64,1152]{1,0:T(8,128)} async-done(((f32[4096,1152]{1,0:T(8,128)}), f32[64,1152]{1,0:T(8,128)}) %reduce-scatter.5.cloned.1.call-update) | async-done | bytes 294928 | tf_op jit(solution)/shard_map/reduce_scatter | solution.py:87
  1082.6 1.2 multiply_reduce_fusion
  1083.8 3.5 convolution_convert_fusion
  (7 shorter events, 0.0 us)
Async XLA Ops:
  7.2 7.1 copy-start
  7.2 164.2 %all-gather.2.cloned.1.call-start = ((), (), s32[]{:S(2)}) async-start(), calls=%async_computation.2 | async-start | bytes 9584640 | tf_op jit(solution)/shard_map/all_gather | solution.py:76
  10.7 194.0 %reduce-scatter.3.cloned.1.call-start = ((), (), s32[]{:S(2)}) async-start(), calls=%async_computation.3 | async-start | bytes 1474560 | tf_op jit(solution)/shard_map/reduce_scatter | solution.py:86
  171.4 8.6 copy-start.1
  178.7 1.3 copy-start.2
  183.9 898.7 %reduce-scatter.5.cloned.1.call-start = ((), (), s32[]{:S(2)}) async-start(), calls=%async_computation.4 | async-start | bytes 19169280 | tf_op jit(solution)/shard_map/reduce_scatter | solution.py:87
  195.1 10.8 copy-start.3
  195.1 10.8 copy-start.4
Sparse Core Ops, SparseCore 0:
  12.3 159.0 all-gather.1
  184.1 20.5 reduce-scatter.2
  210.9 871.7 reduce-scatter.4
where the time goes:
time: 1100 us; the launch traced here: 1090 us
  waiting for transfers between devices  1030 us (94%)
  matrix products  32.1 us (3%)
  between operations  15.2 us (1%)
    reduce_scatter x1, waiting for transfers between devices, shards(): lax.psum_scatter(logit_scale * jnp.dot(make_grad_turned, near_all, prefer...  874 us
    all_gather x1, waiting for transfers between devices, shards(): piece_rows = lax.all_gather(text_emb, 'blk', axis=0, tiled=True)  147 us
  transfers between devices with their start and end apart: 3, of which 3 were waited for; matrix products, arithmetic and copies ran while one was open for 2% of the time, Pallas kernels for 0%

commit v1 on v0

v1 whole, which is shorter than its diff:
```python
import jax
import jax.numpy as jnp
from jax import lax
from jax.experimental import pallas as pl
from jax.experimental.pallas import tpu as pltpu
from jax.sharding import PartitionSpec as P

AXES = ("grp", "blk")
BF = jnp.bfloat16
F32 = jnp.float32
ROWS = 64
LOG2E = 1.4426950408889634


def flat(x, y, z, c):
    return ((((x % 2) * 2 + c) * 2 + x // 2) * 8 + z) * 4 + y


PLACES = [(x, y, z, c) for x in range(4) for y in range(4) for z in range(8) for c in range(2)]


def send(value, target):
    return lax.ppermute(value, AXES, [(flat(*p), flat(*target(*p))) for p in PLACES])


def send_z(value, k):
    return send(value, lambda x, y, z, c: (x, y, (z + k) % 8, c))


def send_core(value):
    return send(value, lambda x, y, z, c: (x, y, z, 1 - c))


def send_xy(value, k, second):
    def target(x, y, z, c):
        if (c == 1) == second:
            return (x, (y + k) % 4, z, c)
        return ((x + k) % 4, y, z, c)

    return send(value, target)


def unit_rows(project):
    length = jnp.sqrt(jnp.sum(project * project, axis=-1, keepdims=True) + 1e-06)
    unit = project / length
    return (unit.astype(BF), unit, length)


def image_forward(features, norm_gain, weight):
    values = features.astype(F32)
    center = values - jnp.mean(values, axis=-1, keepdims=True)
    inv_std = lax.rsqrt(jnp.mean(center * center, axis=-1, keepdims=True) + 1e-06)
    normed = center * inv_std
    hidden = (normed * norm_gain).astype(BF)
    project = jnp.dot(hidden, weight, preferred_element_type=F32)
    emb, unit, length = unit_rows(project)
    return (emb, unit, length, normed, inv_std)


def text_forward(features, weight):
    project = jnp.dot(features, weight, preferred_element_type=F32)
    return unit_rows(project)


def unit_backward(grad_unit, unit, length):
    return (grad_unit - unit * jnp.sum(unit * grad_unit, axis=-1, keepdims=True)) / length


def image_backward(grad_unit, unit, length, normed, inv_std, norm_gain, weight):
    grad_proj = unit_backward(grad_unit, unit, length).astype(BF)
    grad_hidden = jnp.dot(grad_proj, weight.T, preferred_element_type=F32)
    grad_normed = grad_hidden * norm_gain
    grad_in = inv_std * (
        grad_normed
        - jnp.mean(grad_normed, axis=-1, keepdims=True)
        - normed * jnp.mean(grad_normed * normed, axis=-1, keepdims=True)
    )
    return grad_in.astype(BF)


def text_backward(grad_unit, unit, length, weight):
    grad_proj = unit_backward(grad_unit, unit, length).astype(BF)
    return jnp.dot(grad_proj, weight.T, preferred_element_type=F32).astype(BF)


def pair_kernel(scal, i0, i1, i2, i3, t_own, t_sib, gi0, gi1, gi2, gi3, gt_own, gt_sib, img, txt, acc):
    half = t_own.shape[0]
    quarter = i0.shape[0]
    for n, ref in enumerate((i0, i1, i2, i3)):
        img[pl.ds(n * quarter, quarter), :] = ref[...]
    txt[pl.ds(0, half), :] = t_own[...]
    txt[pl.ds(half, half), :] = t_sib[...]
    slope = -scal[0] * LOG2E
    offset = -scal[1] * LOG2E
    images = img[...]
    width = 256
    for n in range(2 * half // width):
        texts = txt[pl.ds(n * width, width), :]
        cosine = lax.dot_general(images, texts, (((1,), (1,)), ((), ())), preferred_element_type=F32)
        power = cosine * slope + offset
        if n == 0:
            row = lax.broadcasted_iota(jnp.int32, power.shape, 0)
            col = lax.broadcasted_iota(jnp.int32, power.shape, 1)
            same = (row == col) & (row < ROWS)
            grad = 1.0 / (1.0 + jnp.exp2(jnp.where(same, -power, power)))
            grad = jnp.where(same, -grad, grad).astype(BF)
        else:
            grad = (1.0 / (1.0 + jnp.exp2(power))).astype(BF)
        part = jnp.dot(grad, texts, preferred_element_type=F32)
        if n == 0:
            acc[...] = part
        else:
            acc[...] += part
        back = lax.dot_general(grad, images, (((0,), (0,)), ((), ())), preferred_element_type=F32)
        if n * width < half:
            gt_own[pl.ds(n * width, width), :] = back
        else:
            gt_sib[pl.ds(n * width - half, width), :] = back.astype(BF)
    gi0[...] = acc[pl.ds(0, quarter), :]
    for n, ref in enumerate((gi1, gi2, gi3)):
        ref[...] = acc[pl.ds((n + 1) * quarter, quarter), :].astype(BF)


def pair_block(scal, images, t_own, t_sib):
    quarter, width = images[0].shape
    half = t_own.shape[0]
    shape = jax.ShapeDtypeStruct
    vmem = pl.BlockSpec(memory_space=pltpu.VMEM)
    return pl.pallas_call(
        pair_kernel,
        out_shape=[shape((quarter, width), F32)]
        + [shape((quarter, width), BF)] * 3
        + [shape((half, width), F32), shape((half, width), BF)],
        in_specs=[pl.BlockSpec(memory_space=pltpu.SMEM)] + [vmem] * 6,
        out_specs=[vmem] * 6,
        scratch_shapes=[
            pltpu.VMEM((4 * quarter, width), BF),
            pltpu.VMEM((2 * half, width), BF),
            pltpu.VMEM((4 * quarter, width), F32),
        ],
        compiler_params=pltpu.CompilerParams(vmem_limit_bytes=48 * 1024 * 1024),
        cost_estimate=pl.CostEstimate(
            flops=6 * 8 * quarter * half * width, bytes_accessed=16 * 1024 * 1024, transcendentals=0
        ),
    )(scal, *images, t_own, t_sib)


def shards(image_feat, text_feat, norm_gain, w_image, w_text, log_scale, bias):
    text_emb, text_unit, text_len = text_forward(text_feat, w_text)
    half = ROWS // 2
    fwd, bwd = [text_emb], [text_emb]
    for _ in range(3):
        fwd.append(send_z(fwd[-1], 1))
        bwd.append(send_z(bwd[-1], -1))
    far_f = send_z(fwd[3][:half], 1)
    far_b = send_z(bwd[3][half:], -1)
    text_own = jnp.concatenate(fwd + bwd[1:] + [far_f, far_b])
    text_sib = send_core(text_own)

    image_emb, image_unit, image_len, normed, inv_std = image_forward(
        image_feat, norm_gain, w_image
    )
    near = jnp.concatenate([image_emb] + [send_xy(image_emb, k, False) for k in (1, -1, 2)])
    images = [near] + [send_xy(near, k, True) for k in (1, -1, 2)]

    logit_scale = jnp.exp(log_scale)
    scal = jnp.concatenate([logit_scale, bias])
    gi0, gi1, gi2, gi3, gt_own, gt_sib = pair_block(scal, images, text_own, text_sib)

    near_sum = gi0
    for part, k in ((gi1, 1), (gi2, -1), (gi3, 2)):
        near_sum = near_sum + send_xy(part, -k, True).astype(F32)
    image_gu = near_sum[:ROWS]
    near_back = near_sum.astype(BF)
    for n, k in ((1, 1), (2, -1), (3, 2)):
        back = send_xy(near_back[n * ROWS : (n + 1) * ROWS], -k, False)
        image_gu = image_gu + back.astype(F32)

    both = gt_own + send_core(gt_sib).astype(F32)
    own, f1, f2, f3, b1, b2, b3, far = [both[n * ROWS : (n + 1) * ROWS] for n in range(8)]

    def ring(parts, far_half, k, low):
        got = send_z(far_half.astype(BF), k).astype(F32)
        if low:
            total = jnp.concatenate([parts[0][:half] + got, parts[0][half:]])
        else:
            total = jnp.concatenate([parts[0][:half], parts[0][half:] + got])
        for nxt in parts[1:]:
            total = nxt + send_z(total.astype(BF), k).astype(F32)
        return send_z(total.astype(BF), k).astype(F32)

    text_gu = own + ring((f3, f2, f1), far[:half], -1, True) + ring((b3, b2, b1), far[half:], 1, False)

    d_image = image_backward(
        logit_scale * image_gu, image_unit, image_len, normed, inv_std, norm_gain, w_image
    )
    d_text = text_backward(logit_scale * text_gu, text_unit, text_len, w_text)
    return (d_image, d_text)


def solution(mesh):
    placed = (P(AXES, None), P(AXES, None), P(), P(), P(), P(), P())
    return jax.shard_map(
        shards,
        mesh=mesh,
        in_specs=placed,
        out_specs=(P(AXES, None), P(AXES, None)),
        check_vma=False,
    )
```

time: 1100 us -> 133 us (0.12)
  waiting for transfers between devices: 1030 us -> 63.9 us
  starting transfers between devices: 0.12 us -> 41.8 us
  matrix products: 32.1 us -> 6.14 us
  Pallas kernels: 0 us -> 13.6 us
  between operations: 15.2 us -> 2.22 us
    reduce_scatter x2 -> x0, waiting for transfers between devices: 884 us -> none  [the longest x1 874 us: shards(): lax.psum_scatter(logit_scale * jnp.dot(make_grad_turned, near_all, prefer...]
    all_gather x1 -> x0, waiting for transfers between devices: 147 us -> none  [shards(): piece_rows = lax.all_gather(text_emb, 'blk', axis=0, tiled=True)]
    ppermute x0 -> x30, waiting for transfers between devices: none -> 63.9 us  [send(): lax.ppermute(value, AXES, [(flat(*p), flat(*target(*p))) for p in PLACES])]
    ppermute x0 -> x30, starting transfers between devices: none -> 41.8 us  [send(): lax.ppermute(value, AXES, [(flat(*p), flat(*target(*p))) for p in PLACES])]
    dot_general x7 -> x4, matrix products: 32.1 us -> 6.14 us  [the longest x1 2.69 us: text_forward(): project = jnp.dot(features, weight, preferred_element_type=F32)]
    pallas_call x0 -> x1, Pallas kernels: none -> 13.6 us  [pair_block(): pl.pallas_call(pair_kernel, out_shape=[shape((quarter, width), F32)] + [s...]
  transfers between devices with their start and end apart: 3 -> 30, of which waited for: 3 -> 21; matrix products, arithmetic and copies ran while one was open for 2% -> 3% of each run, Pallas kernels for 0% -> 0%
where the time goes in v1:
time: 133 us; the launch traced here: 132 us
  waiting for transfers between devices  63.9 us (48%)
  starting transfers between devices  41.8 us (31%)
  Pallas kernels  13.6 us (10%)
  matrix products  6.14 us (5%)
  other arithmetic  2.6 us (2%)
  between operations  2.22 us (2%)
    ppermute x30, waiting for transfers between devices, send(): lax.ppermute(value, AXES, [(flat(*p), flat(*target(*p))) for p in PLACES])  63.9 us
    ppermute x30, starting transfers between devices, send(): lax.ppermute(value, AXES, [(flat(*p), flat(*target(*p))) for p in PLACES])  41.8 us
    pallas_call x1, Pallas kernels, pair_block(): pl.pallas_call(pair_kernel, out_shape=[shape((quarter, width), F32)] + [s...  13.6 us
    dot_general x1, matrix products, text_forward(): project = jnp.dot(features, weight, preferred_element_type=F32)  2.69 us
  transfers between devices with their start and end apart: 30, of which 21 were waited for; matrix products, arithmetic and copies ran while one was open for 3% of the time, Pallas kernels for 0%

profile of v1, /device:TPU:32, one launch (start us, length us, event | category | flops | bytes accessed | tf_op | source)
XLA Modules:
  0.0 131.5 jit_solution(13412560960134433125)
XLA Ops:
  0.6 0.0 copy-start
  0.7 2.7 %multiply_reduce_fusion.2 = (f32[64]{0:T(128)S(1)}, f32[64,1152]{1,0:T(8,128)S(1)}) fusion(bf16[64,1152]{1,0:T(8,128)(2,1)} %param.8, bf16[1152,1152]{1,0:T(8,128)(2,1)} %param.11), kind=kOutput, calls=%fused_computation.37 | convolution fusion | flops 170016704 | bytes 3096832 | tf_op jit(solution)/shard_map/dot_general | solution.py:61
  3.4 0.1 constant_dynamic-update-slice_fusion.8
  3.5 1.9 %collective-permute-start.9 = (bf16[64,1152]{1,0:T(8,128)(2,1)S(1)}, bf16[64,1152]{1,0:T(8,128)(2,1)S(1)}, u32[]{:S(2)}, u32[]{:S(2)}) collective-permute-start(bf16[64,1152]{1,0:T(8,128)(2,1)S(1)} %get-tuple-element.21), channel_id=1, source_target_pairs={{0,28},{64,92},{4,0},{68,64},{8,4},{72,68},{12,8},{76,72},{16,12},... | collective-permute-start | bytes 442376 | tf_op jit(solution)/shard_map/ppermute | solution.py:23
  5.4 0.2 collective-permute-start.6
  5.6 0.1 convert_reduce_fusion
  5.7 0.2 fusion.10
  6.0 0.7 multiply_reduce_fusion.3
  6.7 2.6 %collective-permute-done.9 = bf16[64,1152]{1,0:T(8,128)(2,1)S(1)} collective-permute-done((bf16[64,1152]{1,0:T(8,128)(2,1)S(1)}, bf16[64,1152]{1,0:T(8,128)(2,1)S(1)}, u32[]{:S(2)}, u32[]{:S(2)}) %collective-permute-start.9) | collective-permute-done | bytes 147488 | tf_op jit(solution)/shard_map/ppermute | solution.py:23
  9.3 3.3 %collective-permute-start.10 = (bf16[64,1152]{1,0:T(8,128)(2,1)S(1)}, bf16[64,1152]{1,0:T(8,128)(2,1)S(1)}, u32[]{:S(2)}, u32[]{:S(2)}) collective-permute-start(bf16[64,1152]{1,0:T(8,128)(2,1)S(1)} %collective-permute-done.9), channel_id=1, source_target_pairs={{0,28},{64,92},{4,0},{68,64},{8,4},{72,68},{12,8},{76,72},{16,12},... | collective-permute-start | bytes 442376 | tf_op jit(solution)/shard_map/ppermute | solution.py:23
  12.6 0.5 collective-permute-done.6
  13.1 2.2 %collective-permute-done.10 = bf16[64,1152]{1,0:T(8,128)(2,1)S(1)} collective-permute-done((bf16[64,1152]{1,0:T(8,128)(2,1)S(1)}, bf16[64,1152]{1,0:T(8,128)(2,1)S(1)}, u32[]{:S(2)}, u32[]{:S(2)}) %collective-permute-start.10) | collective-permute-done | bytes 147488 | tf_op jit(solution)/shard_map/ppermute | solution.py:23
  15.3 3.7 %collective-permute-start.11 = (bf16[64,1152]{1,0:T(8,128)(2,1)S(1)}, bf16[64,1152]{1,0:T(8,128)(2,1)S(1)}, u32[]{:S(2)}, u32[]{:S(2)}) collective-permute-start(bf16[64,1152]{1,0:T(8,128)(2,1)S(1)} %collective-permute-done.10), channel_id=1, source_target_pairs={{0,28},{64,92},{4,0},{68,64},{8,4},{72,68},{12,8},{76,72},{16,12},... | collective-permute-start | bytes 442376 | tf_op jit(solution)/shard_map/ppermute | solution.py:23
  19.0 0.4 collective-permute-done.7
  19.5 2.2 %collective-permute-done.11 = bf16[64,1152]{1,0:T(8,128)(2,1)S(1)} collective-permute-done((bf16[64,1152]{1,0:T(8,128)(2,1)S(1)}, bf16[64,1152]{1,0:T(8,128)(2,1)S(1)}, u32[]{:S(2)}, u32[]{:S(2)}) %collective-permute-start.11) | collective-permute-done | bytes 147488 | tf_op jit(solution)/shard_map/ppermute | solution.py:23
  21.7 3.7 %collective-permute-start.13 = (bf16[32,1152]{1,0:T(8,128)(2,1)S(1)}, bf16[32,1152]{1,0:T(8,128)(2,1)S(1)}, u32[]{:S(2)}, u32[]{:S(2)}) collective-permute-start(bf16[32,1152]{1,0:T(8,128)(2,1)S(1)} %slice.82), channel_id=1, source_target_pairs={{0,28},{64,92},{4,0},{68,64},{8,4},{72,68},{12,8},{76,72},{16,12},... | collective-permute-start | bytes 221192 | tf_op jit(solution)/shard_map/ppermute | solution.py:23
  25.4 0.4 collective-permute-done.8
  25.8 0.0 collective-permute-start.12
  25.9 5.5 %collective-permute-done.12 = bf16[32,1152]{1,0:T(8,128)(2,1)S(1)} collective-permute-done((bf16[32,1152]{1,0:T(8,128)(2,1)S(1)}, bf16[32,1152]{1,0:T(8,128)(2,1)S(1)}, u32[]{:S(2)}, u32[]{:S(2)}) %collective-permute-start.12) | collective-permute-done | bytes 73760 | tf_op jit(solution)/shard_map/ppermute | solution.py:23
  31.5 0.1 collective-permute-start.14
  31.6 0.1 fusion.33
  31.7 3.3 %collective-permute-start.2 = (bf16[64,1152]{1,0:T(8,128)(2,1)S(1)}, bf16[64,1152]{1,0:T(8,128)(2,1)S(1)}, u32[]{:S(2)}, u32[]{:S(2)}) collective-permute-start(bf16[64,1152]{1,0:T(8,128)(2,1)S(1)} %fusion.33), channel_id=1, source_target_pairs={{0,2},{64,96},{4,6},{68,100},{8,10},{72,104},{12,14},{76,108},{16,... | collective-permute-start | bytes 442376 | tf_op jit(solution)/shard_map/ppermute | solution.py:23
  35.0 1.1 collective-permute-start.1
  36.1 1.0 collective-permute-start
  37.0 1.4 %collective-permute-done.2 = bf16[64,1152]{1,0:T(8,128)(2,1)S(1)} collective-permute-done((bf16[64,1152]{1,0:T(8,128)(2,1)S(1)}, bf16[64,1152]{1,0:T(8,128)(2,1)S(1)}, u32[]{:S(2)}, u32[]{:S(2)}) %collective-permute-start.2) | collective-permute-done | bytes 147488 | tf_op jit(solution)/shard_map/ppermute | solution.py:23
  38.5 1.9 %collective-permute-done.1 = bf16[64,1152]{1,0:T(8,128)(2,1)S(1)} collective-permute-done((bf16[64,1152]{1,0:T(8,128)(2,1)S(1)}, bf16[64,1152]{1,0:T(8,128)(2,1)S(1)}, u32[]{:S(2)}, u32[]{:S(2)}) %collective-permute-start.1) | collective-permute-done | bytes 147488 | tf_op jit(solution)/shard_map/ppermute | solution.py:23
  40.4 2.0 %collective-permute-done = bf16[64,1152]{1,0:T(8,128)(2,1)S(1)} collective-permute-done((bf16[64,1152]{1,0:T(8,128)(2,1)S(1)}, bf16[64,1152]{1,0:T(8,128)(2,1)S(1)}, u32[]{:S(2)}, u32[]{:S(2)}) %collective-permute-start) | collective-permute-done | bytes 147488 | tf_op jit(solution)/shard_map/ppermute | solution.py:23
  42.5 3.1 %collective-permute-start.5 = (bf16[256,1152]{1,0:T(8,128)(2,1)S(1)}, bf16[256,1152]{1,0:T(8,128)(2,1)S(1)}, u32[]{:S(2)}, u32[]{:S(2)}) collective-permute-start(bf16[256,1152]{1,0:T(8,128)(2,1)S(1)} %pad_maximum_fusion.i0), channel_id=1, source_target_pairs={{0,32},{64,66},{4,36},{68,70},{8,40},{72,74},{12,44},{76,78},{16,4... | collective-permute-start | bytes 1769480 | tf_op jit(solution)/shard_map/ppermute | solution.py:23
  45.6 1.1 collective-permute-start.4
  46.7 0.9 collective-permute-start.3
  48.9 0.1 pad_maximum_fusion.3.scal
  49.0 5.0 %collective-permute-done.5.i3 = bf16[256,1152]{1,0:T(8,128)(2,1)S(1)} collective-permute-done((bf16[256,1152]{1,0:T(8,128)(2,1)S(1)}, bf16[256,1152]{1,0:T(8,128)(2,1)S(1)}, u32[]{:S(2)}, u32[]{:S(2)}) %collective-permute-start.5) | collective-permute-done | bytes 589856 | tf_op jit(solution)/shard_map/ppermute | solution.py:23
  54.0 6.3 %collective-permute-done.4.i2 = bf16[256,1152]{1,0:T(8,128)(2,1)S(1)} collective-permute-done((bf16[256,1152]{1,0:T(8,128)(2,1)S(1)}, bf16[256,1152]{1,0:T(8,128)(2,1)S(1)}, u32[]{:S(2)}, u32[]{:S(2)}) %collective-permute-start.4) | collective-permute-done | bytes 589856 | tf_op jit(solution)/shard_map/ppermute | solution.py:23
  60.4 1.0 copy-done.6
  61.4 13.6 %shard_map.86 = (f32[256,1152]{1,0:T(8,128)S(1)}, bf16[256,1152]{1,0:T(8,128)(2,1)S(1)}, bf16[256,1152]{1,0:T(8,128)(2,1)S(1)}, bf16[256,1152]{1,0:T(8,128)(2,1)...) custom-call(f32[2]{0:T(128)S(1)} %pad_maximum_fusion.3.scal, bf16[256,1152]{1,0:T(8,128)(2,1)S(1)} %pad_maximum_fusion.i0, ...), custom_call_target="tpu_custom_call" | custom-call | flops 7247757312 | bytes 16777216 | tf_op jit(solution)/shard_map/pallas_call | solution.py:129
  75.0 2.6 %collective-permute-start.15 = (bf16[256,1152]{1,0:T(8,128)(2,1)S(1)}, bf16[256,1152]{1,0:T(8,128)(2,1)S(1)}, u32[]{:S(2)}, u32[]{:S(2)}) collective-permute-start(bf16[256,1152]{1,0:T(8,128)(2,1)S(1)} %get-tuple-element.9), channel_id=1, source_target_pairs={{0,160},{64,67},{4,164},{68,71},{8,168},{72,75},{12,172},{76,79},{... | collective-permute-start | bytes 1769480 | tf_op jit(solution)/shard_map/ppermute | solution.py:23
  77.6 2.3 %collective-permute-start.17 = (bf16[256,1152]{1,0:T(8,128)(2,1)S(1)}, bf16[256,1152]{1,0:T(8,128)(2,1)S(1)}, u32[]{:S(2)}, u32[]{:S(2)}) collective-permute-start(bf16[256,1152]{1,0:T(8,128)(2,1)S(1)} %get-tuple-element.11), channel_id=1, source_target_pairs={{0,32},{64,66},{4,36},{68,70},{8,40},{72,74},{12,44},{76,78},{16,4... | collective-permute-start | bytes 1769480 | tf_op jit(solution)/shard_map/ppermute | solution.py:23
  79.9 11.5 %collective-permute-done.15 = bf16[256,1152]{1,0:T(8,128)(2,1)S(1)} collective-permute-done((bf16[256,1152]{1,0:T(8,128)(2,1)S(1)}, bf16[256,1152]{1,0:T(8,128)(2,1)S(1)}, u32[]{:S(2)}, u32[]{:S(2)}) %collective-permute-start.15) | collective-permute-done | bytes 589856 | tf_op jit(solution)/shard_map/ppermute | solution.py:23
  91.4 3.7 %collective-permute-done.16 = bf16[256,1152]{1,0:T(8,128)(2,1)S(1)} collective-permute-done((bf16[256,1152]{1,0:T(8,128)(2,1)S(1)}, bf16[256,1152]{1,0:T(8,128)(2,1)S(1)}, u32[]{:S(2)}, u32[]{:S(2)}) %collective-permute-start.16) | collective-permute-done | bytes 589856 | tf_op jit(solution)/shard_map/ppermute | solution.py:23
  95.0 0.3 fusion.37
  95.3 0.7 collective-permute-start.18
  96.1 1.2 collective-permute-start.20
  97.2 0.4 collective-permute-start.19
  97.7 0.3 fusion.36
  98.0 3.3 %collective-permute-start.22 = (bf16[32,1152]{1,0:T(8,128)(2,1)S(1)}, bf16[32,1152]{1,0:T(8,128)(2,1)S(1)}, u32[]{:S(2)}, u32[]{:S(2)}) collective-permute-start(bf16[32,1152]{1,0:T(8,128)(2,1)S(1)} %get-tuple-element.26), channel_id=1, source_target_pairs={{0,28},{64,92},{4,0},{68,64},{8,4},{72,68},{12,8},{76,72},{16,12},... | collective-permute-start | bytes 221192 | tf_op jit(solution)/shard_map/ppermute | solution.py:23
  101.3 1.5 %collective-permute-done.20 = bf16[64,1152]{1,0:T(8,128)(2,1)S(1)} collective-permute-done((bf16[64,1152]{1,0:T(8,128)(2,1)S(1)}, bf16[64,1152]{1,0:T(8,128)(2,1)S(1)}, u32[]{:S(2)}, u32[]{:S(2)}) %collective-permute-start.20) | collective-permute-done | bytes 147488 | tf_op jit(solution)/shard_map/ppermute | solution.py:23
  102.8 1.5 %collective-permute-done.19 = bf16[64,1152]{1,0:T(8,128)(2,1)S(1)} collective-permute-done((bf16[64,1152]{1,0:T(8,128)(2,1)S(1)}, bf16[64,1152]{1,0:T(8,128)(2,1)S(1)}, u32[]{:S(2)}, u32[]{:S(2)}) %collective-permute-start.19) | collective-permute-done | bytes 147488 | tf_op jit(solution)/shard_map/ppermute | solution.py:23
  104.3 0.2 multiply_reduce_fusion.1
  104.5 1.1 collective-permute-done.26
  105.7 2.2 %collective-permute-start.23 = (bf16[64,1152]{1,0:T(8,128)(2,1)S(1)}, bf16[64,1152]{1,0:T(8,128)(2,1)S(1)}, u32[]{:S(2)}, u32[]{:S(2)}) collective-permute-start(bf16[64,1152]{1,0:T(8,128)(2,1)S(1)} %pad_maximum_fusion.1), channel_id=1, source_target_pairs={{0,28},{64,92},{4,0},{68,64},{8,4},{72,68},{12,8},{76,72},{16,12},... | collective-permute-start | bytes 442376 | tf_op jit(solution)/shard_map/ppermute | solution.py:23
  107.9 0.1 collective-permute-start.27
  108.0 3.6 %collective-permute-done.23 = bf16[64,1152]{1,0:T(8,128)(2,1)S(1)} collective-permute-done((bf16[64,1152]{1,0:T(8,128)(2,1)S(1)}, bf16[64,1152]{1,0:T(8,128)(2,1)S(1)}, u32[]{:S(2)}, u32[]{:S(2)}) %collective-permute-start.23) | collective-permute-done | bytes 147488 | tf_op jit(solution)/shard_map/ppermute | solution.py:23
  111.7 2.3 %collective-permute-start.24 = (bf16[64,1152]{1,0:T(8,128)(2,1)S(1)}, bf16[64,1152]{1,0:T(8,128)(2,1)S(1)}, u32[]{:S(2)}, u32[]{:S(2)}) collective-permute-start(bf16[64,1152]{1,0:T(8,128)(2,1)S(1)} %fusion.13), channel_id=1, source_target_pairs={{0,28},{64,92},{4,0},{68,64},{8,4},{72,68},{12,8},{76,72},{16,12},... | collective-permute-start | bytes 442376 | tf_op jit(solution)/shard_map/ppermute | solution.py:23
  113.9 1.1 fusion.35
  115.0 2.6 %collective-permute-done.24 = bf16[64,1152]{1,0:T(8,128)(2,1)S(1)} collective-permute-done((bf16[64,1152]{1,0:T(8,128)(2,1)S(1)}, bf16[64,1152]{1,0:T(8,128)(2,1)S(1)}, u32[]{:S(2)}, u32[]{:S(2)}) %collective-permute-start.24) | collective-permute-done | bytes 147488 | tf_op jit(solution)/shard_map/ppermute | solution.py:23
  117.6 0.1 fusion.14
  117.6 0.1 collective-permute-start.28
  117.8 2.0 %collective-permute-start.25 = (bf16[64,1152]{1,0:T(8,128)(2,1)S(1)}, bf16[64,1152]{1,0:T(8,128)(2,1)S(1)}, u32[]{:S(2)}, u32[]{:S(2)}) collective-permute-start(bf16[64,1152]{1,0:T(8,128)(2,1)S(1)} %get-tuple-element.22), channel_id=1, source_target_pairs={{0,28},{64,92},{4,0},{68,64},{8,4},{72,68},{12,8},{76,72},{16,12},... | collective-permute-start | bytes 442376 | tf_op jit(solution)/shard_map/ppermute | solution.py:23
  119.8 3.1 %collective-permute-done.28 = bf16[64,1152]{1,0:T(8,128)(2,1)S(1)} collective-permute-done((bf16[64,1152]{1,0:T(8,128)(2,1)S(1)}, bf16[64,1152]{1,0:T(8,128)(2,1)S(1)}, u32[]{:S(2)}, u32[]{:S(2)}) %collective-permute-start.28) | collective-permute-done | bytes 147488 | tf_op jit(solution)/shard_map/ppermute | solution.py:23
  122.9 1.3 collective-permute-start.29
  124.2 0.8 fusion.9
  125.0 4.7 %collective-permute-done.29 = bf16[64,1152]{1,0:T(8,128)(2,1)S(1)} collective-permute-done((bf16[64,1152]{1,0:T(8,128)(2,1)S(1)}, bf16[64,1152]{1,0:T(8,128)(2,1)S(1)}, u32[]{:S(2)}, u32[]{:S(2)}) %collective-permute-start.29) | collective-permute-done | bytes 147488 | tf_op jit(solution)/shard_map/ppermute | solution.py:23
  129.7 0.2 multiply_reduce_fusion
  129.9 1.6 %convolution_convert_fusion = bf16[64,1152]{1,0:T(8,128)(2,1)} fusion(bf16[1152,1152]{1,0:T(8,128)(2,1)S(1)} %copy-done.1, f32[64]{0:T(128)S(1)} %multiply_reduce_fusion, f32[64]{0:T(128)S(1)} %add_sqrt_fusion, f32[512,1152]{1,0:T(8,128)S(1)} %get-tuple-element.17, bf16[64,1152]{1,0:T(8,128)(2,1)S(1)} %collective-permute-done.29, ...), kind=kOutput, calls=%fused_computation.2 | convolution fusion | flops 170680320 | bytes 3687428 | tf_op jit(solution)/shard_map/dot_general | solution.py:83
  (49 shorter events, 0.5 us)
Async XLA Ops:
  0.6 5.3 %copy-start = (bf16[1152,1152]{1,0:T(8,128)(2,1)S(1)}, bf16[1152,1152]{1,0:T(8,128)(2,1)}, u32[]{:S(2)}) copy-start(bf16[1152,1152]{1,0:T(8,128)(2,1)} %param.10) | copy-start | bytes 7962628
  0.6 5.0 %copy-start.3 = (bf16[64,1152]{1,0:T(8,128)(2,1)S(1)}, bf16[64,1152]{1,0:T(8,128)(2,1)}, u32[]{:S(2)}) copy-start(bf16[64,1152]{1,0:T(8,128)(2,1)} %param.7) | copy-start | bytes 442372
  0.7 5.3 %copy-start.5 = (f32[1152]{0:T(1024)S(1)}, f32[1152]{0:T(1024)}, u32[]{:S(2)}) copy-start(f32[1152]{0:T(1024)} %param.9) | copy-start | bytes 13828
  3.5 5.8 %collective-permute-start.9 = (bf16[64,1152]{1,0:T(8,128)(2,1)S(1)}, bf16[64,1152]{1,0:T(8,128)(2,1)S(1)}, u32[]{:S(2)}, u32[]{:S(2)}) collective-permute-start(bf16[64,1152]{1,0:T(8,128)(2,1)S(1)} %get-tuple-element.21), channel_id=1, source_target_pairs={{0,28},{64,92},{4,0},{68,64},{8,4},{72,68},{12,8},{76,72},{16,12},... | collective-permute-start | bytes 442376 | tf_op jit(solution)/shard_map/ppermute | solution.py:23
  5.4 7.7 %collective-permute-start.6 = (bf16[64,1152]{1,0:T(8,128)(2,1)S(1)}, bf16[64,1152]{1,0:T(8,128)(2,1)S(1)}, u32[]{:S(2)}, u32[]{:S(2)}) collective-permute-start(bf16[64,1152]{1,0:T(8,128)(2,1)S(1)} %get-tuple-element.21), channel_id=1, source_target_pairs={{0,4},{64,68},{4,8},{68,72},{8,12},{72,76},{12,16},{76,80},{16,20}... | collective-permute-start | bytes 442376 | tf_op jit(solution)/shard_map/ppermute | solution.py:23
  9.3 6.0 %collective-permute-start.10 = (bf16[64,1152]{1,0:T(8,128)(2,1)S(1)}, bf16[64,1152]{1,0:T(8,128)(2,1)S(1)}, u32[]{:S(2)}, u32[]{:S(2)}) collective-permute-start(bf16[64,1152]{1,0:T(8,128)(2,1)S(1)} %collective-permute-done.9), channel_id=1, source_target_pairs={{0,28},{64,92},{4,0},{68,64},{8,4},{72,68},{12,8},{76,72},{16,12},... | collective-permute-start | bytes 442376 | tf_op jit(solution)/shard_map/ppermute | solution.py:23
  13.1 6.4 %collective-permute-start.7 = (bf16[64,1152]{1,0:T(8,128)(2,1)S(1)}, bf16[64,1152]{1,0:T(8,128)(2,1)S(1)}, u32[]{:S(2)}, u32[]{:S(2)}) collective-permute-start(bf16[64,1152]{1,0:T(8,128)(2,1)S(1)} %collective-permute-done.6), channel_id=1, source_target_pairs={{0,4},{64,68},{4,8},{68,72},{8,12},{72,76},{12,16},{76,80},{16,20}... | collective-permute-start | bytes 442376 | tf_op jit(solution)/shard_map/ppermute | solution.py:23
  15.3 6.4 %collective-permute-start.11 = (bf16[64,1152]{1,0:T(8,128)(2,1)S(1)}, bf16[64,1152]{1,0:T(8,128)(2,1)S(1)}, u32[]{:S(2)}, u32[]{:S(2)}) collective-permute-start(bf16[64,1152]{1,0:T(8,128)(2,1)S(1)} %collective-permute-done.10), channel_id=1, source_target_pairs={{0,28},{64,92},{4,0},{68,64},{8,4},{72,68},{12,8},{76,72},{16,12},... | collective-permute-start | bytes 442376 | tf_op jit(solution)/shard_map/ppermute | solution.py:23
  19.5 6.4 %collective-permute-start.8 = (bf16[64,1152]{1,0:T(8,128)(2,1)S(1)}, bf16[64,1152]{1,0:T(8,128)(2,1)S(1)}, u32[]{:S(2)}, u32[]{:S(2)}) collective-permute-start(bf16[64,1152]{1,0:T(8,128)(2,1)S(1)} %collective-permute-done.7), channel_id=1, source_target_pairs={{0,4},{64,68},{4,8},{68,72},{8,12},{72,76},{12,16},{76,80},{16,20}... | collective-permute-start | bytes 442376 | tf_op jit(solution)/shard_map/ppermute | solution.py:23
  21.7 9.8 %collective-permute-start.13 = (bf16[32,1152]{1,0:T(8,128)(2,1)S(1)}, bf16[32,1152]{1,0:T(8,128)(2,1)S(1)}, u32[]{:S(2)}, u32[]{:S(2)}) collective-permute-start(bf16[32,1152]{1,0:T(8,128)(2,1)S(1)} %slice.82), channel_id=1, source_target_pairs={{0,28},{64,92},{4,0},{68,64},{8,4},{72,68},{12,8},{76,72},{16,12},... | collective-permute-start | bytes 221192 | tf_op jit(solution)/shard_map/ppermute | solution.py:23
  25.8 5.7 %collective-permute-start.12 = (bf16[32,1152]{1,0:T(8,128)(2,1)S(1)}, bf16[32,1152]{1,0:T(8,128)(2,1)S(1)}, u32[]{:S(2)}, u32[]{:S(2)}) collective-permute-start(bf16[32,1152]{1,0:T(8,128)(2,1)S(1)} %slice.81), channel_id=1, source_target_pairs={{0,4},{64,68},{4,8},{68,72},{8,12},{72,76},{12,16},{76,80},{16,20}... | collective-permute-start | bytes 221192 | tf_op jit(solution)/shard_map/ppermute | solution.py:23
  31.5 28.9 %copy-start.4 = (bf16[512,1152]{1,0:T(8,128)(2,1)}, bf16[512,1152]{1,0:T(8,128)(2,1)S(1)}, u32[]{:S(2)}) copy-start(bf16[512,1152]{1,0:T(8,128)(2,1)S(1)} %constant_dynamic-update-slice_fusion.t_own) | copy-start | bytes 3538948
  31.5 28.9 %collective-permute-start.14 = (bf16[512,1152]{1,0:T(8,128)(2,1)S(1)}, bf16[512,1152]{1,0:T(8,128)(2,1)S(1)}, u32[]{:S(2)}, u32[]{:S(2)}) collective-permute-start(bf16[512,1152]{1,0:T(8,128)(2,1)S(1)} %constant_dynamic-update-slice_fusion.t_own), channel_id=1, source_target_pairs={{0,64},{64,0},{4,68},{68,4},{8,72},{72,8},{12,76},{76,12},{16,80},... | collective-permute-start | bytes 3538952 | tf_op jit(solution)/shard_map/ppermute | solution.py:23
  31.7 6.7 %collective-permute-start.2 = (bf16[64,1152]{1,0:T(8,128)(2,1)S(1)}, bf16[64,1152]{1,0:T(8,128)(2,1)S(1)}, u32[]{:S(2)}, u32[]{:S(2)}) collective-permute-start(bf16[64,1152]{1,0:T(8,128)(2,1)S(1)} %fusion.33), channel_id=1, source_target_pairs={{0,2},{64,96},{4,6},{68,100},{8,10},{72,104},{12,14},{76,108},{16,... | collective-permute-start | bytes 442376 | tf_op jit(solution)/shard_map/ppermute | solution.py:23
  35.0 5.4 %collective-permute-start.1 = (bf16[64,1152]{1,0:T(8,128)(2,1)S(1)}, bf16[64,1152]{1,0:T(8,128)(2,1)S(1)}, u32[]{:S(2)}, u32[]{:S(2)}) collective-permute-start(bf16[64,1152]{1,0:T(8,128)(2,1)S(1)} %fusion.33), channel_id=1, source_target_pairs={{0,3},{64,224},{4,7},{68,228},{8,11},{72,232},{12,15},{76,236},{16... | collective-permute-start | bytes 442376 | tf_op jit(solution)/shard_map/ppermute | solution.py:23
  36.1 6.4 %collective-permute-start = (bf16[64,1152]{1,0:T(8,128)(2,1)S(1)}, bf16[64,1152]{1,0:T(8,128)(2,1)S(1)}, u32[]{:S(2)}, u32[]{:S(2)}) collective-permute-start(bf16[64,1152]{1,0:T(8,128)(2,1)S(1)} %fusion.33), channel_id=1, source_target_pairs={{0,1},{64,192},{4,5},{68,196},{8,9},{72,200},{12,13},{76,204},{16,... | collective-permute-start | bytes 442376 | tf_op jit(solution)/shard_map/ppermute | solution.py:23
  42.5 11.6 %collective-permute-start.5 = (bf16[256,1152]{1,0:T(8,128)(2,1)S(1)}, bf16[256,1152]{1,0:T(8,128)(2,1)S(1)}, u32[]{:S(2)}, u32[]{:S(2)}) collective-permute-start(bf16[256,1152]{1,0:T(8,128)(2,1)S(1)} %pad_maximum_fusion.i0), channel_id=1, source_target_pairs={{0,32},{64,66},{4,36},{68,70},{8,40},{72,74},{12,44},{76,78},{16,4... | collective-permute-start | bytes 1769480 | tf_op jit(solution)/shard_map/ppermute | solution.py:23
  45.6 14.8 %collective-permute-start.4 = (bf16[256,1152]{1,0:T(8,128)(2,1)S(1)}, bf16[256,1152]{1,0:T(8,128)(2,1)S(1)}, u32[]{:S(2)}, u32[]{:S(2)}) collective-permute-start(bf16[256,1152]{1,0:T(8,128)(2,1)S(1)} %pad_maximum_fusion.i0), channel_id=1, source_target_pairs={{0,160},{64,67},{4,164},{68,71},{8,168},{72,75},{12,172},{76,79},{... | collective-permute-start | bytes 1769480 | tf_op jit(solution)/shard_map/ppermute | solution.py:23
  46.7 13.7 %collective-permute-start.3 = (bf16[256,1152]{1,0:T(8,128)(2,1)S(1)}, bf16[256,1152]{1,0:T(8,128)(2,1)S(1)}, u32[]{:S(2)}, u32[]{:S(2)}) collective-permute-start(bf16[256,1152]{1,0:T(8,128)(2,1)S(1)} %pad_maximum_fusion.i0), channel_id=1, source_target_pairs={{0,128},{64,65},{4,132},{68,69},{8,136},{72,73},{12,140},{76,77},{... | collective-permute-start | bytes 1769480 | tf_op jit(solution)/shard_map/ppermute | solution.py:23
  60.4 1.0 copy-start.6
  75.0 16.4 %collective-permute-start.15 = (bf16[256,1152]{1,0:T(8,128)(2,1)S(1)}, bf16[256,1152]{1,0:T(8,128)(2,1)S(1)}, u32[]{:S(2)}, u32[]{:S(2)}) collective-permute-start(bf16[256,1152]{1,0:T(8,128)(2,1)S(1)} %get-tuple-element.9), channel_id=1, source_target_pairs={{0,160},{64,67},{4,164},{68,71},{8,168},{72,75},{12,172},{76,79},{... | collective-permute-start | bytes 1769480 | tf_op jit(solution)/shard_map/ppermute | solution.py:23
  77.6 17.4 %collective-permute-start.16 = (bf16[256,1152]{1,0:T(8,128)(2,1)S(1)}, bf16[256,1152]{1,0:T(8,128)(2,1)S(1)}, u32[]{:S(2)}, u32[]{:S(2)}) collective-permute-start(bf16[256,1152]{1,0:T(8,128)(2,1)S(1)} %get-tuple-element.10), channel_id=1, source_target_pairs={{0,128},{64,65},{4,132},{68,69},{8,136},{72,73},{12,140},{76,77},{... | collective-permute-start | bytes 1769480 | tf_op jit(solution)/shard_map/ppermute | solution.py:23
  77.6 17.4 %collective-permute-start.17 = (bf16[256,1152]{1,0:T(8,128)(2,1)S(1)}, bf16[256,1152]{1,0:T(8,128)(2,1)S(1)}, u32[]{:S(2)}, u32[]{:S(2)}) collective-permute-start(bf16[256,1152]{1,0:T(8,128)(2,1)S(1)} %get-tuple-element.11), channel_id=1, source_target_pairs={{0,32},{64,66},{4,36},{68,70},{8,40},{72,74},{12,44},{76,78},{16,4... | collective-permute-start | bytes 1769480 | tf_op jit(solution)/shard_map/ppermute | solution.py:23
  79.9 17.7 %collective-permute-start.21 = (bf16[512,1152]{1,0:T(8,128)(2,1)}, bf16[512,1152]{1,0:T(8,128)(2,1)S(1)}, u32[]{:S(2)}, u32[]{:S(2)}) collective-permute-start(bf16[512,1152]{1,0:T(8,128)(2,1)} %get-tuple-element.13), channel_id=1, source_target_pairs={{0,64},{64,0},{4,68},{68,4},{8,72},{72,8},{12,76},{76,12},{16,80},... | collective-permute-start | bytes 3538952 | tf_op jit(solution)/shard_map/ppermute | solution.py:23
  95.0 2.6 %copy-start.2 = (f32[512,1152]{1,0:T(8,128)S(1)}, f32[512,1152]{1,0:T(8,128)}, u32[]{:S(2)}) copy-start(f32[512,1152]{1,0:T(8,128)} %get-tuple-element.12) | copy-start | bytes 7077892
  95.3 5.9 %collective-permute-start.18 = (bf16[64,1152]{1,0:T(8,128)(2,1)S(1)}, bf16[64,1152]{1,0:T(8,128)(2,1)S(1)}, u32[]{:S(2)}, u32[]{:S(2)}) collective-permute-start(bf16[64,1152]{1,0:T(8,128)(2,1)S(1)} %get-tuple-element.30), channel_id=1, source_target_pairs={{0,3},{64,224},{4,7},{68,228},{8,11},{72,232},{12,15},{76,236},{16... | collective-permute-start | bytes 442376 | tf_op jit(solution)/shard_map/ppermute | solution.py:23
  96.1 6.7 %collective-permute-start.20 = (bf16[64,1152]{1,0:T(8,128)(2,1)S(1)}, bf16[64,1152]{1,0:T(8,128)(2,1)S(1)}, u32[]{:S(2)}, u32[]{:S(2)}) collective-permute-start(bf16[64,1152]{1,0:T(8,128)(2,1)S(1)} %get-tuple-element.31), channel_id=1, source_target_pairs={{0,2},{64,96},{4,6},{68,100},{8,10},{72,104},{12,14},{76,108},{16,... | collective-permute-start | bytes 442376 | tf_op jit(solution)/shard_map/ppermute | solution.py:23
  97.2 7.0 %collective-permute-start.19 = (bf16[64,1152]{1,0:T(8,128)(2,1)S(1)}, bf16[64,1152]{1,0:T(8,128)(2,1)S(1)}, u32[]{:S(2)}, u32[]{:S(2)}) collective-permute-start(bf16[64,1152]{1,0:T(8,128)(2,1)S(1)} %get-tuple-element.32), channel_id=1, source_target_pairs={{0,1},{64,192},{4,5},{68,196},{8,9},{72,200},{12,13},{76,204},{16,... | collective-permute-start | bytes 442376 | tf_op jit(solution)/shard_map/ppermute | solution.py:23
  98.0 6.5 %collective-permute-start.22 = (bf16[32,1152]{1,0:T(8,128)(2,1)S(1)}, bf16[32,1152]{1,0:T(8,128)(2,1)S(1)}, u32[]{:S(2)}, u32[]{:S(2)}) collective-permute-start(bf16[32,1152]{1,0:T(8,128)(2,1)S(1)} %get-tuple-element.26), channel_id=1, source_target_pairs={{0,28},{64,92},{4,0},{68,64},{8,4},{72,68},{12,8},{76,72},{16,12},... | collective-permute-start | bytes 221192 | tf_op jit(solution)/shard_map/ppermute | solution.py:23
  101.3 4.4 %collective-permute-start.26 = (bf16[32,1152]{1,0:T(8,128)(2,1)S(1)}, bf16[32,1152]{1,0:T(8,128)(2,1)S(1)}, u32[]{:S(2)}, u32[]{:S(2)}) collective-permute-start(bf16[32,1152]{1,0:T(8,128)(2,1)S(1)} %get-tuple-element.27), channel_id=1, source_target_pairs={{0,4},{64,68},{4,8},{68,72},{8,12},{72,76},{12,16},{76,80},{16,20}... | collective-permute-start | bytes 221192 | tf_op jit(solution)/shard_map/ppermute | solution.py:23
  105.7 5.9 %collective-permute-start.23 = (bf16[64,1152]{1,0:T(8,128)(2,1)S(1)}, bf16[64,1152]{1,0:T(8,128)(2,1)S(1)}, u32[]{:S(2)}, u32[]{:S(2)}) collective-permute-start(bf16[64,1152]{1,0:T(8,128)(2,1)S(1)} %pad_maximum_fusion.1), channel_id=1, source_target_pairs={{0,28},{64,92},{4,0},{68,64},{8,4},{72,68},{12,8},{76,72},{16,12},... | collective-permute-start | bytes 442376 | tf_op jit(solution)/shard_map/ppermute | solution.py:23
  107.9 7.1 %collective-permute-start.27 = (bf16[64,1152]{1,0:T(8,128)(2,1)S(1)}, bf16[64,1152]{1,0:T(8,128)(2,1)S(1)}, u32[]{:S(2)}, u32[]{:S(2)}) collective-permute-start(bf16[64,1152]{1,0:T(8,128)(2,1)S(1)} %pad_maximum_fusion.2), channel_id=1, source_target_pairs={{0,4},{64,68},{4,8},{68,72},{8,12},{72,76},{12,16},{76,80},{16,20}... | collective-permute-start | bytes 442376 | tf_op jit(solution)/shard_map/ppermute | solution.py:23
  111.7 5.9 %collective-permute-start.24 = (bf16[64,1152]{1,0:T(8,128)(2,1)S(1)}, bf16[64,1152]{1,0:T(8,128)(2,1)S(1)}, u32[]{:S(2)}, u32[]{:S(2)}) collective-permute-start(bf16[64,1152]{1,0:T(8,128)(2,1)S(1)} %fusion.13), channel_id=1, source_target_pairs={{0,28},{64,92},{4,0},{68,64},{8,4},{72,68},{12,8},{76,72},{16,12},... | collective-permute-start | bytes 442376 | tf_op jit(solution)/shard_map/ppermute | solution.py:23
  117.6 12.3 %copy-start.1 = (bf16[1152,1152]{1,0:T(8,128)(2,1)S(1)}, bf16[1152,1152]{1,0:T(8,128)(2,1)}, u32[]{:S(2)}) copy-start(bf16[1152,1152]{1,0:T(8,128)(2,1)} %param.11) | copy-start | bytes 7962628
  117.6 5.2 %collective-permute-start.28 = (bf16[64,1152]{1,0:T(8,128)(2,1)S(1)}, bf16[64,1152]{1,0:T(8,128)(2,1)S(1)}, u32[]{:S(2)}, u32[]{:S(2)}) collective-permute-start(bf16[64,1152]{1,0:T(8,128)(2,1)S(1)} %get-tuple-element.23), channel_id=1, source_target_pairs={{0,4},{64,68},{4,8},{68,72},{8,12},{72,76},{12,16},{76,80},{16,20}... | collective-permute-start | bytes 442376 | tf_op jit(solution)/shard_map/ppermute | solution.py:23
  117.8 7.2 %collective-permute-start.25 = (bf16[64,1152]{1,0:T(8,128)(2,1)S(1)}, bf16[64,1152]{1,0:T(8,128)(2,1)S(1)}, u32[]{:S(2)}, u32[]{:S(2)}) collective-permute-start(bf16[64,1152]{1,0:T(8,128)(2,1)S(1)} %get-tuple-element.22), channel_id=1, source_target_pairs={{0,28},{64,92},{4,0},{68,64},{8,4},{72,68},{12,8},{76,72},{16,12},... | collective-permute-start | bytes 442376 | tf_op jit(solution)/shard_map/ppermute | solution.py:23
  122.9 6.8 %collective-permute-start.29 = (bf16[64,1152]{1,0:T(8,128)(2,1)S(1)}, bf16[64,1152]{1,0:T(8,128)(2,1)S(1)}, u32[]{:S(2)}, u32[]{:S(2)}) collective-permute-start(bf16[64,1152]{1,0:T(8,128)(2,1)S(1)} %fusion.12), channel_id=1, source_target_pairs={{0,4},{64,68},{4,8},{68,72},{8,12},{72,76},{12,16},{76,80},{16,20}... | collective-permute-start | bytes 442376 | tf_op jit(solution)/shard_map/ppermute | solution.py:23

commit v2 on v1

v2 whole, which is shorter than its diff:
```python
import functools

import jax
import jax.numpy as jnp
from jax import lax
from jax.experimental import pallas as pl
from jax.experimental.pallas import tpu as pltpu
from jax.sharding import PartitionSpec as P

AXES = ("grp", "blk")
BF = jnp.bfloat16
F32 = jnp.float32
ROWS = 64
LOG2E = 1.4426950408889634


def flat(x, y, z, c):
    return ((((x % 2) * 2 + c) * 2 + x // 2) * 8 + z) * 4 + y


PLACES = [(x, y, z, c) for x in range(4) for y in range(4) for z in range(8) for c in range(2)]


def send(value, target):
    return lax.ppermute(value, AXES, [(flat(*p), flat(*target(*p))) for p in PLACES])


def send_z(value, k):
    return send(value, lambda x, y, z, c: (x, y, (z + k) % 8, c))


def send_core(value):
    return send(value, lambda x, y, z, c: (x, y, z, 1 - c))


def send_xy(value, k, second):
    def target(x, y, z, c):
        if (c == 1) == second:
            return (x, (y + k) % 4, z, c)
        return ((x + k) % 4, y, z, c)

    return send(value, target)


def unit_rows(project):
    length = jnp.sqrt(jnp.sum(project * project, axis=-1, keepdims=True) + 1e-06)
    unit = project / length
    return (unit.astype(BF), unit, length)


def image_forward(features, norm_gain, weight):
    values = features.astype(F32)
    center = values - jnp.mean(values, axis=-1, keepdims=True)
    inv_std = lax.rsqrt(jnp.mean(center * center, axis=-1, keepdims=True) + 1e-06)
    normed = center * inv_std
    hidden = (normed * norm_gain).astype(BF)
    project = jnp.dot(hidden, weight, preferred_element_type=F32)
    emb, unit, length = unit_rows(project)
    return (emb, unit, length, normed, inv_std)


def text_forward(features, weight):
    project = jnp.dot(features, weight, preferred_element_type=F32)
    return unit_rows(project)


def unit_backward(grad_unit, unit, length):
    return (grad_unit - unit * jnp.sum(unit * grad_unit, axis=-1, keepdims=True)) / length


def image_backward(grad_unit, unit, length, normed, inv_std, norm_gain, weight):
    grad_proj = unit_backward(grad_unit, unit, length).astype(BF)
    grad_hidden = jnp.dot(grad_proj, weight.T, preferred_element_type=F32)
    grad_normed = grad_hidden * norm_gain
    grad_in = inv_std * (
        grad_normed
        - jnp.mean(grad_normed, axis=-1, keepdims=True)
        - normed * jnp.mean(grad_normed * normed, axis=-1, keepdims=True)
    )
    return grad_in.astype(BF)


def text_backward(grad_unit, unit, length, weight):
    grad_proj = unit_backward(grad_unit, unit, length).astype(BF)
    return jnp.dot(grad_proj, weight.T, preferred_element_type=F32).astype(BF)


def pair_kernel(counts, has_diag, scal, *refs):
    refs = list(refs)
    images, texts, img_old, txt_old, img_out, txt_out = [
        [refs.pop(0) for _ in range(n)] for n in counts
    ]
    img, txt, grad = refs

    def spans(group):
        at, places = 0, []
        for ref in group:
            places.append(pl.ds(at, ref.shape[0]))
            at += ref.shape[0]
        return list(zip(group, places))

    for group, whole in ((images, img), (texts, txt)):
        for ref, place in spans(group):
            whole[place, :] = ref[...]
    slope = -scal[0] * LOG2E
    offset = -scal[1] * LOG2E
    width = 256
    for n in range(txt.shape[0] // width):
        cols = pl.ds(n * width, width)
        cosine = lax.dot_general(
            img[...], txt[cols, :], (((1,), (1,)), ((), ())), preferred_element_type=F32
        )
        power = cosine * slope + offset
        if has_diag and n == 0:
            row = lax.broadcasted_iota(jnp.int32, power.shape, 0)
            col = lax.broadcasted_iota(jnp.int32, power.shape, 1)
            same = (row == col) & (row < ROWS)
            value = 1.0 / (1.0 + jnp.exp2(jnp.where(same, -power, power)))
            value = jnp.where(same, -value, value)
        else:
            value = 1.0 / (1.0 + jnp.exp2(power))
        grad[:, cols] = value.astype(BF)
    for n, (ref, place) in enumerate(spans(img_out)):
        value = jnp.dot(grad[place, :], txt[...], preferred_element_type=F32)
        if img_old:
            value = value + img_old[n][...]
        ref[...] = value.astype(ref.dtype)
    for n, (ref, place) in enumerate(spans(txt_out)):
        value = lax.dot_general(
            grad[:, place], img[...], (((0,), (0,)), ((), ())), preferred_element_type=F32
        )
        if n < len(txt_old):
            value = value + txt_old[n][...]
        ref[...] = value.astype(ref.dtype)


def pair_block(scal, images, texts, img_out, txt_out, img_old=(), txt_old=(), has_diag=False):
    width = images[0].shape[1]
    vmem = pl.BlockSpec(memory_space=pltpu.VMEM)
    m, n = sum(v.shape[0] for v in images), sum(v.shape[0] for v in texts)
    operands = [*images, *texts, *img_old, *txt_old]
    outs = [jax.ShapeDtypeStruct((r, width), d) for r, d in [*img_out, *txt_out]]
    counts = tuple(len(v) for v in (images, texts, img_old, txt_old, img_out, txt_out))
    got = pl.pallas_call(
        functools.partial(pair_kernel, counts, has_diag),
        out_shape=outs,
        in_specs=[pl.BlockSpec(memory_space=pltpu.SMEM)] + [vmem] * len(operands),
        out_specs=[vmem] * len(outs),
        scratch_shapes=[
            pltpu.VMEM((m, width), BF),
            pltpu.VMEM((n, width), BF),
            pltpu.VMEM((m, n), BF),
        ],
        compiler_params=pltpu.CompilerParams(vmem_limit_bytes=24 * 1024 * 1024),
        cost_estimate=pl.CostEstimate(flops=1024, bytes_accessed=1024, transcendentals=0),
    )(scal, *operands)
    return got[: len(img_out)], got[len(img_out) :]


def shards(image_feat, text_feat, norm_gain, w_image, w_text, log_scale, bias):
    half = ROWS // 2
    cat = jnp.concatenate
    tie = lax.optimization_barrier
    logit_scale = jnp.exp(log_scale)
    scal = cat([logit_scale, bias])

    text_emb, text_unit, text_len = text_forward(text_feat, w_text)
    f1, b1 = send_z(text_emb, 1), send_z(text_emb, -1)
    f2, b2 = send_z(f1, 1), send_z(b1, -1)
    image_emb, image_unit, image_len, normed, inv_std = image_forward(
        image_feat, norm_gain, w_image
    )
    near = [send_xy(image_emb, k, False) for k in (1, -1, 2)]
    near = cat([image_emb] + near)
    next_p, next_m = [send_xy(near, k, True) for k in (1, -1)]
    across_p = send_xy(next_p[: 2 * ROWS], 1, True)
    across_m = send_xy(next_m[2 * ROWS :], -1, True)
    far_f = send_z(cat([f1, f2[:half]]), 2)
    far_b = send_z(cat([b1, b2[half:]]), -2)
    early = cat([text_emb, f1, b1, f2])
    early_sib = send_core(early)

    sides = [near, next_p, next_m]
    side = 4 * ROWS
    side_acc, early_acc = pair_block(
        scal, sides, [early, early_sib], [(side, F32)] * 3, [(side, F32)] * 2, has_diag=True
    )
    b2, far_f, far_b, across_p, across_m, side_acc, early_acc = tie(
        (b2, far_f, far_b, across_p, across_m, side_acc, early_acc)
    )
    late = cat([b2, far_f, far_b])
    late_sib = send_core(late)
    (across_pg, across_mg), (ge_own, ge_sib, *late_acc) = pair_block(
        scal, [across_p, across_m], [early, early_sib, late, late_sib], [(2 * ROWS, BF)] * 2,
        [(side, F32), (side, BF), (side, F32), (side, F32)], txt_old=early_acc,
    )
    (near_g, next_pg, next_mg), (gl_own, gl_sib) = pair_block(
        scal, sides, [late, late_sib], [(side, F32)] * 3, [(side, F32), (side, BF)],
        img_old=side_acc, txt_old=late_acc,
    )

    across_pg, across_mg = send_xy(across_pg, -1, True), send_xy(across_mg, 1, True)
    across_pg, across_mg, gl_sib = tie((across_pg, across_mg, gl_sib))
    low, high = across_pg.astype(F32), across_mg.astype(F32)
    next_pg = cat([next_pg[: 2 * ROWS] + low, next_pg[2 * ROWS :]]).astype(BF)
    next_mg = cat([next_mg[: 2 * ROWS], next_mg[2 * ROWS :] + high]).astype(BF)
    late_sum = gl_own + send_core(gl_sib).astype(F32)
    early_sum = ge_own + send_core(ge_sib).astype(F32)

    next_pg, next_mg, late_sum, early_sum = tie((next_pg, next_mg, late_sum, early_sum))

    def hop(value, k):
        return send_z(value.astype(BF), k).astype(F32)

    near_sum = near_g
    for part, k in ((next_pg, -1), (next_mg, 1)):
        near_sum = near_sum + send_xy(part, k, True).astype(F32)
    own, s1, s2, s3 = [early_sum[n * ROWS : (n + 1) * ROWS] for n in range(4)]
    s4 = late_sum[:ROWS]
    cut = 2 * ROWS + half
    low, high = hop(late_sum[ROWS:cut], -2), hop(late_sum[cut:], 2)
    near_sum, low, high = tie((near_sum, low, high))

    near_back = near_sum.astype(BF)
    image_gu = near_sum[:ROWS]
    for n, k in ((1, 1), (2, -1), (3, 2)):
        back = send_xy(near_back[n * ROWS : (n + 1) * ROWS], -k, False)
        image_gu = image_gu + back.astype(F32)
    s1, s2 = s1 + low[:ROWS], s2 + high[:ROWS]
    s3 = cat([s3[:half] + low[ROWS:], s3[half:]])
    s4 = cat([s4[:half], s4[half:] + high[ROWS:]])
    text_gu = own + hop(s1, -1) + hop(s2, 1) + hop(s3, -2) + hop(s4, 2)

    d_image = image_backward(
        logit_scale * image_gu, image_unit, image_len, normed, inv_std, norm_gain, w_image
    )
    d_text = text_backward(logit_scale * text_gu, text_unit, text_len, w_text)
    return (d_image, d_text)


def solution(mesh):
    placed = (P(AXES, None), P(AXES, None), P(), P(), P(), P(), P())
    return jax.shard_map(
        shards,
        mesh=mesh,
        in_specs=placed,
        out_specs=(P(AXES, None), P(AXES, None)),
        check_vma=False,
    )
```

time: 133 us -> 102 us (0.77)
  waiting for transfers between devices: 63.9 us -> 37.6 us
  Pallas kernels: 13.6 us -> 11.1 us
    ppermute x30, waiting for transfers between devices: 63.9 us -> 37.6 us  [send(): lax.ppermute(value, AXES, [(flat(*p), flat(*target(*p))) for p in PLACES])]
    pallas_call x1 -> x3, Pallas kernels: 13.6 us -> 11.1 us  [pair_block(): pl.pallas_call(functools.partial(pair_kernel, counts, has_diag), out_shap...]
  transfers between devices with their start and end apart: 30 -> 30, of which waited for: 21 -> 13; matrix products, arithmetic and copies ran while one was open for 3% -> 3% of each run, Pallas kernels for 0% -> 8%
where the time goes in v2:
time: 102 us
  starting transfers between devices  41.3 us (40%)
  waiting for transfers between devices  37.6 us (37%)
  Pallas kernels  11.1 us (11%)
  matrix products  6.14 us (6%)
  other arithmetic  3.01 us (3%)
  between operations  2.36 us (2%)
    ppermute x30, starting transfers between devices, send(): lax.ppermute(value, AXES, [(flat(*p), flat(*target(*p))) for p in PLACES])  41.3 us
    ppermute x30, waiting for transfers between devices, send(): lax.ppermute(value, AXES, [(flat(*p), flat(*target(*p))) for p in PLACES])  37.6 us
    pallas_call x3, Pallas kernels, pair_block(): pl.pallas_call(functools.partial(pair_kernel, counts, has_diag), out_shap...  11.1 us
    dot_general x1, matrix products, text_forward(): project = jnp.dot(features, weight, preferred_element_type=F32)  2.69 us
  transfers between devices with their start and end apart: 30, of which 13 were waited for; matrix products, arithmetic and copies ran while one was open for 3% of the time, Pallas kernels for 8%

profile of v2, /device:TPU:32, one launch (start us, length us, event | category | flops | bytes accessed | tf_op | source)
XLA Modules:
  0.0 101.7 jit_solution(3332433211484484507)
XLA Ops:
  0.6 0.0 copy-start
  0.7 2.7 %multiply_reduce_fusion.2 = (f32[64]{0:T(128)S(1)}, f32[64,1152]{1,0:T(8,128)S(1)}) fusion(bf16[64,1152]{1,0:T(8,128)(2,1)} %param.8, bf16[1152,1152]{1,0:T(8,128)(2,1)} %param.11), kind=kOutput, calls=%fused_computation.34 | convolution fusion | flops 170016704 | bytes 3096832 | tf_op jit(solution)/shard_map/dot_general | solution.py:63
  3.4 0.1 fusion.21
  3.5 2.0 %collective-permute-start.7 = (bf16[64,1152]{1,0:T(8,128)(2,1)S(1)}, bf16[64,1152]{1,0:T(8,128)(2,1)S(1)}, u32[]{:S(2)}, u32[]{:S(2)}) collective-permute-start(bf16[64,1152]{1,0:T(8,128)(2,1)S(1)} %fusion.21), channel_id=1, source_target_pairs={{0,4},{64,68},{4,8},{68,72},{8,12},{72,76},{12,16},{76,80},{16,20}... | collective-permute-start | bytes 442376 | tf_op jit(solution)/shard_map/ppermute | solution.py:25
  5.5 0.1 convert_reduce_fusion
  5.6 0.2 fusion.10
  5.8 0.7 multiply_reduce_fusion.3
  6.6 0.1 fusion.20
  6.7 1.7 %collective-permute-start = (bf16[64,1152]{1,0:T(8,128)(2,1)S(1)}, bf16[64,1152]{1,0:T(8,128)(2,1)S(1)}, u32[]{:S(2)}, u32[]{:S(2)}) collective-permute-start(bf16[64,1152]{1,0:T(8,128)(2,1)S(1)} %fusion.20), channel_id=1, source_target_pairs={{0,1},{64,192},{4,5},{68,196},{8,9},{72,200},{12,13},{76,204},{16,... | collective-permute-start | bytes 442376 | tf_op jit(solution)/shard_map/ppermute | solution.py:25
  8.4 1.7 %collective-permute-start.1 = (bf16[64,1152]{1,0:T(8,128)(2,1)S(1)}, bf16[64,1152]{1,0:T(8,128)(2,1)S(1)}, u32[]{:S(2)}, u32[]{:S(2)}) collective-permute-start(bf16[64,1152]{1,0:T(8,128)(2,1)S(1)} %fusion.20), channel_id=1, source_target_pairs={{0,3},{64,224},{4,7},{68,228},{8,11},{72,232},{12,15},{76,236},{16... | collective-permute-start | bytes 442376 | tf_op jit(solution)/shard_map/ppermute | solution.py:25
  10.0 2.0 %collective-permute-start.2 = (bf16[64,1152]{1,0:T(8,128)(2,1)S(1)}, bf16[64,1152]{1,0:T(8,128)(2,1)S(1)}, u32[]{:S(2)}, u32[]{:S(2)}) collective-permute-start(bf16[64,1152]{1,0:T(8,128)(2,1)S(1)} %fusion.20), channel_id=1, source_target_pairs={{0,2},{64,96},{4,6},{68,100},{8,10},{72,104},{12,14},{76,108},{16,... | collective-permute-start | bytes 442376 | tf_op jit(solution)/shard_map/ppermute | solution.py:25
  12.0 0.1 collective-permute-start.5
  12.1 1.9 %collective-permute-start.8 = (bf16[64,1152]{1,0:T(8,128)(2,1)S(1)}, bf16[64,1152]{1,0:T(8,128)(2,1)S(1)}, u32[]{:S(2)}, u32[]{:S(2)}) collective-permute-start(bf16[64,1152]{1,0:T(8,128)(2,1)S(1)} %collective-permute-done.7), channel_id=1, source_target_pairs={{0,4},{64,68},{4,8},{68,72},{8,12},{72,76},{12,16},{76,80},{16,20}... | collective-permute-start | bytes 442376 | tf_op jit(solution)/shard_map/ppermute | solution.py:25
  14.0 2.6 %collective-permute-done.2 = bf16[64,1152]{1,0:T(8,128)(2,1)S(1)} collective-permute-done((bf16[64,1152]{1,0:T(8,128)(2,1)S(1)}, bf16[64,1152]{1,0:T(8,128)(2,1)S(1)}, u32[]{:S(2)}, u32[]{:S(2)}) %collective-permute-start.2) | collective-permute-done | bytes 147488 | tf_op jit(solution)/shard_map/ppermute | solution.py:25
  16.7 1.6 %collective-permute-start.3 = (bf16[256,1152]{1,0:T(8,128)(2,1)S(1)}, bf16[256,1152]{1,0:T(8,128)(2,1)S(1)}, u32[]{:S(2)}, u32[]{:S(2)}) collective-permute-start(bf16[256,1152]{1,0:T(8,128)(2,1)S(1)} %pad_maximum_fusion.refs_0_), channel_id=1, source_target_pairs={{0,128},{64,65},{4,132},{68,69},{8,136},{72,73},{12,140},{76,77},{... | collective-permute-start | bytes 1769480 | tf_op jit(solution)/shard_map/ppermute | solution.py:25
  18.3 1.7 %collective-permute-start.4 = (bf16[256,1152]{1,0:T(8,128)(2,1)S(1)}, bf16[256,1152]{1,0:T(8,128)(2,1)S(1)}, u32[]{:S(2)}, u32[]{:S(2)}) collective-permute-start(bf16[256,1152]{1,0:T(8,128)(2,1)S(1)} %pad_maximum_fusion.refs_0_), channel_id=1, source_target_pairs={{0,160},{64,67},{4,164},{68,71},{8,168},{72,75},{12,172},{76,79},{... | collective-permute-start | bytes 1769480 | tf_op jit(solution)/shard_map/ppermute | solution.py:25
  20.0 0.1 collective-permute-start.6
  20.2 0.1 collective-permute-start.13
  20.3 4.9 %collective-permute-done.6 = bf16[64,1152]{1,0:T(8,128)(2,1)S(1)} collective-permute-done((bf16[64,1152]{1,0:T(8,128)(2,1)S(1)}, bf16[64,1152]{1,0:T(8,128)(2,1)S(1)}, u32[]{:S(2)}, u32[]{:S(2)}) %collective-permute-start.6) | collective-permute-done | bytes 147488 | tf_op jit(solution)/shard_map/ppermute | solution.py:25
  25.2 4.8 %collective-permute-start.10 = (bf16[96,1152]{1,0:T(8,128)(2,1)S(1)}, bf16[96,1152]{1,0:T(8,128)(2,1)S(1)}, u32[]{:S(2)}, u32[]{:S(2)}) collective-permute-start(bf16[96,1152]{1,0:T(8,128)(2,1)S(1)} %pad_maximum_fusion.5), channel_id=1, source_target_pairs={{0,24},{64,88},{4,28},{68,92},{8,0},{72,64},{12,4},{76,68},{16,8},... | collective-permute-start | bytes 663560 | tf_op jit(solution)/shard_map/ppermute | solution.py:25
  30.1 0.4 collective-permute-start.11
  30.4 3.0 %collective-permute-start.12 = (bf16[128,1152]{1,0:T(8,128)(2,1)S(1)}, bf16[128,1152]{1,0:T(8,128)(2,1)S(1)}, u32[]{:S(2)}, u32[]{:S(2)}) collective-permute-start(bf16[128,1152]{1,0:T(8,128)(2,1)S(1)} %slice.115), channel_id=1, source_target_pairs={{0,160},{64,67},{4,164},{68,71},{8,168},{72,75},{12,172},{76,79},{... | collective-permute-start | bytes 884744 | tf_op jit(solution)/shard_map/ppermute | solution.py:25
  33.5 2.6 %collective-permute-start.9 = (bf16[96,1152]{1,0:T(8,128)(2,1)S(1)}, bf16[96,1152]{1,0:T(8,128)(2,1)S(1)}, u32[]{:S(2)}, u32[]{:S(2)}) collective-permute-start(bf16[96,1152]{1,0:T(8,128)(2,1)S(1)} %pad_maximum_fusion.4), channel_id=1, source_target_pairs={{0,8},{64,72},{4,12},{68,76},{8,16},{72,80},{12,20},{76,84},{16,24... | collective-permute-start | bytes 663560 | tf_op jit(solution)/shard_map/ppermute | solution.py:25
  37.4 0.1 pad_maximum_fusion.8.scal
  37.5 4.0 %shard_map.86 = (f32[256,1152]{1,0:T(8,128)S(1)}, f32[256,1152]{1,0:T(8,128)S(1)}, f32[256,1152]{1,0:T(8,128)S(1)}, f32[256,1152]{1,0:T(8,128)S(1)}, f32[256,1152]{1,0:T(8,128)S(1)}) custom-call(f32[2]{0:T(128)S(1)} %pad_maximum_fusion.8.scal, bf16[256,1152]{1,0:T(8,128)(2,1)S(1)} %pad_maximum_fusion.refs_0_, ...), custom_call_target="tpu_custom_call" | custom-call | flops 1024 | bytes 1024 | tf_op jit(solution)/shard_map/pallas_call | solution.py:144
  41.6 2.6 %collective-permute-done.9 = bf16[96,1152]{1,0:T(8,128)(2,1)S(1)} collective-permute-done((bf16[96,1152]{1,0:T(8,128)(2,1)S(1)}, bf16[96,1152]{1,0:T(8,128)(2,1)S(1)}, u32[]{:S(2)}, u32[]{:S(2)}) %collective-permute-start.9) | collective-permute-done | bytes 221216 | tf_op jit(solution)/shard_map/ppermute | solution.py:25
  44.3 0.1 collective-permute-start.14
  44.4 2.0 %collective-permute-done.14.refs_5_.refs_4_ = bf16[256,1152]{1,0:T(8,128)(2,1)S(1)} collective-permute-done((bf16[256,1152]{1,0:T(8,128)(2,1)S(1)}, bf16[256,1152]{1,0:T(8,128)(2,1)S(1)}, u32[]{:S(2)}, u32[]{:S(2)}) %collective-permute-start.14) | collective-permute-done | bytes 589856 | tf_op jit(solution)/shard_map/ppermute | solution.py:25
  46.4 2.9 %shard_map.87 = (bf16[128,1152]{1,0:T(8,128)(2,1)S(1)}, bf16[128,1152]{1,0:T(8,128)(2,1)S(1)}, f32[256,1152]{1,0:T(8,128)S(1)}, bf16[256,1152]{1,0:T(8,128)(2,1)...) custom-call(f32[2]{0:T(128)S(1)} %pad_maximum_fusion.8.scal, ...), custom_call_target="tpu_custom_call" | custom-call | flops 1024 | bytes 1024 | tf_op jit(solution)/shard_map/pallas_call | solution.py:144
  49.3 1.0 collective-permute-start.15
  50.2 1.2 %collective-permute-start.16 = (bf16[128,1152]{1,0:T(8,128)(2,1)S(1)}, bf16[128,1152]{1,0:T(8,128)(2,1)S(1)}, u32[]{:S(2)}, u32[]{:S(2)}) collective-permute-start(bf16[128,1152]{1,0:T(8,128)(2,1)S(1)} %get-tuple-element.58), channel_id=1, source_target_pairs={{0,128},{64,65},{4,132},{68,69},{8,136},{72,73},{12,140},{76,77},{... | collective-permute-start | bytes 884744 | tf_op jit(solution)/shard_map/ppermute | solution.py:25
  51.4 4.1 %shard_map.88 = (f32[256,1152]{1,0:T(8,128)S(1)}, f32[256,1152]{1,0:T(8,128)S(1)}, f32[256,1152]{1,0:T(8,128)S(1)}, f32[256,1152]{1,0:T(8,128)S(1)}, bf16[256,1152]{1,0:T(8,128)(2,1)S(1)}) custom-call(f32[2]{0:T(128)S(1)} %pad_maximum_fusion.8.scal, bf16[256,1152]{1,0:T(8,128)(2,1)S(1)} %pad_maximum_fusion.refs_0_, ...), custom_call_target="tpu_custom_call" | custom-call | flops 1024 | bytes 1024 | tf_op jit(solution)/shard_map/pallas_call | solution.py:144
  55.6 0.5 collective-permute-done.15
  56.1 2.1 %collective-permute-done.16 = bf16[128,1152]{1,0:T(8,128)(2,1)S(1)} collective-permute-done((bf16[128,1152]{1,0:T(8,128)(2,1)S(1)}, bf16[128,1152]{1,0:T(8,128)(2,1)S(1)}, u32[]{:S(2)}, u32[]{:S(2)}) %collective-permute-start.16) | collective-permute-done | bytes 294944 | tf_op jit(solution)/shard_map/ppermute | solution.py:25
  58.2 0.1 add_convert_fusion
  58.4 0.1 convert_add_fusion.1
  58.5 1.6 %collective-permute-done.17 = bf16[256,1152]{1,0:T(8,128)(2,1)S(1)} collective-permute-done((bf16[256,1152]{1,0:T(8,128)(2,1)S(1)}, bf16[256,1152]{1,0:T(8,128)(2,1)S(1)}, u32[]{:S(2)}, u32[]{:S(2)}) %collective-permute-start.17) | collective-permute-done | bytes 589856 | tf_op jit(solution)/shard_map/ppermute | solution.py:25
  60.2 0.1 convert_add_fusion.2
  60.3 0.3 collective-permute-start.19
  60.6 2.0 %collective-permute-start.20 = (bf16[256,1152]{1,0:T(8,128)(2,1)S(1)}, bf16[256,1152]{1,0:T(8,128)(2,1)S(1)}, u32[]{:S(2)}, u32[]{:S(2)}) collective-permute-start(bf16[256,1152]{1,0:T(8,128)(2,1)S(1)} %pad_maximum_fusion.3), channel_id=1, source_target_pairs={{0,128},{64,65},{4,132},{68,69},{8,136},{72,73},{12,140},{76,77},{... | collective-permute-start | bytes 1769480 | tf_op jit(solution)/shard_map/ppermute | solution.py:25
  62.6 0.1 convert.34
  62.7 1.2 %collective-permute-start.21 = (bf16[96,1152]{1,0:T(8,128)(2,1)S(1)}, bf16[96,1152]{1,0:T(8,128)(2,1)S(1)}, u32[]{:S(2)}, u32[]{:S(2)}) collective-permute-start(bf16[96,1152]{1,0:T(8,128)(2,1)S(1)} %get-tuple-element.84), channel_id=1, source_target_pairs={{0,24},{64,88},{4,28},{68,92},{8,0},{72,64},{12,4},{76,68},{16,8},... | collective-permute-start | bytes 663560 | tf_op jit(solution)/shard_map/ppermute | solution.py:25
  64.0 1.8 %collective-permute-start.22 = (bf16[96,1152]{1,0:T(8,128)(2,1)S(1)}, bf16[96,1152]{1,0:T(8,128)(2,1)S(1)}, u32[]{:S(2)}, u32[]{:S(2)}) collective-permute-start(bf16[96,1152]{1,0:T(8,128)(2,1)S(1)} %get-tuple-element.83), channel_id=1, source_target_pairs={{0,8},{64,72},{4,12},{68,76},{8,16},{72,80},{12,20},{76,84},{16,24... | collective-permute-start | bytes 663560 | tf_op jit(solution)/shard_map/ppermute | solution.py:25
  65.8 8.4 %collective-permute-done.21 = bf16[96,1152]{1,0:T(8,128)(2,1)S(1)} collective-permute-done((bf16[96,1152]{1,0:T(8,128)(2,1)S(1)}, bf16[96,1152]{1,0:T(8,128)(2,1)S(1)}, u32[]{:S(2)}, u32[]{:S(2)}) %collective-permute-start.21) | collective-permute-done | bytes 221216 | tf_op jit(solution)/shard_map/ppermute | solution.py:25
  74.2 4.0 %collective-permute-done.22 = bf16[96,1152]{1,0:T(8,128)(2,1)S(1)} collective-permute-done((bf16[96,1152]{1,0:T(8,128)(2,1)S(1)}, bf16[96,1152]{1,0:T(8,128)(2,1)S(1)}, u32[]{:S(2)}, u32[]{:S(2)}) %collective-permute-start.22) | collective-permute-done | bytes 221216 | tf_op jit(solution)/shard_map/ppermute | solution.py:25
  78.3 0.2 convert_add_fusion
  78.5 0.1 add_convert_fusion.3
  78.6 0.1 collective-permute-start.26
  78.7 2.0 %collective-permute-start.27 = (bf16[64,1152]{1,0:T(8,128)(2,1)S(1)}, bf16[64,1152]{1,0:T(8,128)(2,1)S(1)}, u32[]{:S(2)}, u32[]{:S(2)}) collective-permute-start(bf16[64,1152]{1,0:T(8,128)(2,1)S(1)} %get-tuple-element.79), channel_id=1, source_target_pairs={{0,4},{64,68},{4,8},{68,72},{8,12},{72,76},{12,16},{76,80},{16,20}... | collective-permute-start | bytes 442376 | tf_op jit(solution)/shard_map/ppermute | solution.py:25
  80.7 0.1 convert_element_type.96
  80.8 1.6 %collective-permute-start.23 = (bf16[64,1152]{1,0:T(8,128)(2,1)S(1)}, bf16[64,1152]{1,0:T(8,128)(2,1)S(1)}, u32[]{:S(2)}, u32[]{:S(2)}) collective-permute-start(bf16[64,1152]{1,0:T(8,128)(2,1)S(1)} %get-tuple-element.80), channel_id=1, source_target_pairs={{0,3},{64,224},{4,7},{68,228},{8,11},{72,232},{12,15},{76,236},{16... | collective-permute-start | bytes 442376 | tf_op jit(solution)/shard_map/ppermute | solution.py:25
  82.4 0.6 collective-permute-start.24
  82.9 1.0 collective-permute-start.25
  84.0 2.1 %collective-permute-done.23 = bf16[64,1152]{1,0:T(8,128)(2,1)S(1)} collective-permute-done((bf16[64,1152]{1,0:T(8,128)(2,1)S(1)}, bf16[64,1152]{1,0:T(8,128)(2,1)S(1)}, u32[]{:S(2)}, u32[]{:S(2)}) %collective-permute-start.23) | collective-permute-done | bytes 147488 | tf_op jit(solution)/shard_map/ppermute | solution.py:25
  86.0 3.0 %collective-permute-start.28 = (bf16[64,1152]{1,0:T(8,128)(2,1)S(1)}, bf16[64,1152]{1,0:T(8,128)(2,1)S(1)}, u32[]{:S(2)}, u32[]{:S(2)}) collective-permute-start(bf16[64,1152]{1,0:T(8,128)(2,1)S(1)} %pad_maximum_fusion.6), channel_id=1, source_target_pairs={{0,24},{64,88},{4,28},{68,92},{8,0},{72,64},{12,4},{76,68},{16,8},... | collective-permute-start | bytes 442376 | tf_op jit(solution)/shard_map/ppermute | solution.py:25
  89.1 1.2 %collective-permute-done.24 = bf16[64,1152]{1,0:T(8,128)(2,1)S(1)} collective-permute-done((bf16[64,1152]{1,0:T(8,128)(2,1)S(1)}, bf16[64,1152]{1,0:T(8,128)(2,1)S(1)}, u32[]{:S(2)}, u32[]{:S(2)}) %collective-permute-start.24) | collective-permute-done | bytes 147488 | tf_op jit(solution)/shard_map/ppermute | solution.py:25
  90.3 1.9 %collective-permute-start.29 = (bf16[64,1152]{1,0:T(8,128)(2,1)S(1)}, bf16[64,1152]{1,0:T(8,128)(2,1)S(1)}, u32[]{:S(2)}, u32[]{:S(2)}) collective-permute-start(bf16[64,1152]{1,0:T(8,128)(2,1)S(1)} %pad_maximum_fusion.7), channel_id=1, source_target_pairs={{0,8},{64,72},{4,12},{68,76},{8,16},{72,80},{12,20},{76,84},{16,24... | collective-permute-start | bytes 442376 | tf_op jit(solution)/shard_map/ppermute | solution.py:25
  92.2 0.2 multiply_reduce_fusion.1
  92.4 1.1 %fusion.22 = (f32[64]{0:T(128)S(1)}, f32[64]{0:T(128)S(1)}, f32[64,1152]{1,0:T(8,128)S(1)}) fusion(f32[64]{0:T(128)S(1)} %add_rsqrt_fusion, f32[64]{0:T(128)S(1)} %broadcast_multiply_fusion.2, bf16[64,1152]{1,0:T(8,128)(2,1)S(1)} %copy-done.2, f32[1152]{0:T(1024)S(1)} %copy-done.4, bf16[1152,1152]{1,0:T(8,128)(2,1)S(1)} %copy-done, ...), kind=kOutput, calls=%fused_computation.65 | convolution fusion | flops 171270016 | bytes 4139524 | tf_op jit(solution)/shard_map/dot_general | solution.py:73
  93.5 0.1 collective-permute-done.28
  93.6 5.4 %collective-permute-done.29 = bf16[64,1152]{1,0:T(8,128)(2,1)S(1)} collective-permute-done((bf16[64,1152]{1,0:T(8,128)(2,1)S(1)}, bf16[64,1152]{1,0:T(8,128)(2,1)S(1)}, u32[]{:S(2)}, u32[]{:S(2)}) %collective-permute-start.29) | collective-permute-done | bytes 147488 | tf_op jit(solution)/shard_map/ppermute | solution.py:25
  99.1 0.2 multiply_reduce_fusion
  99.3 1.6 %convolution_convert_fusion = bf16[64,1152]{1,0:T(8,128)(2,1)} fusion(bf16[1152,1152]{1,0:T(8,128)(2,1)S(1)} %copy-done.1, f32[64,1152]{1,0:T(8,128)S(1)} %get-tuple-element.77, f32[64]{0:T(128)S(1)} %get-tuple-element.76, f32[64]{0:T(128)S(1)} %add_sqrt_fusion, f32[64,1152]{1,0:T(8,128)S(1)} %get-tuple-element.88), kind=kOutput, calls=%fused_computation.1 | convolution fusion | flops 170311680 | bytes 3392000 | tf_op jit(solution)/shard_map/dot_general | solution.py:85
  100.9 0.8 fusion.9
  (60 shorter events, 0.7 us)
Async XLA Ops:
  0.6 5.2 %copy-start = (bf16[1152,1152]{1,0:T(8,128)(2,1)S(1)}, bf16[1152,1152]{1,0:T(8,128)(2,1)}, u32[]{:S(2)}) copy-start(bf16[1152,1152]{1,0:T(8,128)(2,1)} %param.10) | copy-start | bytes 7962628
  0.6 4.8 %copy-start.2 = (bf16[64,1152]{1,0:T(8,128)(2,1)S(1)}, bf16[64,1152]{1,0:T(8,128)(2,1)}, u32[]{:S(2)}) copy-start(bf16[64,1152]{1,0:T(8,128)(2,1)} %param.7) | copy-start | bytes 442372
  0.7 5.2 %copy-start.4 = (f32[1152]{0:T(1024)S(1)}, f32[1152]{0:T(1024)}, u32[]{:S(2)}) copy-start(f32[1152]{0:T(1024)} %param.9) | copy-start | bytes 13828
  3.5 8.6 %collective-permute-start.7 = (bf16[64,1152]{1,0:T(8,128)(2,1)S(1)}, bf16[64,1152]{1,0:T(8,128)(2,1)S(1)}, u32[]{:S(2)}, u32[]{:S(2)}) collective-permute-start(bf16[64,1152]{1,0:T(8,128)(2,1)S(1)} %fusion.21), channel_id=1, source_target_pairs={{0,4},{64,68},{4,8},{68,72},{8,12},{72,76},{12,16},{76,80},{16,20}... | collective-permute-start | bytes 442376 | tf_op jit(solution)/shard_map/ppermute | solution.py:25
  6.7 7.3 %collective-permute-start = (bf16[64,1152]{1,0:T(8,128)(2,1)S(1)}, bf16[64,1152]{1,0:T(8,128)(2,1)S(1)}, u32[]{:S(2)}, u32[]{:S(2)}) collective-permute-start(bf16[64,1152]{1,0:T(8,128)(2,1)S(1)} %fusion.20), channel_id=1, source_target_pairs={{0,1},{64,192},{4,5},{68,196},{8,9},{72,200},{12,13},{76,204},{16,... | collective-permute-start | bytes 442376 | tf_op jit(solution)/shard_map/ppermute | solution.py:25
  8.4 5.7 %collective-permute-start.1 = (bf16[64,1152]{1,0:T(8,128)(2,1)S(1)}, bf16[64,1152]{1,0:T(8,128)(2,1)S(1)}, u32[]{:S(2)}, u32[]{:S(2)}) collective-permute-start(bf16[64,1152]{1,0:T(8,128)(2,1)S(1)} %fusion.20), channel_id=1, source_target_pairs={{0,3},{64,224},{4,7},{68,228},{8,11},{72,232},{12,15},{76,236},{16... | collective-permute-start | bytes 442376 | tf_op jit(solution)/shard_map/ppermute | solution.py:25
  10.0 6.6 %collective-permute-start.2 = (bf16[64,1152]{1,0:T(8,128)(2,1)S(1)}, bf16[64,1152]{1,0:T(8,128)(2,1)S(1)}, u32[]{:S(2)}, u32[]{:S(2)}) collective-permute-start(bf16[64,1152]{1,0:T(8,128)(2,1)S(1)} %fusion.20), channel_id=1, source_target_pairs={{0,2},{64,96},{4,6},{68,100},{8,10},{72,104},{12,14},{76,108},{16,... | collective-permute-start | bytes 442376 | tf_op jit(solution)/shard_map/ppermute | solution.py:25
  12.0 8.0 %collective-permute-start.5 = (bf16[64,1152]{1,0:T(8,128)(2,1)S(1)}, bf16[64,1152]{1,0:T(8,128)(2,1)S(1)}, u32[]{:S(2)}, u32[]{:S(2)}) collective-permute-start(bf16[64,1152]{1,0:T(8,128)(2,1)S(1)} %fusion.21), channel_id=1, source_target_pairs={{0,28},{64,92},{4,0},{68,64},{8,4},{72,68},{12,8},{76,72},{16,12},... | collective-permute-start | bytes 442376 | tf_op jit(solution)/shard_map/ppermute | solution.py:25
  12.1 8.0 %collective-permute-start.8 = (bf16[64,1152]{1,0:T(8,128)(2,1)S(1)}, bf16[64,1152]{1,0:T(8,128)(2,1)S(1)}, u32[]{:S(2)}, u32[]{:S(2)}) collective-permute-start(bf16[64,1152]{1,0:T(8,128)(2,1)S(1)} %collective-permute-done.7), channel_id=1, source_target_pairs={{0,4},{64,68},{4,8},{68,72},{8,12},{72,76},{12,16},{76,80},{16,20}... | collective-permute-start | bytes 442376 | tf_op jit(solution)/shard_map/ppermute | solution.py:25
  16.7 13.3 %collective-permute-start.3 = (bf16[256,1152]{1,0:T(8,128)(2,1)S(1)}, bf16[256,1152]{1,0:T(8,128)(2,1)S(1)}, u32[]{:S(2)}, u32[]{:S(2)}) collective-permute-start(bf16[256,1152]{1,0:T(8,128)(2,1)S(1)} %pad_maximum_fusion.refs_0_), channel_id=1, source_target_pairs={{0,128},{64,65},{4,132},{68,69},{8,136},{72,73},{12,140},{76,77},{... | collective-permute-start | bytes 1769480 | tf_op jit(solution)/shard_map/ppermute | solution.py:25
  18.3 12.1 %collective-permute-start.4 = (bf16[256,1152]{1,0:T(8,128)(2,1)S(1)}, bf16[256,1152]{1,0:T(8,128)(2,1)S(1)}, u32[]{:S(2)}, u32[]{:S(2)}) collective-permute-start(bf16[256,1152]{1,0:T(8,128)(2,1)S(1)} %pad_maximum_fusion.refs_0_), channel_id=1, source_target_pairs={{0,160},{64,67},{4,164},{68,71},{8,168},{72,75},{12,172},{76,79},{... | collective-permute-start | bytes 1769480 | tf_op jit(solution)/shard_map/ppermute | solution.py:25
  20.0 5.1 %collective-permute-start.6 = (bf16[64,1152]{1,0:T(8,128)(2,1)S(1)}, bf16[64,1152]{1,0:T(8,128)(2,1)S(1)}, u32[]{:S(2)}, u32[]{:S(2)}) collective-permute-start(bf16[64,1152]{1,0:T(8,128)(2,1)S(1)} %collective-permute-done.5), channel_id=1, source_target_pairs={{0,28},{64,92},{4,0},{68,64},{8,4},{72,68},{12,8},{76,72},{16,12},... | collective-permute-start | bytes 442376 | tf_op jit(solution)/shard_map/ppermute | solution.py:25
  20.2 17.3 %collective-permute-start.13 = (bf16[256,1152]{1,0:T(8,128)(2,1)S(1)}, bf16[256,1152]{1,0:T(8,128)(2,1)S(1)}, u32[]{:S(2)}, u32[]{:S(2)}) collective-permute-start(bf16[256,1152]{1,0:T(8,128)(2,1)S(1)} %pad_maximum_fusion.1.refs_3_.refs_2_), channel_id=1, source_target_pairs={{0,64},{64,0},{4,68},{68,4},{8,72},{72,8},{12,76},{76,12},{16,80},... | collective-permute-start | bytes 1769480 | tf_op jit(solution)/shard_map/ppermute | solution.py:25
  25.2 16.4 %collective-permute-start.10 = (bf16[96,1152]{1,0:T(8,128)(2,1)S(1)}, bf16[96,1152]{1,0:T(8,128)(2,1)S(1)}, u32[]{:S(2)}, u32[]{:S(2)}) collective-permute-start(bf16[96,1152]{1,0:T(8,128)(2,1)S(1)} %pad_maximum_fusion.5), channel_id=1, source_target_pairs={{0,24},{64,88},{4,28},{68,92},{8,0},{72,64},{12,4},{76,68},{16,8},... | collective-permute-start | bytes 663560 | tf_op jit(solution)/shard_map/ppermute | solution.py:25
  30.1 14.1 %collective-permute-start.11 = (bf16[128,1152]{1,0:T(8,128)(2,1)S(1)}, bf16[128,1152]{1,0:T(8,128)(2,1)S(1)}, u32[]{:S(2)}, u32[]{:S(2)}) collective-permute-start(bf16[128,1152]{1,0:T(8,128)(2,1)S(1)} %slice.114), channel_id=1, source_target_pairs={{0,128},{64,65},{4,132},{68,69},{8,136},{72,73},{12,140},{76,77},{... | collective-permute-start | bytes 884744 | tf_op jit(solution)/shard_map/ppermute | solution.py:25
  30.4 13.8 %collective-permute-start.12 = (bf16[128,1152]{1,0:T(8,128)(2,1)S(1)}, bf16[128,1152]{1,0:T(8,128)(2,1)S(1)}, u32[]{:S(2)}, u32[]{:S(2)}) collective-permute-start(bf16[128,1152]{1,0:T(8,128)(2,1)S(1)} %slice.115), channel_id=1, source_target_pairs={{0,160},{64,67},{4,164},{68,71},{8,168},{72,75},{12,172},{76,79},{... | collective-permute-start | bytes 884744 | tf_op jit(solution)/shard_map/ppermute | solution.py:25
  33.5 10.7 %collective-permute-start.9 = (bf16[96,1152]{1,0:T(8,128)(2,1)S(1)}, bf16[96,1152]{1,0:T(8,128)(2,1)S(1)}, u32[]{:S(2)}, u32[]{:S(2)}) collective-permute-start(bf16[96,1152]{1,0:T(8,128)(2,1)S(1)} %pad_maximum_fusion.4), channel_id=1, source_target_pairs={{0,8},{64,72},{4,12},{68,76},{8,16},{72,80},{12,20},{76,84},{16,24... | collective-permute-start | bytes 663560 | tf_op jit(solution)/shard_map/ppermute | solution.py:25
  44.3 2.1 %collective-permute-start.14 = (bf16[256,1152]{1,0:T(8,128)(2,1)S(1)}, bf16[256,1152]{1,0:T(8,128)(2,1)S(1)}, u32[]{:S(2)}, u32[]{:S(2)}) collective-permute-start(bf16[256,1152]{1,0:T(8,128)(2,1)S(1)} %constant_dynamic-update-slice_fusion.refs_4_.refs_3_), channel_id=1, source_target_pairs={{0,64},{64,0},{4,68},{68,4},{8,72},{72,8},{12,76},{76,12},{16,80},... | collective-permute-start | bytes 1769480 | tf_op jit(solution)/shard_map/ppermute | solution.py:25
  49.3 6.8 %collective-permute-start.15 = (bf16[128,1152]{1,0:T(8,128)(2,1)S(1)}, bf16[128,1152]{1,0:T(8,128)(2,1)S(1)}, u32[]{:S(2)}, u32[]{:S(2)}) collective-permute-start(bf16[128,1152]{1,0:T(8,128)(2,1)S(1)} %get-tuple-element.57), channel_id=1, source_target_pairs={{0,160},{64,67},{4,164},{68,71},{8,168},{72,75},{12,172},{76,79},{... | collective-permute-start | bytes 884744 | tf_op jit(solution)/shard_map/ppermute | solution.py:25
  50.2 7.9 %collective-permute-start.16 = (bf16[128,1152]{1,0:T(8,128)(2,1)S(1)}, bf16[128,1152]{1,0:T(8,128)(2,1)S(1)}, u32[]{:S(2)}, u32[]{:S(2)}) collective-permute-start(bf16[128,1152]{1,0:T(8,128)(2,1)S(1)} %get-tuple-element.58), channel_id=1, source_target_pairs={{0,128},{64,65},{4,132},{68,69},{8,136},{72,73},{12,140},{76,77},{... | collective-permute-start | bytes 884744 | tf_op jit(solution)/shard_map/ppermute | solution.py:25
  51.4 7.0 %collective-permute-start.18 = (bf16[256,1152]{1,0:T(8,128)(2,1)S(1)}, bf16[256,1152]{1,0:T(8,128)(2,1)S(1)}, u32[]{:S(2)}, u32[]{:S(2)}) collective-permute-start(bf16[256,1152]{1,0:T(8,128)(2,1)S(1)} %get-tuple-element.66), channel_id=1, source_target_pairs={{0,64},{64,0},{4,68},{68,4},{8,72},{72,8},{12,76},{76,12},{16,80},... | collective-permute-start | bytes 1769480 | tf_op jit(solution)/shard_map/ppermute | solution.py:25
  58.2 2.0 %collective-permute-start.17 = (bf16[256,1152]{1,0:T(8,128)(2,1)S(1)}, bf16[256,1152]{1,0:T(8,128)(2,1)S(1)}, u32[]{:S(2)}, u32[]{:S(2)}) collective-permute-start(bf16[256,1152]{1,0:T(8,128)(2,1)S(1)} %get-tuple-element.64), channel_id=1, source_target_pairs={{0,64},{64,0},{4,68},{68,4},{8,72},{72,8},{12,76},{76,12},{16,80},... | collective-permute-start | bytes 1769480 | tf_op jit(solution)/shard_map/ppermute | solution.py:25
  60.3 17.9 %collective-permute-start.19 = (bf16[256,1152]{1,0:T(8,128)(2,1)S(1)}, bf16[256,1152]{1,0:T(8,128)(2,1)S(1)}, u32[]{:S(2)}, u32[]{:S(2)}) collective-permute-start(bf16[256,1152]{1,0:T(8,128)(2,1)S(1)} %pad_maximum_fusion.2), channel_id=1, source_target_pairs={{0,160},{64,67},{4,164},{68,71},{8,168},{72,75},{12,172},{76,79},{... | collective-permute-start | bytes 1769480 | tf_op jit(solution)/shard_map/ppermute | solution.py:25
  60.6 17.6 %collective-permute-start.20 = (bf16[256,1152]{1,0:T(8,128)(2,1)S(1)}, bf16[256,1152]{1,0:T(8,128)(2,1)S(1)}, u32[]{:S(2)}, u32[]{:S(2)}) collective-permute-start(bf16[256,1152]{1,0:T(8,128)(2,1)S(1)} %pad_maximum_fusion.3), channel_id=1, source_target_pairs={{0,128},{64,65},{4,132},{68,69},{8,136},{72,73},{12,140},{76,77},{... | collective-permute-start | bytes 1769480 | tf_op jit(solution)/shard_map/ppermute | solution.py:25
  62.7 15.5 %copy-start.3 = (bf16[256,1152]{1,0:T(8,128)(2,1)}, bf16[256,1152]{1,0:T(8,128)(2,1)S(1)}, u32[]{:S(2)}) copy-start(bf16[256,1152]{1,0:T(8,128)(2,1)S(1)} %convert.34) | copy-start | bytes 1769476
  62.7 11.4 %collective-permute-start.21 = (bf16[96,1152]{1,0:T(8,128)(2,1)S(1)}, bf16[96,1152]{1,0:T(8,128)(2,1)S(1)}, u32[]{:S(2)}, u32[]{:S(2)}) collective-permute-start(bf16[96,1152]{1,0:T(8,128)(2,1)S(1)} %get-tuple-element.84), channel_id=1, source_target_pairs={{0,24},{64,88},{4,28},{68,92},{8,0},{72,64},{12,4},{76,68},{16,8},... | collective-permute-start | bytes 663560 | tf_op jit(solution)/shard_map/ppermute | solution.py:25
  64.0 14.2 %collective-permute-start.22 = (bf16[96,1152]{1,0:T(8,128)(2,1)S(1)}, bf16[96,1152]{1,0:T(8,128)(2,1)S(1)}, u32[]{:S(2)}, u32[]{:S(2)}) collective-permute-start(bf16[96,1152]{1,0:T(8,128)(2,1)S(1)} %get-tuple-element.83), channel_id=1, source_target_pairs={{0,8},{64,72},{4,12},{68,76},{8,16},{72,80},{12,20},{76,84},{16,24... | collective-permute-start | bytes 663560 | tf_op jit(solution)/shard_map/ppermute | solution.py:25
  78.6 14.9 %collective-permute-start.26 = (bf16[64,1152]{1,0:T(8,128)(2,1)S(1)}, bf16[64,1152]{1,0:T(8,128)(2,1)S(1)}, u32[]{:S(2)}, u32[]{:S(2)}) collective-permute-start(bf16[64,1152]{1,0:T(8,128)(2,1)S(1)} %get-tuple-element.78), channel_id=1, source_target_pairs={{0,28},{64,92},{4,0},{68,64},{8,4},{72,68},{12,8},{76,72},{16,12},... | collective-permute-start | bytes 442376 | tf_op jit(solution)/shard_map/ppermute | solution.py:25
  78.7 5.2 %slice-start = ((bf16[256,1152]{1,0:T(8,128)(2,1)}), bf16[32,1152]{1,0:T(8,128)(2,1)S(1)}, s32[]{:S(2)}) async-start(bf16[256,1152]{1,0:T(8,128)(2,1)} %copy-done.3), calls=%async_computation | async-start | bytes 147456 | tf_op jit(solution)/shard_map/slice | solution.py:231
  78.7 14.8 %collective-permute-start.27 = (bf16[64,1152]{1,0:T(8,128)(2,1)S(1)}, bf16[64,1152]{1,0:T(8,128)(2,1)S(1)}, u32[]{:S(2)}, u32[]{:S(2)}) collective-permute-start(bf16[64,1152]{1,0:T(8,128)(2,1)S(1)} %get-tuple-element.79), channel_id=1, source_target_pairs={{0,4},{64,68},{4,8},{68,72},{8,12},{72,76},{12,16},{76,80},{16,20}... | collective-permute-start | bytes 442376 | tf_op jit(solution)/shard_map/ppermute | solution.py:25
  80.8 5.2 %collective-permute-start.23 = (bf16[64,1152]{1,0:T(8,128)(2,1)S(1)}, bf16[64,1152]{1,0:T(8,128)(2,1)S(1)}, u32[]{:S(2)}, u32[]{:S(2)}) collective-permute-start(bf16[64,1152]{1,0:T(8,128)(2,1)S(1)} %get-tuple-element.80), channel_id=1, source_target_pairs={{0,3},{64,224},{4,7},{68,228},{8,11},{72,232},{12,15},{76,236},{16... | collective-permute-start | bytes 442376 | tf_op jit(solution)/shard_map/ppermute | solution.py:25
  82.4 7.9 %collective-permute-start.24 = (bf16[64,1152]{1,0:T(8,128)(2,1)S(1)}, bf16[64,1152]{1,0:T(8,128)(2,1)S(1)}, u32[]{:S(2)}, u32[]{:S(2)}) collective-permute-start(bf16[64,1152]{1,0:T(8,128)(2,1)S(1)} %get-tuple-element.82), channel_id=1, source_target_pairs={{0,1},{64,192},{4,5},{68,196},{8,9},{72,200},{12,13},{76,204},{16,... | collective-permute-start | bytes 442376 | tf_op jit(solution)/shard_map/ppermute | solution.py:25
  82.9 9.3 %collective-permute-start.25 = (bf16[64,1152]{1,0:T(8,128)(2,1)S(1)}, bf16[64,1152]{1,0:T(8,128)(2,1)S(1)}, u32[]{:S(2)}, u32[]{:S(2)}) collective-permute-start(bf16[64,1152]{1,0:T(8,128)(2,1)S(1)} %get-tuple-element.81), channel_id=1, source_target_pairs={{0,2},{64,96},{4,6},{68,100},{8,10},{72,104},{12,14},{76,108},{16,... | collective-permute-start | bytes 442376 | tf_op jit(solution)/shard_map/ppermute | solution.py:25
  86.0 7.6 %collective-permute-start.28 = (bf16[64,1152]{1,0:T(8,128)(2,1)S(1)}, bf16[64,1152]{1,0:T(8,128)(2,1)S(1)}, u32[]{:S(2)}, u32[]{:S(2)}) collective-permute-start(bf16[64,1152]{1,0:T(8,128)(2,1)S(1)} %pad_maximum_fusion.6), channel_id=1, source_target_pairs={{0,24},{64,88},{4,28},{68,92},{8,0},{72,64},{12,4},{76,68},{16,8},... | collective-permute-start | bytes 442376 | tf_op jit(solution)/shard_map/ppermute | solution.py:25
  90.3 8.8 %collective-permute-start.29 = (bf16[64,1152]{1,0:T(8,128)(2,1)S(1)}, bf16[64,1152]{1,0:T(8,128)(2,1)S(1)}, u32[]{:S(2)}, u32[]{:S(2)}) collective-permute-start(bf16[64,1152]{1,0:T(8,128)(2,1)S(1)} %pad_maximum_fusion.7), channel_id=1, source_target_pairs={{0,8},{64,72},{4,12},{68,76},{8,16},{72,80},{12,20},{76,84},{16,24... | collective-permute-start | bytes 442376 | tf_op jit(solution)/shard_map/ppermute | solution.py:25
  92.4 6.9 %copy-start.1 = (bf16[1152,1152]{1,0:T(8,128)(2,1)S(1)}, bf16[1152,1152]{1,0:T(8,128)(2,1)}, u32[]{:S(2)}) copy-start(bf16[1152,1152]{1,0:T(8,128)(2,1)} %param.11) | copy-start | bytes 7962628

commit v3 on v2

--- a/solution.py
+++ b/solution.py
@@ -27,6 +27,10 @@
 
 def send_z(value, k):
     return send(value, lambda x, y, z, c: (x, y, (z + k) % 8, c))
+
+
+def send_ring(value, k):
+    return send(value, lambda x, y, z, c: (x, y, (z + (k if c == 0 else -k)) % 8, c))
 
 
 def send_core(value):
@@ -105,13 +109,13 @@
     slope = -scal[0] * LOG2E
     offset = -scal[1] * LOG2E
     width = 256
-    for n in range(txt.shape[0] // width):
-        cols = pl.ds(n * width, width)
+    for at in range(0, txt.shape[0], width):
+        cols = pl.ds(at, min(width, txt.shape[0] - at))
         cosine = lax.dot_general(
             img[...], txt[cols, :], (((1,), (1,)), ((), ())), preferred_element_type=F32
         )
         power = cosine * slope + offset
-        if has_diag and n == 0:
+        if has_diag and at == 0:
             row = lax.broadcasted_iota(jnp.int32, power.shape, 0)
             col = lax.broadcasted_iota(jnp.int32, power.shape, 1)
             same = (row == col) & (row < ROWS)
@@ -122,7 +126,9 @@
         grad[:, cols] = value.astype(BF)
     for n, (ref, place) in enumerate(spans(img_out)):
         value = jnp.dot(grad[place, :], txt[...], preferred_element_type=F32)
-        if img_old:
+        if img_old and len(img_out) == 1:
+            value = value + jnp.concatenate([old[...] for old in img_old])
+        elif n < len(img_old):
             value = value + img_old[n][...]
         ref[...] = value.astype(ref.dtype)
     for n, (ref, place) in enumerate(spans(txt_out)):
@@ -158,78 +164,75 @@
 
 
 def shards(image_feat, text_feat, norm_gain, w_image, w_text, log_scale, bias):
-    half = ROWS // 2
     cat = jnp.concatenate
     tie = lax.optimization_barrier
     logit_scale = jnp.exp(log_scale)
     scal = cat([logit_scale, bias])
 
     text_emb, text_unit, text_len = text_forward(text_feat, w_text)
-    f1, b1 = send_z(text_emb, 1), send_z(text_emb, -1)
-    f2, b2 = send_z(f1, 1), send_z(b1, -1)
+    text_emb, image_feat = tie((text_emb, image_feat))
+    chip_emb = cat([text_emb, send_core(text_emb)])
+    t1 = send_ring(chip_emb, 1)
+    t2 = send_ring(t1, 1)
+    t3 = send_ring(t2, 1)
+    t4 = send_ring(t3[:ROWS], 1)
     image_emb, image_unit, image_len, normed, inv_std = image_forward(
         image_feat, norm_gain, w_image
     )
-    near = [send_xy(image_emb, k, False) for k in (1, -1, 2)]
-    near = cat([image_emb] + near)
+    near = cat([image_emb] + [send_xy(image_emb, k, False) for k in (1, -1, 2)])
     next_p, next_m = [send_xy(near, k, True) for k in (1, -1)]
     across_p = send_xy(next_p[: 2 * ROWS], 1, True)
     across_m = send_xy(next_m[2 * ROWS :], -1, True)
-    far_f = send_z(cat([f1, f2[:half]]), 2)
-    far_b = send_z(cat([b1, b2[half:]]), -2)
-    early = cat([text_emb, f1, b1, f2])
-    early_sib = send_core(early)
+    early = cat([t1, t2])
+    early = [chip_emb, early, send_core(early)]
 
     sides = [near, next_p, next_m]
     side = 4 * ROWS
-    side_acc, early_acc = pair_block(
-        scal, sides, [early, early_sib], [(side, F32)] * 3, [(side, F32)] * 2, has_diag=True
-    )
-    b2, far_f, far_b, across_p, across_m, side_acc, early_acc = tie(
-        (b2, far_f, far_b, across_p, across_m, side_acc, early_acc)
-    )
-    late = cat([b2, far_f, far_b])
-    late_sib = send_core(late)
-    (across_pg, across_mg), (ge_own, ge_sib, *late_acc) = pair_block(
-        scal, [across_p, across_m], [early, early_sib, late, late_sib], [(2 * ROWS, BF)] * 2,
-        [(side, F32), (side, BF), (side, F32), (side, F32)], txt_old=early_acc,
-    )
-    (near_g, next_pg, next_mg), (gl_own, gl_sib) = pair_block(
-        scal, sides, [late, late_sib], [(side, F32)] * 3, [(side, F32), (side, BF)],
-        img_old=side_acc, txt_old=late_acc,
-    )
-
-    across_pg, across_mg = send_xy(across_pg, -1, True), send_xy(across_mg, 1, True)
-    across_pg, across_mg, gl_sib = tie((across_pg, across_mg, gl_sib))
-    low, high = across_pg.astype(F32), across_mg.astype(F32)
-    next_pg = cat([next_pg[: 2 * ROWS] + low, next_pg[2 * ROWS :]]).astype(BF)
-    next_mg = cat([next_mg[: 2 * ROWS], next_mg[2 * ROWS :] + high]).astype(BF)
+    early_rows = [(ROWS, F32)] * 2 + [(side, F32)] * 2
+    near_acc, early_acc = pair_block(
+        scal, [near], early, [(side, F32)], early_rows, has_diag=True
+    )
+    next_acc, early_acc = pair_block(
+        scal, [next_p, next_m], early, [(side, F32)] * 2, early_rows, txt_old=early_acc
+    )
+    side_acc = [*near_acc, *next_acc]
+    t3, t4, across_p, across_m, side_acc, early_acc = tie(
+        (t3, t4, across_p, across_m, side_acc, early_acc)
+    )
+    late = cat([t3, t4])
+    late = [late, send_core(late)]
+    last = 3 * ROWS
+    (near_g, next_pg, next_mg, *across_acc), (gl_own, gl_sib) = pair_block(
+        scal, [*sides, across_p, across_m], late,
+        [(side, F32), (side, BF), (side, BF), (2 * ROWS, F32), (2 * ROWS, F32)],
+        [(last, F32), (last, BF)], img_old=side_acc,
+    )
+    (across_g,), (g_own, g_sib, ge_own, ge_sib) = pair_block(
+        scal, [across_p, across_m], early, [(side, BF)],
+        [(ROWS, F32), (ROWS, BF), (side, F32), (side, BF)],
+        img_old=across_acc, txt_old=early_acc,
+    )
+
+    def hop(value):
+        return send_ring(value.astype(BF), -1).astype(F32)
+
     late_sum = gl_own + send_core(gl_sib).astype(F32)
-    early_sum = ge_own + send_core(ge_sib).astype(F32)
-
-    next_pg, next_mg, late_sum, early_sum = tie((next_pg, next_mg, late_sum, early_sum))
-
-    def hop(value, k):
-        return send_z(value.astype(BF), k).astype(F32)
-
-    near_sum = near_g
-    for part, k in ((next_pg, -1), (next_mg, 1)):
-        near_sum = near_sum + send_xy(part, k, True).astype(F32)
-    own, s1, s2, s3 = [early_sum[n * ROWS : (n + 1) * ROWS] for n in range(4)]
-    s4 = late_sum[:ROWS]
-    cut = 2 * ROWS + half
-    low, high = hop(late_sum[ROWS:cut], -2), hop(late_sum[cut:], 2)
-    near_sum, low, high = tie((near_sum, low, high))
-
+    far = hop(late_sum[2 * ROWS :])
+    next_pg, next_mg = send_xy(next_pg, -1, True), send_xy(next_mg, 1, True)
+    across_g, next_pg, next_mg, _ = tie((across_g, next_pg, next_mg, far))
+    across_g = send_xy(across_g, 2, True)
+    near_sum = near_g + next_pg.astype(F32) + next_mg.astype(F32) + across_g.astype(F32)
+    early_back = send_core(cat([g_sib, ge_sib])).astype(F32)
+    far = hop(cat([late_sum[:ROWS] + far, late_sum[ROWS : 2 * ROWS]]))
+    far = hop(ge_own[2 * ROWS :] + early_back[3 * ROWS :] + far)
     near_back = near_sum.astype(BF)
     image_gu = near_sum[:ROWS]
     for n, k in ((1, 1), (2, -1), (3, 2)):
         back = send_xy(near_back[n * ROWS : (n + 1) * ROWS], -k, False)
         image_gu = image_gu + back.astype(F32)
-    s1, s2 = s1 + low[:ROWS], s2 + high[:ROWS]
-    s3 = cat([s3[:half] + low[ROWS:], s3[half:]])
-    s4 = cat([s4[:half], s4[half:] + high[ROWS:]])
-    text_gu = own + hop(s1, -1) + hop(s2, 1) + hop(s3, -2) + hop(s4, 2)
+    far = hop(ge_own[: 2 * ROWS] + early_back[ROWS : 3 * ROWS] + far)
+    text_gu = g_own + early_back[:ROWS] + far[:ROWS]
+    text_gu = text_gu + send_core(far[ROWS:].astype(BF)).astype(F32)
 
     d_image = image_backward(
         logit_scale * image_gu, image_unit, image_len, normed, inv_std, norm_gain, w_image

time: 102 us -> 91.2 us (0.89); the launches traced: 102 us -> 89.9 us
  starting transfers between devices: 41.3 us -> 29.3 us
  Pallas kernels: 11.1 us -> 13.9 us
  waiting for transfers between devices: 37.6 us -> 35.3 us
    ppermute x30 -> x27, starting transfers between devices: 41.3 us -> 29.3 us  [send(): lax.ppermute(value, AXES, [(flat(*p), flat(*target(*p))) for p in PLACES])]
    pallas_call x3 -> x4, Pallas kernels: 11.1 us -> 13.9 us  [pair_block(): pl.pallas_call(functools.partial(pair_kernel, counts, has_diag), out_shap...]
    ppermute x30 -> x27, waiting for transfers between devices: 37.6 us -> 35.3 us  [send(): lax.ppermute(value, AXES, [(flat(*p), flat(*target(*p))) for p in PLACES])]
  transfers between devices with their start and end apart: 30 -> 27, of which waited for: 13 -> 14; matrix products, arithmetic and copies ran while one was open for 3% -> 5% of each run, Pallas kernels for 8% -> 10%
where the time goes in v3:
time: 91.2 us; the launch traced here: 89.9 us
  waiting for transfers between devices  35.3 us (39%)
  starting transfers between devices  29.3 us (32%)
  Pallas kernels  13.9 us (15%)
  matrix products  6.15 us (7%)
  other arithmetic  2.62 us (3%)
  between operations  2.32 us (3%)
    ppermute x27, waiting for transfers between devices, send(): lax.ppermute(value, AXES, [(flat(*p), flat(*target(*p))) for p in PLACES])  35.3 us
    ppermute x27, starting transfers between devices, send(): lax.ppermute(value, AXES, [(flat(*p), flat(*target(*p))) for p in PLACES])  29.3 us
    pallas_call x4, Pallas kernels, pair_block(): pl.pallas_call(functools.partial(pair_kernel, counts, has_diag), out_shap...  13.9 us
    dot_general x1, matrix products, text_forward(): project = jnp.dot(features, weight, preferred_element_type=F32)  2.69 us
  transfers between devices with their start and end apart: 27, of which 14 were waited for; matrix products, arithmetic and copies ran while one was open for 5% of the time, Pallas kernels for 10%

profile of v3, /device:TPU:32, one launch (start us, length us, event | category | flops | bytes accessed | tf_op | source)
XLA Modules:
  0.0 89.9 jit_solution(12765712058099025390)
XLA Ops:
  0.6 0.0 copy-start
  0.7 2.7 %multiply_reduce_fusion.3 = (f32[64]{0:T(128)S(1)}, f32[64,1152]{1,0:T(8,128)S(1)}) fusion(bf16[64,1152]{1,0:T(8,128)(2,1)} %param.8, bf16[1152,1152]{1,0:T(8,128)(2,1)} %param.11), kind=kOutput, calls=%fused_computation.41 | convolution fusion | flops 170016704 | bytes 3096832 | tf_op jit(solution)/shard_map/dot_general | solution.py:67
  3.4 0.1 fusion.32
  3.5 0.1 collective-permute-start.5
  3.6 0.1 convert_reduce_fusion
  3.7 0.2 fusion.14
  4.0 0.7 multiply_reduce_fusion.2
  4.7 0.2 collective-permute-done.5
  5.0 2.0 %collective-permute-start.6 = (bf16[128,1152]{1,0:T(8,128)(2,1)S(1)}, bf16[128,1152]{1,0:T(8,128)(2,1)S(1)}, u32[]{:S(2)}, u32[]{:S(2)}) collective-permute-start(bf16[128,1152]{1,0:T(8,128)(2,1)S(1)} %constant_dynamic-update-slice_fusion.refs_1_.refs_2_), channel_id=1, source_target_pairs={{0,4},{64,92},{4,8},{68,64},{8,12},{72,68},{12,16},{76,72},{16,20}... | collective-permute-start | bytes 884744 | tf_op jit(solution)/shard_map/ppermute | solution.py:25
  7.0 0.1 fusion.33
  7.1 3.3 %collective-permute-start.2 = (bf16[64,1152]{1,0:T(8,128)(2,1)S(1)}, bf16[64,1152]{1,0:T(8,128)(2,1)S(1)}, u32[]{:S(2)}, u32[]{:S(2)}) collective-permute-start(bf16[64,1152]{1,0:T(8,128)(2,1)S(1)} %fusion.33), channel_id=1, source_target_pairs={{0,2},{64,96},{4,6},{68,100},{8,10},{72,104},{12,14},{76,108},{16,... | collective-permute-start | bytes 442376 | tf_op jit(solution)/shard_map/ppermute | solution.py:25
  10.3 1.1 %collective-permute-start.1 = (bf16[64,1152]{1,0:T(8,128)(2,1)S(1)}, bf16[64,1152]{1,0:T(8,128)(2,1)S(1)}, u32[]{:S(2)}, u32[]{:S(2)}) collective-permute-start(bf16[64,1152]{1,0:T(8,128)(2,1)S(1)} %fusion.33), channel_id=1, source_target_pairs={{0,3},{64,224},{4,7},{68,228},{8,11},{72,232},{12,15},{76,236},{16... | collective-permute-start | bytes 442376 | tf_op jit(solution)/shard_map/ppermute | solution.py:25
  11.4 1.0 %collective-permute-start = (bf16[64,1152]{1,0:T(8,128)(2,1)S(1)}, bf16[64,1152]{1,0:T(8,128)(2,1)S(1)}, u32[]{:S(2)}, u32[]{:S(2)}) collective-permute-start(bf16[64,1152]{1,0:T(8,128)(2,1)S(1)} %fusion.33), channel_id=1, source_target_pairs={{0,1},{64,192},{4,5},{68,196},{8,9},{72,200},{12,13},{76,204},{16,... | collective-permute-start | bytes 442376 | tf_op jit(solution)/shard_map/ppermute | solution.py:25
  12.4 1.9 %collective-permute-start.7 = (bf16[128,1152]{1,0:T(8,128)(2,1)S(1)}, bf16[128,1152]{1,0:T(8,128)(2,1)S(1)}, u32[]{:S(2)}, u32[]{:S(2)}) collective-permute-start(bf16[128,1152]{1,0:T(8,128)(2,1)S(1)} %collective-permute-done.6), channel_id=1, source_target_pairs={{0,4},{64,92},{4,8},{68,64},{8,12},{72,68},{12,16},{76,72},{16,20}... | collective-permute-start | bytes 884744 | tf_op jit(solution)/shard_map/ppermute | solution.py:25
  14.3 0.0 collective-permute-done.2
  14.3 1.4 %collective-permute-done.1 = bf16[64,1152]{1,0:T(8,128)(2,1)S(1)} collective-permute-done((bf16[64,1152]{1,0:T(8,128)(2,1)S(1)}, bf16[64,1152]{1,0:T(8,128)(2,1)S(1)}, u32[]{:S(2)}, u32[]{:S(2)}) %collective-permute-start.1) | collective-permute-done | bytes 147488 | tf_op jit(solution)/shard_map/ppermute | solution.py:25
  15.7 2.0 %collective-permute-done = bf16[64,1152]{1,0:T(8,128)(2,1)S(1)} collective-permute-done((bf16[64,1152]{1,0:T(8,128)(2,1)S(1)}, bf16[64,1152]{1,0:T(8,128)(2,1)S(1)}, u32[]{:S(2)}, u32[]{:S(2)}) %collective-permute-start) | collective-permute-done | bytes 147488 | tf_op jit(solution)/shard_map/ppermute | solution.py:25
  17.8 2.8 %collective-permute-start.4 = (bf16[256,1152]{1,0:T(8,128)(2,1)S(1)}, bf16[256,1152]{1,0:T(8,128)(2,1)S(1)}, u32[]{:S(2)}, u32[]{:S(2)}) collective-permute-start(bf16[256,1152]{1,0:T(8,128)(2,1)S(1)} %pad_maximum_fusion.1.refs_0_), channel_id=1, source_target_pairs={{0,160},{64,67},{4,164},{68,71},{8,168},{72,75},{12,172},{76,79},{... | collective-permute-start | bytes 1769480 | tf_op jit(solution)/shard_map/ppermute | solution.py:25
  20.6 0.0 collective-permute-start.3
  20.7 0.1 collective-permute-start.12
  20.8 2.0 %collective-permute-start.8 = (bf16[128,1152]{1,0:T(8,128)(2,1)S(1)}, bf16[128,1152]{1,0:T(8,128)(2,1)S(1)}, u32[]{:S(2)}, u32[]{:S(2)}) collective-permute-start(bf16[128,1152]{1,0:T(8,128)(2,1)S(1)} %collective-permute-done.7), channel_id=1, source_target_pairs={{0,4},{64,92},{4,8},{68,64},{8,12},{72,68},{12,16},{76,72},{16,20}... | collective-permute-start | bytes 884744 | tf_op jit(solution)/shard_map/ppermute | solution.py:25
  22.8 5.2 %collective-permute-done.4.refs_1_.refs_2_ = bf16[256,1152]{1,0:T(8,128)(2,1)S(1)} collective-permute-done((bf16[256,1152]{1,0:T(8,128)(2,1)S(1)}, bf16[256,1152]{1,0:T(8,128)(2,1)S(1)}, u32[]{:S(2)}, u32[]{:S(2)}) %collective-permute-start.4) | collective-permute-done | bytes 589856 | tf_op jit(solution)/shard_map/ppermute | solution.py:25
  28.1 3.8 %collective-permute-start.11 = (bf16[128,1152]{1,0:T(8,128)(2,1)S(1)}, bf16[128,1152]{1,0:T(8,128)(2,1)S(1)}, u32[]{:S(2)}, u32[]{:S(2)}) collective-permute-start(bf16[128,1152]{1,0:T(8,128)(2,1)S(1)} %slice.77), channel_id=1, source_target_pairs={{0,160},{64,67},{4,164},{68,71},{8,168},{72,75},{12,172},{76,79},{... | collective-permute-start | bytes 884744 | tf_op jit(solution)/shard_map/ppermute | solution.py:25
  31.9 0.1 collective-permute-start.10
  32.0 2.2 %collective-permute-start.9 = (bf16[64,1152]{1,0:T(8,128)(2,1)S(1)}, bf16[64,1152]{1,0:T(8,128)(2,1)S(1)}, u32[]{:S(2)}, u32[]{:S(2)}) collective-permute-start(bf16[64,1152]{1,0:T(8,128)(2,1)S(1)} %slice.75), channel_id=1, source_target_pairs={{0,4},{64,92},{4,8},{68,64},{8,12},{72,68},{12,16},{76,72},{16,20}... | collective-permute-start | bytes 442376 | tf_op jit(solution)/shard_map/ppermute | solution.py:25
  35.5 0.1 pad_maximum_fusion.3.scal
  35.6 2.5 %shard_map.86 = (f32[256,1152]{1,0:T(8,128)S(1)}, f32[64,1152]{1,0:T(8,128)S(1)}, f32[64,1152]{1,0:T(8,128)S(1)}, f32[256,1152]{1,0:T(8,128)S(1)}, f32[256,1152]{1,0:T(8,128)S(1)}) custom-call(f32[2]{0:T(128)S(1)} %pad_maximum_fusion.3.scal, bf16[256,1152]{1,0:T(8,128)(2,1)S(1)} %pad_maximum_fusion.1.refs_0_, ...), custom_call_target="tpu_custom_call" | custom-call | flops 1024 | bytes 1024 | tf_op jit(solution)/shard_map/pallas_call | solution.py:150
  38.1 4.3 %shard_map.87 = (f32[256,1152]{1,0:T(8,128)S(1)}, f32[256,1152]{1,0:T(8,128)S(1)}, f32[64,1152]{1,0:T(8,128)S(1)}, f32[64,1152]{1,0:T(8,128)S(1)}, f32[256,1152]{1,0:T(8,128)S(1)}, /*index=5*/f32[256,1152]{1,0:T(8,128)S(1)}) custom-call(f32[2]{0:T(128)S(1)} %pad_maximum_fusion.3.scal, bf16[256,1152]{1,0:T(8,128)(2,1)S(1)} %collective-permute-done.3.refs_0_.refs_1_, ...), custom_call_target="tpu_custom_call" | custom-call | flops 1024 | bytes 1024 | tf_op jit(solution)/shard_map/pallas_call | solution.py:150
  42.5 0.1 collective-permute-start.13
  42.6 1.8 %collective-permute-done.13.refs_6_ = bf16[192,1152]{1,0:T(8,128)(2,1)S(1)} collective-permute-done((bf16[192,1152]{1,0:T(8,128)(2,1)S(1)}, bf16[192,1152]{1,0:T(8,128)(2,1)S(1)}, u32[]{:S(2)}, u32[]{:S(2)}) %collective-permute-start.13) | collective-permute-done | bytes 442400 | tf_op jit(solution)/shard_map/ppermute | solution.py:25
  44.4 4.5 %shard_map.88 = (f32[256,1152]{1,0:T(8,128)S(1)}, bf16[256,1152]{1,0:T(8,128)(2,1)S(1)}, bf16[256,1152]{1,0:T(8,128)(2,1)S(1)}, f32[128,1152]{1,0:T(8,128)S(1)},...) custom-call(f32[2]{0:T(128)S(1)} %pad_maximum_fusion.3.scal, ...), custom_call_target="tpu_custom_call" | custom-call | flops 1024 | bytes 1024 | tf_op jit(solution)/shard_map/pallas_call | solution.py:150
  48.9 0.2 collective-permute-start.16
  49.2 3.2 %collective-permute-start.14 = (bf16[256,1152]{1,0:T(8,128)(2,1)S(1)}, bf16[256,1152]{1,0:T(8,128)(2,1)S(1)}, u32[]{:S(2)}, u32[]{:S(2)}) collective-permute-start(bf16[256,1152]{1,0:T(8,128)(2,1)S(1)} %get-tuple-element.69), channel_id=1, source_target_pairs={{0,160},{64,67},{4,164},{68,71},{8,168},{72,75},{12,172},{76,79},{... | collective-permute-start | bytes 1769480 | tf_op jit(solution)/shard_map/ppermute | solution.py:25
  52.4 0.0 collective-permute-start.15
  52.4 2.5 %shard_map.89 = (bf16[256,1152]{1,0:T(8,128)(2,1)S(1)}, f32[64,1152]{1,0:T(8,128)S(1)}, bf16[64,1152]{1,0:T(8,128)(2,1)S(1)}, f32[256,1152]{1,0:T(8,128)S(1)}, bf16[256,1152]{1,0:T(8,128)(2,1)S(1)}) custom-call(f32[2]{0:T(128)S(1)} %pad_maximum_fusion.3.scal, bf16[128,1152]{1,0:T(8,128)(2,1)S(1)} %collective-permute-done.10.refs_3_.refs_0_, ...), custom_call_target="tpu_custom_call" | custom-call | flops 1024 | bytes 1024 | tf_op jit(solution)/shard_map/pallas_call | solution.py:150
  54.9 0.1 fusion.36
  55.1 0.2 collective-permute-start.17
  55.3 0.1 pad_maximum_fusion
  55.3 1.4 %collective-permute-start.22 = (bf16[320,1152]{1,0:T(8,128)(2,1)S(1)}, bf16[320,1152]{1,0:T(8,128)(2,1)S(1)}, u32[]{:S(2)}, u32[]{:S(2)}) collective-permute-start(bf16[320,1152]{1,0:T(8,128)(2,1)S(1)} %pad_maximum_fusion), channel_id=1, source_target_pairs={{0,64},{64,0},{4,68},{68,4},{8,72},{72,8},{12,76},{76,12},{16,80},... | collective-permute-start | bytes 2211848 | tf_op jit(solution)/shard_map/ppermute | solution.py:25
  56.8 4.6 %collective-permute-done.17 = bf16[64,1152]{1,0:T(8,128)(2,1)S(1)} collective-permute-done((bf16[64,1152]{1,0:T(8,128)(2,1)S(1)}, bf16[64,1152]{1,0:T(8,128)(2,1)S(1)}, u32[]{:S(2)}, u32[]{:S(2)}) %collective-permute-start.17) | collective-permute-done | bytes 147488 | tf_op jit(solution)/shard_map/ppermute | solution.py:25
  61.5 0.1 collective-permute-start.23
  61.6 1.9 %collective-permute-done.15 = bf16[256,1152]{1,0:T(8,128)(2,1)S(1)} collective-permute-done((bf16[256,1152]{1,0:T(8,128)(2,1)S(1)}, bf16[256,1152]{1,0:T(8,128)(2,1)S(1)}, u32[]{:S(2)}, u32[]{:S(2)}) %collective-permute-start.15) | collective-permute-done | bytes 589856 | tf_op jit(solution)/shard_map/ppermute | solution.py:25
  63.5 0.1 convert_element_type.88
  63.6 4.7 %collective-permute-done.23 = bf16[128,1152]{1,0:T(8,128)(2,1)S(1)} collective-permute-done((bf16[128,1152]{1,0:T(8,128)(2,1)S(1)}, bf16[128,1152]{1,0:T(8,128)(2,1)S(1)}, u32[]{:S(2)}, u32[]{:S(2)}) %collective-permute-start.23) | collective-permute-done | bytes 294944 | tf_op jit(solution)/shard_map/ppermute | solution.py:25
  68.3 0.1 fusion.1
  68.3 0.1 collective-permute-start.24
  68.4 6.4 %collective-permute-done.18 = bf16[256,1152]{1,0:T(8,128)(2,1)S(1)} collective-permute-done((bf16[256,1152]{1,0:T(8,128)(2,1)S(1)}, bf16[256,1152]{1,0:T(8,128)(2,1)S(1)}, u32[]{:S(2)}, u32[]{:S(2)}) %collective-permute-start.18) | collective-permute-done | bytes 589856 | tf_op jit(solution)/shard_map/ppermute | solution.py:25
  74.9 0.3 fusion.37
  75.2 0.7 collective-permute-start.19
  75.9 1.2 %collective-permute-start.21 = (bf16[64,1152]{1,0:T(8,128)(2,1)S(1)}, bf16[64,1152]{1,0:T(8,128)(2,1)S(1)}, u32[]{:S(2)}, u32[]{:S(2)}) collective-permute-start(bf16[64,1152]{1,0:T(8,128)(2,1)S(1)} %get-tuple-element.89), channel_id=1, source_target_pairs={{0,2},{64,96},{4,6},{68,100},{8,10},{72,104},{12,14},{76,108},{16,... | collective-permute-start | bytes 442376 | tf_op jit(solution)/shard_map/ppermute | solution.py:25
  77.1 0.4 collective-permute-start.20
  77.5 0.1 fusion.3
  77.6 1.3 %collective-permute-start.25 = (bf16[128,1152]{1,0:T(8,128)(2,1)S(1)}, bf16[128,1152]{1,0:T(8,128)(2,1)S(1)}, u32[]{:S(2)}, u32[]{:S(2)}) collective-permute-start(bf16[128,1152]{1,0:T(8,128)(2,1)S(1)} %fusion.3), channel_id=1, source_target_pairs={{0,28},{64,68},{4,0},{68,72},{8,4},{72,76},{12,8},{76,80},{16,12},... | collective-permute-start | bytes 884744 | tf_op jit(solution)/shard_map/ppermute | solution.py:25
  78.9 1.5 %collective-permute-done.19 = bf16[64,1152]{1,0:T(8,128)(2,1)S(1)} collective-permute-done((bf16[64,1152]{1,0:T(8,128)(2,1)S(1)}, bf16[64,1152]{1,0:T(8,128)(2,1)S(1)}, u32[]{:S(2)}, u32[]{:S(2)}) %collective-permute-start.19) | collective-permute-done | bytes 147488 | tf_op jit(solution)/shard_map/ppermute | solution.py:25
  80.4 2.2 %collective-permute-done.21 = bf16[64,1152]{1,0:T(8,128)(2,1)S(1)} collective-permute-done((bf16[64,1152]{1,0:T(8,128)(2,1)S(1)}, bf16[64,1152]{1,0:T(8,128)(2,1)S(1)}, u32[]{:S(2)}, u32[]{:S(2)}) %collective-permute-start.21) | collective-permute-done | bytes 147488 | tf_op jit(solution)/shard_map/ppermute | solution.py:25
  82.6 1.5 %collective-permute-done.20 = bf16[64,1152]{1,0:T(8,128)(2,1)S(1)} collective-permute-done((bf16[64,1152]{1,0:T(8,128)(2,1)S(1)}, bf16[64,1152]{1,0:T(8,128)(2,1)S(1)}, u32[]{:S(2)}, u32[]{:S(2)}) %collective-permute-start.20) | collective-permute-done | bytes 147488 | tf_op jit(solution)/shard_map/ppermute | solution.py:25
  84.1 0.2 multiply_reduce_fusion.1
  84.3 1.1 %fusion.34 = (f32[64]{0:T(128)S(1)}, f32[64]{0:T(128)S(1)}, f32[64,1152]{1,0:T(8,128)S(1)}) fusion(f32[64]{0:T(128)S(1)} %add_rsqrt_fusion, f32[64]{0:T(128)S(1)} %broadcast_multiply_fusion.2, bf16[64,1152]{1,0:T(8,128)(2,1)S(1)} %copy-done.2, f32[1152]{0:T(1024)S(1)} %copy-done.3, bf16[1152,1152]{1,0:T(8,128)(2,1)S(1)} %copy-done, ...), kind=kOutput, calls=%fused_computation.67 | convolution fusion | flops 171270016 | bytes 4139524 | tf_op jit(solution)/shard_map/dot_general | solution.py:77
  85.4 1.2 %collective-permute-done.25 = bf16[128,1152]{1,0:T(8,128)(2,1)S(1)} collective-permute-done((bf16[128,1152]{1,0:T(8,128)(2,1)S(1)}, bf16[128,1152]{1,0:T(8,128)(2,1)S(1)}, u32[]{:S(2)}, u32[]{:S(2)}) %collective-permute-start.25) | collective-permute-done | bytes 294944 | tf_op jit(solution)/shard_map/ppermute | solution.py:25
  86.6 0.1 collective-permute-start.26
  86.7 0.8 fusion.13
  87.5 0.5 collective-permute-done.26
  88.1 0.2 multiply_reduce_fusion
  88.3 1.6 %convolution_convert_fusion = bf16[64,1152]{1,0:T(8,128)(2,1)} fusion(bf16[1152,1152]{1,0:T(8,128)(2,1)S(1)} %copy-done.1, f32[64,1152]{1,0:T(8,128)S(1)} %get-tuple-element.83, f32[64]{0:T(128)S(1)} %get-tuple-element.82, f32[64]{0:T(128)S(1)} %add_sqrt_fusion.1, f32[64,1152]{1,0:T(8,128)S(1)} %get-tuple-element.94), kind=kOutput, calls=%fused_computation.1 | convolution fusion | flops 170311680 | bytes 3392000 | tf_op jit(solution)/shard_map/dot_general | solution.py:89
  (40 shorter events, 0.4 us)
Async XLA Ops:
  0.6 3.3 %copy-start = (bf16[1152,1152]{1,0:T(8,128)(2,1)S(1)}, bf16[1152,1152]{1,0:T(8,128)(2,1)}, u32[]{:S(2)}) copy-start(bf16[1152,1152]{1,0:T(8,128)(2,1)} %param.10) | copy-start | bytes 7962628
  0.6 3.0 %copy-start.2 = (bf16[64,1152]{1,0:T(8,128)(2,1)S(1)}, bf16[64,1152]{1,0:T(8,128)(2,1)}, u32[]{:S(2)}) copy-start(bf16[64,1152]{1,0:T(8,128)(2,1)} %param.7) | copy-start | bytes 442372
  0.7 3.3 %copy-start.3 = (f32[1152]{0:T(1024)S(1)}, f32[1152]{0:T(1024)}, u32[]{:S(2)}) copy-start(f32[1152]{0:T(1024)} %param.9) | copy-start | bytes 13828
  3.5 1.5 %collective-permute-start.5 = (bf16[64,1152]{1,0:T(8,128)(2,1)S(1)}, bf16[64,1152]{1,0:T(8,128)(2,1)S(1)}, u32[]{:S(2)}, u32[]{:S(2)}) collective-permute-start(bf16[64,1152]{1,0:T(8,128)(2,1)S(1)} %fusion.32), channel_id=1, source_target_pairs={{0,64},{64,0},{4,68},{68,4},{8,72},{72,8},{12,76},{76,12},{16,80},... | collective-permute-start | bytes 442376 | tf_op jit(solution)/shard_map/ppermute | solution.py:25
  5.0 7.4 %collective-permute-start.6 = (bf16[128,1152]{1,0:T(8,128)(2,1)S(1)}, bf16[128,1152]{1,0:T(8,128)(2,1)S(1)}, u32[]{:S(2)}, u32[]{:S(2)}) collective-permute-start(bf16[128,1152]{1,0:T(8,128)(2,1)S(1)} %constant_dynamic-update-slice_fusion.refs_1_.refs_2_), channel_id=1, source_target_pairs={{0,4},{64,92},{4,8},{68,64},{8,12},{72,68},{12,16},{76,72},{16,20}... | collective-permute-start | bytes 884744 | tf_op jit(solution)/shard_map/ppermute | solution.py:25
  7.1 7.2 %collective-permute-start.2 = (bf16[64,1152]{1,0:T(8,128)(2,1)S(1)}, bf16[64,1152]{1,0:T(8,128)(2,1)S(1)}, u32[]{:S(2)}, u32[]{:S(2)}) collective-permute-start(bf16[64,1152]{1,0:T(8,128)(2,1)S(1)} %fusion.33), channel_id=1, source_target_pairs={{0,2},{64,96},{4,6},{68,100},{8,10},{72,104},{12,14},{76,108},{16,... | collective-permute-start | bytes 442376 | tf_op jit(solution)/shard_map/ppermute | solution.py:25
  10.3 5.4 %collective-permute-start.1 = (bf16[64,1152]{1,0:T(8,128)(2,1)S(1)}, bf16[64,1152]{1,0:T(8,128)(2,1)S(1)}, u32[]{:S(2)}, u32[]{:S(2)}) collective-permute-start(bf16[64,1152]{1,0:T(8,128)(2,1)S(1)} %fusion.33), channel_id=1, source_target_pairs={{0,3},{64,224},{4,7},{68,228},{8,11},{72,232},{12,15},{76,236},{16... | collective-permute-start | bytes 442376 | tf_op jit(solution)/shard_map/ppermute | solution.py:25
  11.4 6.4 %collective-permute-start = (bf16[64,1152]{1,0:T(8,128)(2,1)S(1)}, bf16[64,1152]{1,0:T(8,128)(2,1)S(1)}, u32[]{:S(2)}, u32[]{:S(2)}) collective-permute-start(bf16[64,1152]{1,0:T(8,128)(2,1)S(1)} %fusion.33), channel_id=1, source_target_pairs={{0,1},{64,192},{4,5},{68,196},{8,9},{72,200},{12,13},{76,204},{16,... | collective-permute-start | bytes 442376 | tf_op jit(solution)/shard_map/ppermute | solution.py:25
  12.4 8.3 %collective-permute-start.7 = (bf16[128,1152]{1,0:T(8,128)(2,1)S(1)}, bf16[128,1152]{1,0:T(8,128)(2,1)S(1)}, u32[]{:S(2)}, u32[]{:S(2)}) collective-permute-start(bf16[128,1152]{1,0:T(8,128)(2,1)S(1)} %collective-permute-done.6), channel_id=1, source_target_pairs={{0,4},{64,92},{4,8},{68,64},{8,12},{72,68},{12,16},{76,72},{16,20}... | collective-permute-start | bytes 884744 | tf_op jit(solution)/shard_map/ppermute | solution.py:25
  17.8 10.2 %collective-permute-start.4 = (bf16[256,1152]{1,0:T(8,128)(2,1)S(1)}, bf16[256,1152]{1,0:T(8,128)(2,1)S(1)}, u32[]{:S(2)}, u32[]{:S(2)}) collective-permute-start(bf16[256,1152]{1,0:T(8,128)(2,1)S(1)} %pad_maximum_fusion.1.refs_0_), channel_id=1, source_target_pairs={{0,160},{64,67},{4,164},{68,71},{8,168},{72,75},{12,172},{76,79},{... | collective-permute-start | bytes 1769480 | tf_op jit(solution)/shard_map/ppermute | solution.py:25
  20.6 11.2 %collective-permute-start.3 = (bf16[256,1152]{1,0:T(8,128)(2,1)S(1)}, bf16[256,1152]{1,0:T(8,128)(2,1)S(1)}, u32[]{:S(2)}, u32[]{:S(2)}) collective-permute-start(bf16[256,1152]{1,0:T(8,128)(2,1)S(1)} %pad_maximum_fusion.1.refs_0_), channel_id=1, source_target_pairs={{0,128},{64,65},{4,132},{68,69},{8,136},{72,73},{12,140},{76,77},{... | collective-permute-start | bytes 1769480 | tf_op jit(solution)/shard_map/ppermute | solution.py:25
  20.7 14.9 %collective-permute-start.12 = (bf16[256,1152]{1,0:T(8,128)(2,1)S(1)}, bf16[256,1152]{1,0:T(8,128)(2,1)S(1)}, u32[]{:S(2)}, u32[]{:S(2)}) collective-permute-start(bf16[256,1152]{1,0:T(8,128)(2,1)S(1)} %constant_dynamic-update-slice_fusion.2.refs_2_.refs_3_), channel_id=1, source_target_pairs={{0,64},{64,0},{4,68},{68,4},{8,72},{72,8},{12,76},{76,12},{16,80},... | collective-permute-start | bytes 1769480 | tf_op jit(solution)/shard_map/ppermute | solution.py:25
  20.8 11.1 %collective-permute-start.8 = (bf16[128,1152]{1,0:T(8,128)(2,1)S(1)}, bf16[128,1152]{1,0:T(8,128)(2,1)S(1)}, u32[]{:S(2)}, u32[]{:S(2)}) collective-permute-start(bf16[128,1152]{1,0:T(8,128)(2,1)S(1)} %collective-permute-done.7), channel_id=1, source_target_pairs={{0,4},{64,92},{4,8},{68,64},{8,12},{72,68},{12,16},{76,72},{16,20}... | collective-permute-start | bytes 884744 | tf_op jit(solution)/shard_map/ppermute | solution.py:25
  28.1 14.4 %collective-permute-start.11 = (bf16[128,1152]{1,0:T(8,128)(2,1)S(1)}, bf16[128,1152]{1,0:T(8,128)(2,1)S(1)}, u32[]{:S(2)}, u32[]{:S(2)}) collective-permute-start(bf16[128,1152]{1,0:T(8,128)(2,1)S(1)} %slice.77), channel_id=1, source_target_pairs={{0,160},{64,67},{4,164},{68,71},{8,168},{72,75},{12,172},{76,79},{... | collective-permute-start | bytes 884744 | tf_op jit(solution)/shard_map/ppermute | solution.py:25
  31.9 10.6 %collective-permute-start.10 = (bf16[128,1152]{1,0:T(8,128)(2,1)S(1)}, bf16[128,1152]{1,0:T(8,128)(2,1)S(1)}, u32[]{:S(2)}, u32[]{:S(2)}) collective-permute-start(bf16[128,1152]{1,0:T(8,128)(2,1)S(1)} %slice.76), channel_id=1, source_target_pairs={{0,128},{64,65},{4,132},{68,69},{8,136},{72,73},{12,140},{76,77},{... | collective-permute-start | bytes 884744 | tf_op jit(solution)/shard_map/ppermute | solution.py:25
  32.0 10.5 %collective-permute-start.9 = (bf16[64,1152]{1,0:T(8,128)(2,1)S(1)}, bf16[64,1152]{1,0:T(8,128)(2,1)S(1)}, u32[]{:S(2)}, u32[]{:S(2)}) collective-permute-start(bf16[64,1152]{1,0:T(8,128)(2,1)S(1)} %slice.75), channel_id=1, source_target_pairs={{0,4},{64,92},{4,8},{68,64},{8,12},{72,68},{12,16},{76,72},{16,20}... | collective-permute-start | bytes 442376 | tf_op jit(solution)/shard_map/ppermute | solution.py:25
  42.5 1.9 %collective-permute-start.13 = (bf16[192,1152]{1,0:T(8,128)(2,1)S(1)}, bf16[192,1152]{1,0:T(8,128)(2,1)S(1)}, u32[]{:S(2)}, u32[]{:S(2)}) collective-permute-start(bf16[192,1152]{1,0:T(8,128)(2,1)S(1)} %constant_dynamic-update-slice_fusion.4.refs_5_), channel_id=1, source_target_pairs={{0,64},{64,0},{4,68},{68,4},{8,72},{72,8},{12,76},{76,12},{16,80},... | collective-permute-start | bytes 1327112 | tf_op jit(solution)/shard_map/ppermute | solution.py:25
  48.9 6.0 %collective-permute-start.16 = (bf16[192,1152]{1,0:T(8,128)(2,1)S(1)}, bf16[192,1152]{1,0:T(8,128)(2,1)S(1)}, u32[]{:S(2)}, u32[]{:S(2)}) collective-permute-start(bf16[192,1152]{1,0:T(8,128)(2,1)S(1)} %get-tuple-element.72), channel_id=1, source_target_pairs={{0,64},{64,0},{4,68},{68,4},{8,72},{72,8},{12,76},{76,12},{16,80},... | collective-permute-start | bytes 1327112 | tf_op jit(solution)/shard_map/ppermute | solution.py:25
  49.2 12.4 %collective-permute-start.14 = (bf16[256,1152]{1,0:T(8,128)(2,1)S(1)}, bf16[256,1152]{1,0:T(8,128)(2,1)S(1)}, u32[]{:S(2)}, u32[]{:S(2)}) collective-permute-start(bf16[256,1152]{1,0:T(8,128)(2,1)S(1)} %get-tuple-element.69), channel_id=1, source_target_pairs={{0,160},{64,67},{4,164},{68,71},{8,168},{72,75},{12,172},{76,79},{... | collective-permute-start | bytes 1769480 | tf_op jit(solution)/shard_map/ppermute | solution.py:25
  52.4 11.1 %collective-permute-start.15 = (bf16[256,1152]{1,0:T(8,128)(2,1)S(1)}, bf16[256,1152]{1,0:T(8,128)(2,1)S(1)}, u32[]{:S(2)}, u32[]{:S(2)}) collective-permute-start(bf16[256,1152]{1,0:T(8,128)(2,1)S(1)} %get-tuple-element.70), channel_id=1, source_target_pairs={{0,128},{64,65},{4,132},{68,69},{8,136},{72,73},{12,140},{76,77},{... | collective-permute-start | bytes 1769480 | tf_op jit(solution)/shard_map/ppermute | solution.py:25
  55.1 6.3 %collective-permute-start.17 = (bf16[64,1152]{1,0:T(8,128)(2,1)S(1)}, bf16[64,1152]{1,0:T(8,128)(2,1)S(1)}, u32[]{:S(2)}, u32[]{:S(2)}) collective-permute-start(bf16[64,1152]{1,0:T(8,128)(2,1)S(1)} %get-tuple-element.91), channel_id=1, source_target_pairs={{0,28},{64,68},{4,0},{68,72},{8,4},{72,76},{12,8},{76,80},{16,12},... | collective-permute-start | bytes 442376 | tf_op jit(solution)/shard_map/ppermute | solution.py:25
  55.3 8.2 %collective-permute-start.22 = (bf16[320,1152]{1,0:T(8,128)(2,1)S(1)}, bf16[320,1152]{1,0:T(8,128)(2,1)S(1)}, u32[]{:S(2)}, u32[]{:S(2)}) collective-permute-start(bf16[320,1152]{1,0:T(8,128)(2,1)S(1)} %pad_maximum_fusion), channel_id=1, source_target_pairs={{0,64},{64,0},{4,68},{68,4},{8,72},{72,8},{12,76},{76,12},{16,80},... | collective-permute-start | bytes 2211848 | tf_op jit(solution)/shard_map/ppermute | solution.py:25
  61.5 6.8 %collective-permute-start.23 = (bf16[128,1152]{1,0:T(8,128)(2,1)S(1)}, bf16[128,1152]{1,0:T(8,128)(2,1)S(1)}, u32[]{:S(2)}, u32[]{:S(2)}) collective-permute-start(bf16[128,1152]{1,0:T(8,128)(2,1)S(1)} %pad_maximum_fusion.2), channel_id=1, source_target_pairs={{0,28},{64,68},{4,0},{68,72},{8,4},{72,76},{12,8},{76,80},{16,12},... | collective-permute-start | bytes 884744 | tf_op jit(solution)/shard_map/ppermute | solution.py:25
  63.5 11.4 %collective-permute-start.18 = (bf16[256,1152]{1,0:T(8,128)(2,1)S(1)}, bf16[256,1152]{1,0:T(8,128)(2,1)S(1)}, u32[]{:S(2)}, u32[]{:S(2)}) collective-permute-start(bf16[256,1152]{1,0:T(8,128)(2,1)S(1)} %get-tuple-element.75), channel_id=1, source_target_pairs={{0,32},{64,66},{4,36},{68,70},{8,40},{72,74},{12,44},{76,78},{16,4... | collective-permute-start | bytes 1769480 | tf_op jit(solution)/shard_map/ppermute | solution.py:25
  68.3 9.2 %collective-permute-start.24 = (bf16[128,1152]{1,0:T(8,128)(2,1)S(1)}, bf16[128,1152]{1,0:T(8,128)(2,1)S(1)}, u32[]{:S(2)}, u32[]{:S(2)}) collective-permute-start(bf16[128,1152]{1,0:T(8,128)(2,1)S(1)} %fusion.1), channel_id=1, source_target_pairs={{0,28},{64,68},{4,0},{68,72},{8,4},{72,76},{12,8},{76,80},{16,12},... | collective-permute-start | bytes 884744 | tf_op jit(solution)/shard_map/ppermute | solution.py:25
  75.2 5.2 %collective-permute-start.19 = (bf16[64,1152]{1,0:T(8,128)(2,1)S(1)}, bf16[64,1152]{1,0:T(8,128)(2,1)S(1)}, u32[]{:S(2)}, u32[]{:S(2)}) collective-permute-start(bf16[64,1152]{1,0:T(8,128)(2,1)S(1)} %get-tuple-element.88), channel_id=1, source_target_pairs={{0,3},{64,224},{4,7},{68,228},{8,11},{72,232},{12,15},{76,236},{16... | collective-permute-start | bytes 442376 | tf_op jit(solution)/shard_map/ppermute | solution.py:25
  75.9 6.7 %collective-permute-start.21 = (bf16[64,1152]{1,0:T(8,128)(2,1)S(1)}, bf16[64,1152]{1,0:T(8,128)(2,1)S(1)}, u32[]{:S(2)}, u32[]{:S(2)}) collective-permute-start(bf16[64,1152]{1,0:T(8,128)(2,1)S(1)} %get-tuple-element.89), channel_id=1, source_target_pairs={{0,2},{64,96},{4,6},{68,100},{8,10},{72,104},{12,14},{76,108},{16,... | collective-permute-start | bytes 442376 | tf_op jit(solution)/shard_map/ppermute | solution.py:25
  77.1 7.0 %collective-permute-start.20 = (bf16[64,1152]{1,0:T(8,128)(2,1)S(1)}, bf16[64,1152]{1,0:T(8,128)(2,1)S(1)}, u32[]{:S(2)}, u32[]{:S(2)}) collective-permute-start(bf16[64,1152]{1,0:T(8,128)(2,1)S(1)} %get-tuple-element.90), channel_id=1, source_target_pairs={{0,1},{64,192},{4,5},{68,196},{8,9},{72,200},{12,13},{76,204},{16,... | collective-permute-start | bytes 442376 | tf_op jit(solution)/shard_map/ppermute | solution.py:25
  77.6 9.0 %collective-permute-start.25 = (bf16[128,1152]{1,0:T(8,128)(2,1)S(1)}, bf16[128,1152]{1,0:T(8,128)(2,1)S(1)}, u32[]{:S(2)}, u32[]{:S(2)}) collective-permute-start(bf16[128,1152]{1,0:T(8,128)(2,1)S(1)} %fusion.3), channel_id=1, source_target_pairs={{0,28},{64,68},{4,0},{68,72},{8,4},{72,76},{12,8},{76,80},{16,12},... | collective-permute-start | bytes 884744 | tf_op jit(solution)/shard_map/ppermute | solution.py:25
  84.3 4.0 %copy-start.1 = (bf16[1152,1152]{1,0:T(8,128)(2,1)S(1)}, bf16[1152,1152]{1,0:T(8,128)(2,1)}, u32[]{:S(2)}) copy-start(bf16[1152,1152]{1,0:T(8,128)(2,1)} %param.11) | copy-start | bytes 7962628
  86.6 1.5 %collective-permute-start.26 = (bf16[64,1152]{1,0:T(8,128)(2,1)S(1)}, bf16[64,1152]{1,0:T(8,128)(2,1)S(1)}, u32[]{:S(2)}, u32[]{:S(2)}) collective-permute-start(bf16[64,1152]{1,0:T(8,128)(2,1)S(1)} %slice.89), channel_id=1, source_target_pairs={{0,64},{64,0},{4,68},{68,4},{8,72},{72,8},{12,76},{76,12},{16,80},... | collective-permute-start | bytes 442376 | tf_op jit(solution)/shard_map/ppermute | solution.py:25

commit v4 on v3

--- a/solution.py
+++ b/solution.py
@@ -106,8 +106,8 @@
     for group, whole in ((images, img), (texts, txt)):
         for ref, place in spans(group):
             whole[place, :] = ref[...]
-    slope = -scal[0] * LOG2E
-    offset = -scal[1] * LOG2E
+    slope = scal[:, :1] * -LOG2E
+    offset = scal[:, 1:2] * -LOG2E
     width = 256
     for at in range(0, txt.shape[0], width):
         cols = pl.ds(at, min(width, txt.shape[0] - at))
@@ -150,7 +150,7 @@
     got = pl.pallas_call(
         functools.partial(pair_kernel, counts, has_diag),
         out_shape=outs,
-        in_specs=[pl.BlockSpec(memory_space=pltpu.SMEM)] + [vmem] * len(operands),
+        in_specs=[vmem] * (1 + len(operands)),
         out_specs=[vmem] * len(outs),
         scratch_shapes=[
             pltpu.VMEM((m, width), BF),
@@ -167,7 +167,7 @@
     cat = jnp.concatenate
     tie = lax.optimization_barrier
     logit_scale = jnp.exp(log_scale)
-    scal = cat([logit_scale, bias])
+    scal = cat([logit_scale, bias]).reshape(1, 2)
 
     text_emb, text_unit, text_len = text_forward(text_feat, w_text)
     text_emb, image_feat = tie((text_emb, image_feat))

time: 91.2 us -> 89 us (0.976)
  Pallas kernels: 13.9 us -> 11.8 us
  waiting for transfers between devices: 35.3 us -> 36.3 us
    pallas_call x4, Pallas kernels: 13.9 us -> 11.8 us  [pair_block(): pl.pallas_call(functools.partial(pair_kernel, counts, has_diag), out_shap...]
    ppermute x27, waiting for transfers between devices: 35.3 us -> 36.3 us  [send(): lax.ppermute(value, AXES, [(flat(*p), flat(*target(*p))) for p in PLACES])]
  transfers between devices with their start and end apart: 27 -> 27, of which waited for: 14 -> 14; matrix products, arithmetic and copies ran while one was open for 5% -> 5% of each run, Pallas kernels for 10% -> 9%
where the time goes in v4:
time: 89 us; the launch traced here: 88.3 us
  waiting for transfers between devices  36.3 us (41%)
  starting transfers between devices  28.8 us (32%)
  Pallas kernels  11.8 us (13%)
  matrix products  6.15 us (7%)
  other arithmetic  2.62 us (3%)
  between operations  2.32 us (3%)
    ppermute x27, waiting for transfers between devices, send(): lax.ppermute(value, AXES, [(flat(*p), flat(*target(*p))) for p in PLACES])  36.3 us
    ppermute x27, starting transfers between devices, send(): lax.ppermute(value, AXES, [(flat(*p), flat(*target(*p))) for p in PLACES])  28.8 us
    pallas_call x4, Pallas kernels, pair_block(): pl.pallas_call(functools.partial(pair_kernel, counts, has_diag), out_shap...  11.8 us
    dot_general x1, matrix products, text_forward(): project = jnp.dot(features, weight, preferred_element_type=F32)  2.69 us
  transfers between devices with their start and end apart: 27, of which 14 were waited for; matrix products, arithmetic and copies ran while one was open for 5% of the time, Pallas kernels for 9%

profile of v4, /device:TPU:32, one launch (start us, length us, event | category | flops | bytes accessed | tf_op | source)
XLA Modules:
  0.0 88.3 jit_solution(5442432822682634745)
XLA Ops:
  0.6 0.0 copy-start
  0.7 2.7 %multiply_reduce_fusion.3 = (f32[64]{0:T(128)S(1)}, f32[64,1152]{1,0:T(8,128)S(1)}) fusion(bf16[64,1152]{1,0:T(8,128)(2,1)} %param.8, bf16[1152,1152]{1,0:T(8,128)(2,1)} %param.11), kind=kOutput, calls=%fused_computation.41 | convolution fusion | flops 170016704 | bytes 3096832 | tf_op jit(solution)/shard_map/dot_general | solution.py:67
  3.4 0.1 fusion.32
  3.5 0.1 collective-permute-start.5
  3.6 0.1 convert_reduce_fusion
  3.7 0.2 fusion.14
  4.0 0.7 multiply_reduce_fusion.2
  4.7 0.2 collective-permute-done.5
  5.0 2.0 %collective-permute-start.6 = (bf16[128,1152]{1,0:T(8,128)(2,1)S(1)}, bf16[128,1152]{1,0:T(8,128)(2,1)S(1)}, u32[]{:S(2)}, u32[]{:S(2)}) collective-permute-start(bf16[128,1152]{1,0:T(8,128)(2,1)S(1)} %constant_dynamic-update-slice_fusion.refs_1_.refs_2_), channel_id=1, source_target_pairs={{0,4},{64,92},{4,8},{68,64},{8,12},{72,68},{12,16},{76,72},{16,20}... | collective-permute-start | bytes 884744 | tf_op jit(solution)/shard_map/ppermute | solution.py:25
  7.0 0.1 fusion.33
  7.1 3.3 %collective-permute-start.2 = (bf16[64,1152]{1,0:T(8,128)(2,1)S(1)}, bf16[64,1152]{1,0:T(8,128)(2,1)S(1)}, u32[]{:S(2)}, u32[]{:S(2)}) collective-permute-start(bf16[64,1152]{1,0:T(8,128)(2,1)S(1)} %fusion.33), channel_id=1, source_target_pairs={{0,2},{64,96},{4,6},{68,100},{8,10},{72,104},{12,14},{76,108},{16,... | collective-permute-start | bytes 442376 | tf_op jit(solution)/shard_map/ppermute | solution.py:25
  10.3 1.1 %collective-permute-start.1 = (bf16[64,1152]{1,0:T(8,128)(2,1)S(1)}, bf16[64,1152]{1,0:T(8,128)(2,1)S(1)}, u32[]{:S(2)}, u32[]{:S(2)}) collective-permute-start(bf16[64,1152]{1,0:T(8,128)(2,1)S(1)} %fusion.33), channel_id=1, source_target_pairs={{0,3},{64,224},{4,7},{68,228},{8,11},{72,232},{12,15},{76,236},{16... | collective-permute-start | bytes 442376 | tf_op jit(solution)/shard_map/ppermute | solution.py:25
  11.4 1.0 %collective-permute-start = (bf16[64,1152]{1,0:T(8,128)(2,1)S(1)}, bf16[64,1152]{1,0:T(8,128)(2,1)S(1)}, u32[]{:S(2)}, u32[]{:S(2)}) collective-permute-start(bf16[64,1152]{1,0:T(8,128)(2,1)S(1)} %fusion.33), channel_id=1, source_target_pairs={{0,1},{64,192},{4,5},{68,196},{8,9},{72,200},{12,13},{76,204},{16,... | collective-permute-start | bytes 442376 | tf_op jit(solution)/shard_map/ppermute | solution.py:25
  12.4 0.0 collective-permute-done.6
  12.4 1.9 %collective-permute-start.7 = (bf16[128,1152]{1,0:T(8,128)(2,1)S(1)}, bf16[128,1152]{1,0:T(8,128)(2,1)S(1)}, u32[]{:S(2)}, u32[]{:S(2)}) collective-permute-start(bf16[128,1152]{1,0:T(8,128)(2,1)S(1)} %collective-permute-done.6), channel_id=1, source_target_pairs={{0,4},{64,92},{4,8},{68,64},{8,12},{72,68},{12,16},{76,72},{16,20}... | collective-permute-start | bytes 884744 | tf_op jit(solution)/shard_map/ppermute | solution.py:25
  14.3 0.0 collective-permute-done.2
  14.3 1.4 %collective-permute-done.1 = bf16[64,1152]{1,0:T(8,128)(2,1)S(1)} collective-permute-done((bf16[64,1152]{1,0:T(8,128)(2,1)S(1)}, bf16[64,1152]{1,0:T(8,128)(2,1)S(1)}, u32[]{:S(2)}, u32[]{:S(2)}) %collective-permute-start.1) | collective-permute-done | bytes 147488 | tf_op jit(solution)/shard_map/ppermute | solution.py:25
  15.7 2.0 %collective-permute-done = bf16[64,1152]{1,0:T(8,128)(2,1)S(1)} collective-permute-done((bf16[64,1152]{1,0:T(8,128)(2,1)S(1)}, bf16[64,1152]{1,0:T(8,128)(2,1)S(1)}, u32[]{:S(2)}, u32[]{:S(2)}) %collective-permute-start) | collective-permute-done | bytes 147488 | tf_op jit(solution)/shard_map/ppermute | solution.py:25
  17.8 2.8 %collective-permute-start.4 = (bf16[256,1152]{1,0:T(8,128)(2,1)S(1)}, bf16[256,1152]{1,0:T(8,128)(2,1)S(1)}, u32[]{:S(2)}, u32[]{:S(2)}) collective-permute-start(bf16[256,1152]{1,0:T(8,128)(2,1)S(1)} %pad_maximum_fusion.1.refs_0_), channel_id=1, source_target_pairs={{0,160},{64,67},{4,164},{68,71},{8,168},{72,75},{12,172},{76,79},{... | collective-permute-start | bytes 1769480 | tf_op jit(solution)/shard_map/ppermute | solution.py:25
  20.7 0.1 collective-permute-start.12
  20.8 2.0 %collective-permute-start.8 = (bf16[128,1152]{1,0:T(8,128)(2,1)S(1)}, bf16[128,1152]{1,0:T(8,128)(2,1)S(1)}, u32[]{:S(2)}, u32[]{:S(2)}) collective-permute-start(bf16[128,1152]{1,0:T(8,128)(2,1)S(1)} %collective-permute-done.7), channel_id=1, source_target_pairs={{0,4},{64,92},{4,8},{68,64},{8,12},{72,68},{12,16},{76,72},{16,20}... | collective-permute-start | bytes 884744 | tf_op jit(solution)/shard_map/ppermute | solution.py:25
  22.8 5.2 %collective-permute-done.4.refs_1_.refs_2_ = bf16[256,1152]{1,0:T(8,128)(2,1)S(1)} collective-permute-done((bf16[256,1152]{1,0:T(8,128)(2,1)S(1)}, bf16[256,1152]{1,0:T(8,128)(2,1)S(1)}, u32[]{:S(2)}, u32[]{:S(2)}) %collective-permute-start.4) | collective-permute-done | bytes 589856 | tf_op jit(solution)/shard_map/ppermute | solution.py:25
  28.1 3.8 %collective-permute-start.11 = (bf16[128,1152]{1,0:T(8,128)(2,1)S(1)}, bf16[128,1152]{1,0:T(8,128)(2,1)S(1)}, u32[]{:S(2)}, u32[]{:S(2)}) collective-permute-start(bf16[128,1152]{1,0:T(8,128)(2,1)S(1)} %slice.77), channel_id=1, source_target_pairs={{0,160},{64,67},{4,164},{68,71},{8,168},{72,75},{12,172},{76,79},{... | collective-permute-start | bytes 884744 | tf_op jit(solution)/shard_map/ppermute | solution.py:25
  31.9 0.1 collective-permute-start.10
  32.0 2.2 %collective-permute-start.9 = (bf16[64,1152]{1,0:T(8,128)(2,1)S(1)}, bf16[64,1152]{1,0:T(8,128)(2,1)S(1)}, u32[]{:S(2)}, u32[]{:S(2)}) collective-permute-start(bf16[64,1152]{1,0:T(8,128)(2,1)S(1)} %slice.75), channel_id=1, source_target_pairs={{0,4},{64,92},{4,8},{68,64},{8,12},{72,68},{12,16},{76,72},{16,20}... | collective-permute-start | bytes 442376 | tf_op jit(solution)/shard_map/ppermute | solution.py:25
  35.5 0.1 maximum_bitcast_fusion.scal
  35.6 2.0 %shard_map.86 = (f32[256,1152]{1,0:T(8,128)S(1)}, f32[64,1152]{1,0:T(8,128)S(1)}, f32[64,1152]{1,0:T(8,128)S(1)}, f32[256,1152]{1,0:T(8,128)S(1)}, f32[256,1152]{1,0:T(8,128)S(1)}) custom-call(f32[1,2]{1,0:T(1,128)S(1)} %maximum_bitcast_fusion.scal, bf16[256,1152]{1,0:T(8,128)(2,1)S(1)} %pad_maximum_fusion.1.refs_0_, ...), custom_call_target="tpu_custom_call" | custom-call | flops 1024 | bytes 1024 | tf_op jit(solution)/shard_map/pallas_call | solution.py:150
  37.5 3.8 %shard_map.87 = (f32[256,1152]{1,0:T(8,128)S(1)}, f32[256,1152]{1,0:T(8,128)S(1)}, f32[64,1152]{1,0:T(8,128)S(1)}, f32[64,1152]{1,0:T(8,128)S(1)}, f32[256,1152]{1,0:T(8,128)S(1)}, /*index=5*/f32[256,1152]{1,0:T(8,128)S(1)}) custom-call(f32[1,2]{1,0:T(1,128)S(1)} %maximum_bitcast_fusion.scal, bf16[256,1152]{1,0:T(8,128)(2,1)S(1)} %collective-permute-done.3.refs_0_.refs_1_, ...), custom_call_target="tpu_custom_call" | custom-call | flops 1024 | bytes 1024 | tf_op jit(solution)/shard_map/pallas_call | solution.py:150
  41.4 0.1 collective-permute-start.13
  41.5 1.8 %collective-permute-done.13.refs_6_ = bf16[192,1152]{1,0:T(8,128)(2,1)S(1)} collective-permute-done((bf16[192,1152]{1,0:T(8,128)(2,1)S(1)}, bf16[192,1152]{1,0:T(8,128)(2,1)S(1)}, u32[]{:S(2)}, u32[]{:S(2)}) %collective-permute-start.13) | collective-permute-done | bytes 442400 | tf_op jit(solution)/shard_map/ppermute | solution.py:25
  43.3 4.1 %shard_map.88 = (f32[256,1152]{1,0:T(8,128)S(1)}, bf16[256,1152]{1,0:T(8,128)(2,1)S(1)}, bf16[256,1152]{1,0:T(8,128)(2,1)S(1)}, f32[128,1152]{1,0:T(8,128)S(1)},...) custom-call(f32[1,2]{1,0:T(1,128)S(1)} %maximum_bitcast_fusion.scal, ...), custom_call_target="tpu_custom_call" | custom-call | flops 1024 | bytes 1024 | tf_op jit(solution)/shard_map/pallas_call | solution.py:150
  47.4 0.2 collective-permute-start.16
  47.6 3.2 %collective-permute-start.14 = (bf16[256,1152]{1,0:T(8,128)(2,1)S(1)}, bf16[256,1152]{1,0:T(8,128)(2,1)S(1)}, u32[]{:S(2)}, u32[]{:S(2)}) collective-permute-start(bf16[256,1152]{1,0:T(8,128)(2,1)S(1)} %get-tuple-element.69), channel_id=1, source_target_pairs={{0,160},{64,67},{4,164},{68,71},{8,168},{72,75},{12,172},{76,79},{... | collective-permute-start | bytes 1769480 | tf_op jit(solution)/shard_map/ppermute | solution.py:25
  50.8 0.0 collective-permute-start.15
  50.8 2.0 %shard_map.89 = (bf16[256,1152]{1,0:T(8,128)(2,1)S(1)}, f32[64,1152]{1,0:T(8,128)S(1)}, bf16[64,1152]{1,0:T(8,128)(2,1)S(1)}, f32[256,1152]{1,0:T(8,128)S(1)}, bf16[256,1152]{1,0:T(8,128)(2,1)S(1)}) custom-call(f32[1,2]{1,0:T(1,128)S(1)} %maximum_bitcast_fusion.scal, bf16[128,1152]{1,0:T(8,128)(2,1)S(1)} %collective-permute-done.10.refs_3_.refs_0_, ...), custom_call_target="tpu_custom_call" | custom-call | flops 1024 | bytes 1024 | tf_op jit(solution)/shard_map/pallas_call | solution.py:150
  52.9 0.1 fusion.36
  53.0 0.2 collective-permute-start.17
  53.2 0.1 pad_maximum_fusion
  53.2 1.5 %collective-permute-start.22 = (bf16[320,1152]{1,0:T(8,128)(2,1)S(1)}, bf16[320,1152]{1,0:T(8,128)(2,1)S(1)}, u32[]{:S(2)}, u32[]{:S(2)}) collective-permute-start(bf16[320,1152]{1,0:T(8,128)(2,1)S(1)} %pad_maximum_fusion), channel_id=1, source_target_pairs={{0,64},{64,0},{4,68},{68,4},{8,72},{72,8},{12,76},{76,12},{16,80},... | collective-permute-start | bytes 2211848 | tf_op jit(solution)/shard_map/ppermute | solution.py:25
  54.7 4.6 %collective-permute-done.17 = bf16[64,1152]{1,0:T(8,128)(2,1)S(1)} collective-permute-done((bf16[64,1152]{1,0:T(8,128)(2,1)S(1)}, bf16[64,1152]{1,0:T(8,128)(2,1)S(1)}, u32[]{:S(2)}, u32[]{:S(2)}) %collective-permute-start.17) | collective-permute-done | bytes 147488 | tf_op jit(solution)/shard_map/ppermute | solution.py:25
  59.4 0.1 collective-permute-start.23
  59.5 2.4 %collective-permute-done.15 = bf16[256,1152]{1,0:T(8,128)(2,1)S(1)} collective-permute-done((bf16[256,1152]{1,0:T(8,128)(2,1)S(1)}, bf16[256,1152]{1,0:T(8,128)(2,1)S(1)}, u32[]{:S(2)}, u32[]{:S(2)}) %collective-permute-start.15) | collective-permute-done | bytes 589856 | tf_op jit(solution)/shard_map/ppermute | solution.py:25
  61.9 0.1 convert_element_type.88
  62.0 4.2 %collective-permute-done.23 = bf16[128,1152]{1,0:T(8,128)(2,1)S(1)} collective-permute-done((bf16[128,1152]{1,0:T(8,128)(2,1)S(1)}, bf16[128,1152]{1,0:T(8,128)(2,1)S(1)}, u32[]{:S(2)}, u32[]{:S(2)}) %collective-permute-start.23) | collective-permute-done | bytes 294944 | tf_op jit(solution)/shard_map/ppermute | solution.py:25
  66.2 0.1 fusion.1
  66.3 0.1 collective-permute-start.24
  66.4 7.0 %collective-permute-done.18 = bf16[256,1152]{1,0:T(8,128)(2,1)S(1)} collective-permute-done((bf16[256,1152]{1,0:T(8,128)(2,1)S(1)}, bf16[256,1152]{1,0:T(8,128)(2,1)S(1)}, u32[]{:S(2)}, u32[]{:S(2)}) %collective-permute-start.18) | collective-permute-done | bytes 589856 | tf_op jit(solution)/shard_map/ppermute | solution.py:25
  73.3 0.3 fusion.37
  73.6 0.7 collective-permute-start.19
  74.3 1.2 %collective-permute-start.21 = (bf16[64,1152]{1,0:T(8,128)(2,1)S(1)}, bf16[64,1152]{1,0:T(8,128)(2,1)S(1)}, u32[]{:S(2)}, u32[]{:S(2)}) collective-permute-start(bf16[64,1152]{1,0:T(8,128)(2,1)S(1)} %get-tuple-element.89), channel_id=1, source_target_pairs={{0,2},{64,96},{4,6},{68,100},{8,10},{72,104},{12,14},{76,108},{16,... | collective-permute-start | bytes 442376 | tf_op jit(solution)/shard_map/ppermute | solution.py:25
  75.5 0.4 collective-permute-start.20
  75.9 0.1 fusion.3
  76.0 0.8 collective-permute-start.25
  76.8 2.0 %collective-permute-done.19 = bf16[64,1152]{1,0:T(8,128)(2,1)S(1)} collective-permute-done((bf16[64,1152]{1,0:T(8,128)(2,1)S(1)}, bf16[64,1152]{1,0:T(8,128)(2,1)S(1)}, u32[]{:S(2)}, u32[]{:S(2)}) %collective-permute-start.19) | collective-permute-done | bytes 147488 | tf_op jit(solution)/shard_map/ppermute | solution.py:25
  78.8 2.2 %collective-permute-done.21 = bf16[64,1152]{1,0:T(8,128)(2,1)S(1)} collective-permute-done((bf16[64,1152]{1,0:T(8,128)(2,1)S(1)}, bf16[64,1152]{1,0:T(8,128)(2,1)S(1)}, u32[]{:S(2)}, u32[]{:S(2)}) %collective-permute-start.21) | collective-permute-done | bytes 147488 | tf_op jit(solution)/shard_map/ppermute | solution.py:25
  81.0 1.5 %collective-permute-done.20 = bf16[64,1152]{1,0:T(8,128)(2,1)S(1)} collective-permute-done((bf16[64,1152]{1,0:T(8,128)(2,1)S(1)}, bf16[64,1152]{1,0:T(8,128)(2,1)S(1)}, u32[]{:S(2)}, u32[]{:S(2)}) %collective-permute-start.20) | collective-permute-done | bytes 147488 | tf_op jit(solution)/shard_map/ppermute | solution.py:25
  82.5 0.2 multiply_reduce_fusion.1
  82.8 1.1 %fusion.34 = (f32[64]{0:T(128)S(1)}, f32[64]{0:T(128)S(1)}, f32[64,1152]{1,0:T(8,128)S(1)}) fusion(f32[64]{0:T(128)S(1)} %add_rsqrt_fusion, f32[64]{0:T(128)S(1)} %broadcast_multiply_fusion.2, bf16[64,1152]{1,0:T(8,128)(2,1)S(1)} %copy-done.2, f32[1152]{0:T(1024)S(1)} %copy-done.3, bf16[1152,1152]{1,0:T(8,128)(2,1)S(1)} %copy-done, ...), kind=kOutput, calls=%fused_computation.67 | convolution fusion | flops 171270016 | bytes 4139524 | tf_op jit(solution)/shard_map/dot_general | solution.py:77
  83.9 1.2 %collective-permute-done.25 = bf16[128,1152]{1,0:T(8,128)(2,1)S(1)} collective-permute-done((bf16[128,1152]{1,0:T(8,128)(2,1)S(1)}, bf16[128,1152]{1,0:T(8,128)(2,1)S(1)}, u32[]{:S(2)}, u32[]{:S(2)}) %collective-permute-start.25) | collective-permute-done | bytes 294944 | tf_op jit(solution)/shard_map/ppermute | solution.py:25
  85.0 0.1 collective-permute-start.26
  85.1 0.8 fusion.13
  85.9 0.5 collective-permute-done.26
  86.5 0.2 multiply_reduce_fusion
  86.7 1.6 %convolution_convert_fusion = bf16[64,1152]{1,0:T(8,128)(2,1)} fusion(bf16[1152,1152]{1,0:T(8,128)(2,1)S(1)} %copy-done.1, f32[64,1152]{1,0:T(8,128)S(1)} %get-tuple-element.83, f32[64]{0:T(128)S(1)} %get-tuple-element.82, f32[64]{0:T(128)S(1)} %add_sqrt_fusion.1, f32[64,1152]{1,0:T(8,128)S(1)} %get-tuple-element.94), kind=kOutput, calls=%fused_computation.1 | convolution fusion | flops 170311680 | bytes 3392000 | tf_op jit(solution)/shard_map/dot_general | solution.py:89
  (40 shorter events, 0.4 us)
Async XLA Ops:
  0.6 3.3 %copy-start = (bf16[1152,1152]{1,0:T(8,128)(2,1)S(1)}, bf16[1152,1152]{1,0:T(8,128)(2,1)}, u32[]{:S(2)}) copy-start(bf16[1152,1152]{1,0:T(8,128)(2,1)} %param.10) | copy-start | bytes 7962628
  0.6 3.0 %copy-start.2 = (bf16[64,1152]{1,0:T(8,128)(2,1)S(1)}, bf16[64,1152]{1,0:T(8,128)(2,1)}, u32[]{:S(2)}) copy-start(bf16[64,1152]{1,0:T(8,128)(2,1)} %param.7) | copy-start | bytes 442372
  0.7 3.3 %copy-start.3 = (f32[1152]{0:T(1024)S(1)}, f32[1152]{0:T(1024)}, u32[]{:S(2)}) copy-start(f32[1152]{0:T(1024)} %param.9) | copy-start | bytes 13828
  3.5 1.5 %collective-permute-start.5 = (bf16[64,1152]{1,0:T(8,128)(2,1)S(1)}, bf16[64,1152]{1,0:T(8,128)(2,1)S(1)}, u32[]{:S(2)}, u32[]{:S(2)}) collective-permute-start(bf16[64,1152]{1,0:T(8,128)(2,1)S(1)} %fusion.32), channel_id=1, source_target_pairs={{0,64},{64,0},{4,68},{68,4},{8,72},{72,8},{12,76},{76,12},{16,80},... | collective-permute-start | bytes 442376 | tf_op jit(solution)/shard_map/ppermute | solution.py:25
  5.0 7.4 %collective-permute-start.6 = (bf16[128,1152]{1,0:T(8,128)(2,1)S(1)}, bf16[128,1152]{1,0:T(8,128)(2,1)S(1)}, u32[]{:S(2)}, u32[]{:S(2)}) collective-permute-start(bf16[128,1152]{1,0:T(8,128)(2,1)S(1)} %constant_dynamic-update-slice_fusion.refs_1_.refs_2_), channel_id=1, source_target_pairs={{0,4},{64,92},{4,8},{68,64},{8,12},{72,68},{12,16},{76,72},{16,20}... | collective-permute-start | bytes 884744 | tf_op jit(solution)/shard_map/ppermute | solution.py:25
  7.1 7.2 %collective-permute-start.2 = (bf16[64,1152]{1,0:T(8,128)(2,1)S(1)}, bf16[64,1152]{1,0:T(8,128)(2,1)S(1)}, u32[]{:S(2)}, u32[]{:S(2)}) collective-permute-start(bf16[64,1152]{1,0:T(8,128)(2,1)S(1)} %fusion.33), channel_id=1, source_target_pairs={{0,2},{64,96},{4,6},{68,100},{8,10},{72,104},{12,14},{76,108},{16,... | collective-permute-start | bytes 442376 | tf_op jit(solution)/shard_map/ppermute | solution.py:25
  10.3 5.4 %collective-permute-start.1 = (bf16[64,1152]{1,0:T(8,128)(2,1)S(1)}, bf16[64,1152]{1,0:T(8,128)(2,1)S(1)}, u32[]{:S(2)}, u32[]{:S(2)}) collective-permute-start(bf16[64,1152]{1,0:T(8,128)(2,1)S(1)} %fusion.33), channel_id=1, source_target_pairs={{0,3},{64,224},{4,7},{68,228},{8,11},{72,232},{12,15},{76,236},{16... | collective-permute-start | bytes 442376 | tf_op jit(solution)/shard_map/ppermute | solution.py:25
  11.4 6.4 %collective-permute-start = (bf16[64,1152]{1,0:T(8,128)(2,1)S(1)}, bf16[64,1152]{1,0:T(8,128)(2,1)S(1)}, u32[]{:S(2)}, u32[]{:S(2)}) collective-permute-start(bf16[64,1152]{1,0:T(8,128)(2,1)S(1)} %fusion.33), channel_id=1, source_target_pairs={{0,1},{64,192},{4,5},{68,196},{8,9},{72,200},{12,13},{76,204},{16,... | collective-permute-start | bytes 442376 | tf_op jit(solution)/shard_map/ppermute | solution.py:25
  12.4 8.3 %collective-permute-start.7 = (bf16[128,1152]{1,0:T(8,128)(2,1)S(1)}, bf16[128,1152]{1,0:T(8,128)(2,1)S(1)}, u32[]{:S(2)}, u32[]{:S(2)}) collective-permute-start(bf16[128,1152]{1,0:T(8,128)(2,1)S(1)} %collective-permute-done.6), channel_id=1, source_target_pairs={{0,4},{64,92},{4,8},{68,64},{8,12},{72,68},{12,16},{76,72},{16,20}... | collective-permute-start | bytes 884744 | tf_op jit(solution)/shard_map/ppermute | solution.py:25
  17.8 10.2 %collective-permute-start.4 = (bf16[256,1152]{1,0:T(8,128)(2,1)S(1)}, bf16[256,1152]{1,0:T(8,128)(2,1)S(1)}, u32[]{:S(2)}, u32[]{:S(2)}) collective-permute-start(bf16[256,1152]{1,0:T(8,128)(2,1)S(1)} %pad_maximum_fusion.1.refs_0_), channel_id=1, source_target_pairs={{0,160},{64,67},{4,164},{68,71},{8,168},{72,75},{12,172},{76,79},{... | collective-permute-start | bytes 1769480 | tf_op jit(solution)/shard_map/ppermute | solution.py:25
  20.6 11.2 %collective-permute-start.3 = (bf16[256,1152]{1,0:T(8,128)(2,1)S(1)}, bf16[256,1152]{1,0:T(8,128)(2,1)S(1)}, u32[]{:S(2)}, u32[]{:S(2)}) collective-permute-start(bf16[256,1152]{1,0:T(8,128)(2,1)S(1)} %pad_maximum_fusion.1.refs_0_), channel_id=1, source_target_pairs={{0,128},{64,65},{4,132},{68,69},{8,136},{72,73},{12,140},{76,77},{... | collective-permute-start | bytes 1769480 | tf_op jit(solution)/shard_map/ppermute | solution.py:25
  20.7 14.9 %collective-permute-start.12 = (bf16[256,1152]{1,0:T(8,128)(2,1)S(1)}, bf16[256,1152]{1,0:T(8,128)(2,1)S(1)}, u32[]{:S(2)}, u32[]{:S(2)}) collective-permute-start(bf16[256,1152]{1,0:T(8,128)(2,1)S(1)} %constant_dynamic-update-slice_fusion.2.refs_2_.refs_3_), channel_id=1, source_target_pairs={{0,64},{64,0},{4,68},{68,4},{8,72},{72,8},{12,76},{76,12},{16,80},... | collective-permute-start | bytes 1769480 | tf_op jit(solution)/shard_map/ppermute | solution.py:25
  20.8 11.1 %collective-permute-start.8 = (bf16[128,1152]{1,0:T(8,128)(2,1)S(1)}, bf16[128,1152]{1,0:T(8,128)(2,1)S(1)}, u32[]{:S(2)}, u32[]{:S(2)}) collective-permute-start(bf16[128,1152]{1,0:T(8,128)(2,1)S(1)} %collective-permute-done.7), channel_id=1, source_target_pairs={{0,4},{64,92},{4,8},{68,64},{8,12},{72,68},{12,16},{76,72},{16,20}... | collective-permute-start | bytes 884744 | tf_op jit(solution)/shard_map/ppermute | solution.py:25
  28.1 13.3 %collective-permute-start.11 = (bf16[128,1152]{1,0:T(8,128)(2,1)S(1)}, bf16[128,1152]{1,0:T(8,128)(2,1)S(1)}, u32[]{:S(2)}, u32[]{:S(2)}) collective-permute-start(bf16[128,1152]{1,0:T(8,128)(2,1)S(1)} %slice.77), channel_id=1, source_target_pairs={{0,160},{64,67},{4,164},{68,71},{8,168},{72,75},{12,172},{76,79},{... | collective-permute-start | bytes 884744 | tf_op jit(solution)/shard_map/ppermute | solution.py:25
  31.9 9.5 %collective-permute-start.10 = (bf16[128,1152]{1,0:T(8,128)(2,1)S(1)}, bf16[128,1152]{1,0:T(8,128)(2,1)S(1)}, u32[]{:S(2)}, u32[]{:S(2)}) collective-permute-start(bf16[128,1152]{1,0:T(8,128)(2,1)S(1)} %slice.76), channel_id=1, source_target_pairs={{0,128},{64,65},{4,132},{68,69},{8,136},{72,73},{12,140},{76,77},{... | collective-permute-start | bytes 884744 | tf_op jit(solution)/shard_map/ppermute | solution.py:25
  32.0 9.4 %collective-permute-start.9 = (bf16[64,1152]{1,0:T(8,128)(2,1)S(1)}, bf16[64,1152]{1,0:T(8,128)(2,1)S(1)}, u32[]{:S(2)}, u32[]{:S(2)}) collective-permute-start(bf16[64,1152]{1,0:T(8,128)(2,1)S(1)} %slice.75), channel_id=1, source_target_pairs={{0,4},{64,92},{4,8},{68,64},{8,12},{72,68},{12,16},{76,72},{16,20}... | collective-permute-start | bytes 442376 | tf_op jit(solution)/shard_map/ppermute | solution.py:25
  41.4 1.9 %collective-permute-start.13 = (bf16[192,1152]{1,0:T(8,128)(2,1)S(1)}, bf16[192,1152]{1,0:T(8,128)(2,1)S(1)}, u32[]{:S(2)}, u32[]{:S(2)}) collective-permute-start(bf16[192,1152]{1,0:T(8,128)(2,1)S(1)} %constant_dynamic-update-slice_fusion.4.refs_5_), channel_id=1, source_target_pairs={{0,64},{64,0},{4,68},{68,4},{8,72},{72,8},{12,76},{76,12},{16,80},... | collective-permute-start | bytes 1327112 | tf_op jit(solution)/shard_map/ppermute | solution.py:25
  47.4 5.5 %collective-permute-start.16 = (bf16[192,1152]{1,0:T(8,128)(2,1)S(1)}, bf16[192,1152]{1,0:T(8,128)(2,1)S(1)}, u32[]{:S(2)}, u32[]{:S(2)}) collective-permute-start(bf16[192,1152]{1,0:T(8,128)(2,1)S(1)} %get-tuple-element.72), channel_id=1, source_target_pairs={{0,64},{64,0},{4,68},{68,4},{8,72},{72,8},{12,76},{76,12},{16,80},... | collective-permute-start | bytes 1327112 | tf_op jit(solution)/shard_map/ppermute | solution.py:25
  47.6 11.9 %collective-permute-start.14 = (bf16[256,1152]{1,0:T(8,128)(2,1)S(1)}, bf16[256,1152]{1,0:T(8,128)(2,1)S(1)}, u32[]{:S(2)}, u32[]{:S(2)}) collective-permute-start(bf16[256,1152]{1,0:T(8,128)(2,1)S(1)} %get-tuple-element.69), channel_id=1, source_target_pairs={{0,160},{64,67},{4,164},{68,71},{8,168},{72,75},{12,172},{76,79},{... | collective-permute-start | bytes 1769480 | tf_op jit(solution)/shard_map/ppermute | solution.py:25
  50.8 11.1 %collective-permute-start.15 = (bf16[256,1152]{1,0:T(8,128)(2,1)S(1)}, bf16[256,1152]{1,0:T(8,128)(2,1)S(1)}, u32[]{:S(2)}, u32[]{:S(2)}) collective-permute-start(bf16[256,1152]{1,0:T(8,128)(2,1)S(1)} %get-tuple-element.70), channel_id=1, source_target_pairs={{0,128},{64,65},{4,132},{68,69},{8,136},{72,73},{12,140},{76,77},{... | collective-permute-start | bytes 1769480 | tf_op jit(solution)/shard_map/ppermute | solution.py:25
  53.0 6.3 %collective-permute-start.17 = (bf16[64,1152]{1,0:T(8,128)(2,1)S(1)}, bf16[64,1152]{1,0:T(8,128)(2,1)S(1)}, u32[]{:S(2)}, u32[]{:S(2)}) collective-permute-start(bf16[64,1152]{1,0:T(8,128)(2,1)S(1)} %get-tuple-element.91), channel_id=1, source_target_pairs={{0,28},{64,68},{4,0},{68,72},{8,4},{72,76},{12,8},{76,80},{16,12},... | collective-permute-start | bytes 442376 | tf_op jit(solution)/shard_map/ppermute | solution.py:25
  53.2 8.7 %collective-permute-start.22 = (bf16[320,1152]{1,0:T(8,128)(2,1)S(1)}, bf16[320,1152]{1,0:T(8,128)(2,1)S(1)}, u32[]{:S(2)}, u32[]{:S(2)}) collective-permute-start(bf16[320,1152]{1,0:T(8,128)(2,1)S(1)} %pad_maximum_fusion), channel_id=1, source_target_pairs={{0,64},{64,0},{4,68},{68,4},{8,72},{72,8},{12,76},{76,12},{16,80},... | collective-permute-start | bytes 2211848 | tf_op jit(solution)/shard_map/ppermute | solution.py:25
  59.4 6.8 %collective-permute-start.23 = (bf16[128,1152]{1,0:T(8,128)(2,1)S(1)}, bf16[128,1152]{1,0:T(8,128)(2,1)S(1)}, u32[]{:S(2)}, u32[]{:S(2)}) collective-permute-start(bf16[128,1152]{1,0:T(8,128)(2,1)S(1)} %pad_maximum_fusion.2), channel_id=1, source_target_pairs={{0,28},{64,68},{4,0},{68,72},{8,4},{72,76},{12,8},{76,80},{16,12},... | collective-permute-start | bytes 884744 | tf_op jit(solution)/shard_map/ppermute | solution.py:25
  61.9 11.4 %collective-permute-start.18 = (bf16[256,1152]{1,0:T(8,128)(2,1)S(1)}, bf16[256,1152]{1,0:T(8,128)(2,1)S(1)}, u32[]{:S(2)}, u32[]{:S(2)}) collective-permute-start(bf16[256,1152]{1,0:T(8,128)(2,1)S(1)} %get-tuple-element.75), channel_id=1, source_target_pairs={{0,32},{64,66},{4,36},{68,70},{8,40},{72,74},{12,44},{76,78},{16,4... | collective-permute-start | bytes 1769480 | tf_op jit(solution)/shard_map/ppermute | solution.py:25
  66.3 9.7 %collective-permute-start.24 = (bf16[128,1152]{1,0:T(8,128)(2,1)S(1)}, bf16[128,1152]{1,0:T(8,128)(2,1)S(1)}, u32[]{:S(2)}, u32[]{:S(2)}) collective-permute-start(bf16[128,1152]{1,0:T(8,128)(2,1)S(1)} %fusion.1), channel_id=1, source_target_pairs={{0,28},{64,68},{4,0},{68,72},{8,4},{72,76},{12,8},{76,80},{16,12},... | collective-permute-start | bytes 884744 | tf_op jit(solution)/shard_map/ppermute | solution.py:25
  73.6 5.2 %collective-permute-start.19 = (bf16[64,1152]{1,0:T(8,128)(2,1)S(1)}, bf16[64,1152]{1,0:T(8,128)(2,1)S(1)}, u32[]{:S(2)}, u32[]{:S(2)}) collective-permute-start(bf16[64,1152]{1,0:T(8,128)(2,1)S(1)} %get-tuple-element.88), channel_id=1, source_target_pairs={{0,3},{64,224},{4,7},{68,228},{8,11},{72,232},{12,15},{76,236},{16... | collective-permute-start | bytes 442376 | tf_op jit(solution)/shard_map/ppermute | solution.py:25
  74.3 6.7 %collective-permute-start.21 = (bf16[64,1152]{1,0:T(8,128)(2,1)S(1)}, bf16[64,1152]{1,0:T(8,128)(2,1)S(1)}, u32[]{:S(2)}, u32[]{:S(2)}) collective-permute-start(bf16[64,1152]{1,0:T(8,128)(2,1)S(1)} %get-tuple-element.89), channel_id=1, source_target_pairs={{0,2},{64,96},{4,6},{68,100},{8,10},{72,104},{12,14},{76,108},{16,... | collective-permute-start | bytes 442376 | tf_op jit(solution)/shard_map/ppermute | solution.py:25
  75.5 7.0 %collective-permute-start.20 = (bf16[64,1152]{1,0:T(8,128)(2,1)S(1)}, bf16[64,1152]{1,0:T(8,128)(2,1)S(1)}, u32[]{:S(2)}, u32[]{:S(2)}) collective-permute-start(bf16[64,1152]{1,0:T(8,128)(2,1)S(1)} %get-tuple-element.90), channel_id=1, source_target_pairs={{0,1},{64,192},{4,5},{68,196},{8,9},{72,200},{12,13},{76,204},{16,... | collective-permute-start | bytes 442376 | tf_op jit(solution)/shard_map/ppermute | solution.py:25
  76.0 9.0 %collective-permute-start.25 = (bf16[128,1152]{1,0:T(8,128)(2,1)S(1)}, bf16[128,1152]{1,0:T(8,128)(2,1)S(1)}, u32[]{:S(2)}, u32[]{:S(2)}) collective-permute-start(bf16[128,1152]{1,0:T(8,128)(2,1)S(1)} %fusion.3), channel_id=1, source_target_pairs={{0,28},{64,68},{4,0},{68,72},{8,4},{72,76},{12,8},{76,80},{16,12},... | collective-permute-start | bytes 884744 | tf_op jit(solution)/shard_map/ppermute | solution.py:25
  82.7 3.9 %copy-start.1 = (bf16[1152,1152]{1,0:T(8,128)(2,1)S(1)}, bf16[1152,1152]{1,0:T(8,128)(2,1)}, u32[]{:S(2)}) copy-start(bf16[1152,1152]{1,0:T(8,128)(2,1)} %param.11) | copy-start | bytes 7962628
  85.0 1.5 %collective-permute-start.26 = (bf16[64,1152]{1,0:T(8,128)(2,1)S(1)}, bf16[64,1152]{1,0:T(8,128)(2,1)S(1)}, u32[]{:S(2)}, u32[]{:S(2)}) collective-permute-start(bf16[64,1152]{1,0:T(8,128)(2,1)S(1)} %slice.89), channel_id=1, source_target_pairs={{0,64},{64,0},{4,68},{68,4},{8,72},{72,8},{12,76},{76,12},{16,80},... | collective-permute-start | bytes 442376 | tf_op jit(solution)/shard_map/ppermute | solution.py:25

commit v5 on v4

--- a/solution.py
+++ b/solution.py
@@ -109,12 +109,21 @@
     slope = scal[:, :1] * -LOG2E
     offset = scal[:, 1:2] * -LOG2E
     width = 256
-    for at in range(0, txt.shape[0], width):
-        cols = pl.ds(at, min(width, txt.shape[0] - at))
-        cosine = lax.dot_general(
-            img[...], txt[cols, :], (((1,), (1,)), ((), ())), preferred_element_type=F32
+    starts = list(range(0, txt.shape[0], width))
+
+    def chunk(at):
+        return pl.ds(at, min(width, txt.shape[0] - at))
+
+    def cosines(at):
+        return lax.dot_general(
+            img[...], txt[chunk(at), :], (((1,), (1,)), ((), ())), preferred_element_type=F32
         )
-        power = cosine * slope + offset
+
+    following = cosines(0)
+    for at in starts:
+        power = following * slope + offset
+        if at + width < txt.shape[0]:
+            following = cosines(at + width)
         if has_diag and at == 0:
             row = lax.broadcasted_iota(jnp.int32, power.shape, 0)
             col = lax.broadcasted_iota(jnp.int32, power.shape, 1)
@@ -123,7 +132,7 @@
             value = jnp.where(same, -value, value)
         else:
             value = 1.0 / (1.0 + jnp.exp2(power))
-        grad[:, cols] = value.astype(BF)
+        grad[:, chunk(at)] = value.astype(BF)
     for n, (ref, place) in enumerate(spans(img_out)):
         value = jnp.dot(grad[place, :], txt[...], preferred_element_type=F32)
         if img_old and len(img_out) == 1:

time: 89 us -> 89 us (level)
  no operation moved by 1% of the time
where the time goes in v5:
time: 89 us; the launch traced here: 88.3 us
  waiting for transfers between devices  36.3 us (41%)
  starting transfers between devices  28.8 us (32%)
  Pallas kernels  11.9 us (13%)
  matrix products  6.15 us (7%)
  other arithmetic  2.62 us (3%)
  between operations  2.32 us (3%)
    ppermute x27, waiting for transfers between devices, send(): lax.ppermute(value, AXES, [(flat(*p), flat(*target(*p))) for p in PLACES])  36.3 us
    ppermute x27, starting transfers between devices, send(): lax.ppermute(value, AXES, [(flat(*p), flat(*target(*p))) for p in PLACES])  28.8 us
    pallas_call x4, Pallas kernels, pair_block(): pl.pallas_call(functools.partial(pair_kernel, counts, has_diag), out_shap...  11.9 us
    dot_general x1, matrix products, text_forward(): project = jnp.dot(features, weight, preferred_element_type=F32)  2.69 us
  transfers between devices with their start and end apart: 27, of which 14 were waited for; matrix products, arithmetic and copies ran while one was open for 5% of the time, Pallas kernels for 9%

profile of v5, /device:TPU:32, one launch (start us, length us, event | category | flops | bytes accessed | tf_op | source)
XLA Modules:
  0.0 88.3 jit_solution(5467058117182764437)
XLA Ops:
  0.6 0.0 copy-start
  0.7 2.7 %multiply_reduce_fusion.3 = (f32[64]{0:T(128)S(1)}, f32[64,1152]{1,0:T(8,128)S(1)}) fusion(bf16[64,1152]{1,0:T(8,128)(2,1)} %param.8, bf16[1152,1152]{1,0:T(8,128)(2,1)} %param.11), kind=kOutput, calls=%fused_computation.41 | convolution fusion | flops 170016704 | bytes 3096832 | tf_op jit(solution)/shard_map/dot_general | solution.py:67
  3.4 0.1 fusion.32
  3.5 0.1 collective-permute-start.5
  3.6 0.1 convert_reduce_fusion
  3.7 0.2 fusion.14
  4.0 0.7 multiply_reduce_fusion.2
  4.7 0.2 collective-permute-done.5
  5.0 2.0 %collective-permute-start.6 = (bf16[128,1152]{1,0:T(8,128)(2,1)S(1)}, bf16[128,1152]{1,0:T(8,128)(2,1)S(1)}, u32[]{:S(2)}, u32[]{:S(2)}) collective-permute-start(bf16[128,1152]{1,0:T(8,128)(2,1)S(1)} %constant_dynamic-update-slice_fusion.refs_1_.refs_2_), channel_id=1, source_target_pairs={{0,4},{64,92},{4,8},{68,64},{8,12},{72,68},{12,16},{76,72},{16,20}... | collective-permute-start | bytes 884744 | tf_op jit(solution)/shard_map/ppermute | solution.py:25
  7.0 0.1 fusion.33
  7.1 3.3 %collective-permute-start.2 = (bf16[64,1152]{1,0:T(8,128)(2,1)S(1)}, bf16[64,1152]{1,0:T(8,128)(2,1)S(1)}, u32[]{:S(2)}, u32[]{:S(2)}) collective-permute-start(bf16[64,1152]{1,0:T(8,128)(2,1)S(1)} %fusion.33), channel_id=1, source_target_pairs={{0,2},{64,96},{4,6},{68,100},{8,10},{72,104},{12,14},{76,108},{16,... | collective-permute-start | bytes 442376 | tf_op jit(solution)/shard_map/ppermute | solution.py:25
  10.3 1.1 %collective-permute-start.1 = (bf16[64,1152]{1,0:T(8,128)(2,1)S(1)}, bf16[64,1152]{1,0:T(8,128)(2,1)S(1)}, u32[]{:S(2)}, u32[]{:S(2)}) collective-permute-start(bf16[64,1152]{1,0:T(8,128)(2,1)S(1)} %fusion.33), channel_id=1, source_target_pairs={{0,3},{64,224},{4,7},{68,228},{8,11},{72,232},{12,15},{76,236},{16... | collective-permute-start | bytes 442376 | tf_op jit(solution)/shard_map/ppermute | solution.py:25
  11.4 1.0 %collective-permute-start = (bf16[64,1152]{1,0:T(8,128)(2,1)S(1)}, bf16[64,1152]{1,0:T(8,128)(2,1)S(1)}, u32[]{:S(2)}, u32[]{:S(2)}) collective-permute-start(bf16[64,1152]{1,0:T(8,128)(2,1)S(1)} %fusion.33), channel_id=1, source_target_pairs={{0,1},{64,192},{4,5},{68,196},{8,9},{72,200},{12,13},{76,204},{16,... | collective-permute-start | bytes 442376 | tf_op jit(solution)/shard_map/ppermute | solution.py:25
  12.4 1.9 %collective-permute-start.7 = (bf16[128,1152]{1,0:T(8,128)(2,1)S(1)}, bf16[128,1152]{1,0:T(8,128)(2,1)S(1)}, u32[]{:S(2)}, u32[]{:S(2)}) collective-permute-start(bf16[128,1152]{1,0:T(8,128)(2,1)S(1)} %collective-permute-done.6), channel_id=1, source_target_pairs={{0,4},{64,92},{4,8},{68,64},{8,12},{72,68},{12,16},{76,72},{16,20}... | collective-permute-start | bytes 884744 | tf_op jit(solution)/shard_map/ppermute | solution.py:25
  14.3 0.0 collective-permute-done.2
  14.3 1.4 %collective-permute-done.1 = bf16[64,1152]{1,0:T(8,128)(2,1)S(1)} collective-permute-done((bf16[64,1152]{1,0:T(8,128)(2,1)S(1)}, bf16[64,1152]{1,0:T(8,128)(2,1)S(1)}, u32[]{:S(2)}, u32[]{:S(2)}) %collective-permute-start.1) | collective-permute-done | bytes 147488 | tf_op jit(solution)/shard_map/ppermute | solution.py:25
  15.7 2.0 %collective-permute-done = bf16[64,1152]{1,0:T(8,128)(2,1)S(1)} collective-permute-done((bf16[64,1152]{1,0:T(8,128)(2,1)S(1)}, bf16[64,1152]{1,0:T(8,128)(2,1)S(1)}, u32[]{:S(2)}, u32[]{:S(2)}) %collective-permute-start) | collective-permute-done | bytes 147488 | tf_op jit(solution)/shard_map/ppermute | solution.py:25
  17.8 2.8 %collective-permute-start.4 = (bf16[256,1152]{1,0:T(8,128)(2,1)S(1)}, bf16[256,1152]{1,0:T(8,128)(2,1)S(1)}, u32[]{:S(2)}, u32[]{:S(2)}) collective-permute-start(bf16[256,1152]{1,0:T(8,128)(2,1)S(1)} %pad_maximum_fusion.1.refs_0_), channel_id=1, source_target_pairs={{0,160},{64,67},{4,164},{68,71},{8,168},{72,75},{12,172},{76,79},{... | collective-permute-start | bytes 1769480 | tf_op jit(solution)/shard_map/ppermute | solution.py:25
  20.6 0.0 collective-permute-start.3
  20.7 0.1 collective-permute-start.12
  20.8 2.0 %collective-permute-start.8 = (bf16[128,1152]{1,0:T(8,128)(2,1)S(1)}, bf16[128,1152]{1,0:T(8,128)(2,1)S(1)}, u32[]{:S(2)}, u32[]{:S(2)}) collective-permute-start(bf16[128,1152]{1,0:T(8,128)(2,1)S(1)} %collective-permute-done.7), channel_id=1, source_target_pairs={{0,4},{64,92},{4,8},{68,64},{8,12},{72,68},{12,16},{76,72},{16,20}... | collective-permute-start | bytes 884744 | tf_op jit(solution)/shard_map/ppermute | solution.py:25
  22.8 5.2 %collective-permute-done.4.refs_1_.refs_2_ = bf16[256,1152]{1,0:T(8,128)(2,1)S(1)} collective-permute-done((bf16[256,1152]{1,0:T(8,128)(2,1)S(1)}, bf16[256,1152]{1,0:T(8,128)(2,1)S(1)}, u32[]{:S(2)}, u32[]{:S(2)}) %collective-permute-start.4) | collective-permute-done | bytes 589856 | tf_op jit(solution)/shard_map/ppermute | solution.py:25
  28.1 3.8 %collective-permute-start.11 = (bf16[128,1152]{1,0:T(8,128)(2,1)S(1)}, bf16[128,1152]{1,0:T(8,128)(2,1)S(1)}, u32[]{:S(2)}, u32[]{:S(2)}) collective-permute-start(bf16[128,1152]{1,0:T(8,128)(2,1)S(1)} %slice.77), channel_id=1, source_target_pairs={{0,160},{64,67},{4,164},{68,71},{8,168},{72,75},{12,172},{76,79},{... | collective-permute-start | bytes 884744 | tf_op jit(solution)/shard_map/ppermute | solution.py:25
  31.9 0.1 collective-permute-start.10
  32.0 2.2 %collective-permute-start.9 = (bf16[64,1152]{1,0:T(8,128)(2,1)S(1)}, bf16[64,1152]{1,0:T(8,128)(2,1)S(1)}, u32[]{:S(2)}, u32[]{:S(2)}) collective-permute-start(bf16[64,1152]{1,0:T(8,128)(2,1)S(1)} %slice.75), channel_id=1, source_target_pairs={{0,4},{64,92},{4,8},{68,64},{8,12},{72,68},{12,16},{76,72},{16,20}... | collective-permute-start | bytes 442376 | tf_op jit(solution)/shard_map/ppermute | solution.py:25
  35.5 0.1 maximum_bitcast_fusion.scal
  35.6 2.0 %shard_map.86 = (f32[256,1152]{1,0:T(8,128)S(1)}, f32[64,1152]{1,0:T(8,128)S(1)}, f32[64,1152]{1,0:T(8,128)S(1)}, f32[256,1152]{1,0:T(8,128)S(1)}, f32[256,1152]{1,0:T(8,128)S(1)}) custom-call(f32[1,2]{1,0:T(1,128)S(1)} %maximum_bitcast_fusion.scal, bf16[256,1152]{1,0:T(8,128)(2,1)S(1)} %pad_maximum_fusion.1.refs_0_, ...), custom_call_target="tpu_custom_call" | custom-call | flops 1024 | bytes 1024 | tf_op jit(solution)/shard_map/pallas_call | solution.py:159
  37.5 3.8 %shard_map.87 = (f32[256,1152]{1,0:T(8,128)S(1)}, f32[256,1152]{1,0:T(8,128)S(1)}, f32[64,1152]{1,0:T(8,128)S(1)}, f32[64,1152]{1,0:T(8,128)S(1)}, f32[256,1152]{1,0:T(8,128)S(1)}, /*index=5*/f32[256,1152]{1,0:T(8,128)S(1)}) custom-call(f32[1,2]{1,0:T(1,128)S(1)} %maximum_bitcast_fusion.scal, bf16[256,1152]{1,0:T(8,128)(2,1)S(1)} %collective-permute-done.3.refs_0_.refs_1_, ...), custom_call_target="tpu_custom_call" | custom-call | flops 1024 | bytes 1024 | tf_op jit(solution)/shard_map/pallas_call | solution.py:159
  41.4 0.1 collective-permute-start.13
  41.5 1.8 %collective-permute-done.13.refs_6_ = bf16[192,1152]{1,0:T(8,128)(2,1)S(1)} collective-permute-done((bf16[192,1152]{1,0:T(8,128)(2,1)S(1)}, bf16[192,1152]{1,0:T(8,128)(2,1)S(1)}, u32[]{:S(2)}, u32[]{:S(2)}) %collective-permute-start.13) | collective-permute-done | bytes 442400 | tf_op jit(solution)/shard_map/ppermute | solution.py:25
  43.3 4.1 %shard_map.88 = (f32[256,1152]{1,0:T(8,128)S(1)}, bf16[256,1152]{1,0:T(8,128)(2,1)S(1)}, bf16[256,1152]{1,0:T(8,128)(2,1)S(1)}, f32[128,1152]{1,0:T(8,128)S(1)},...) custom-call(f32[1,2]{1,0:T(1,128)S(1)} %maximum_bitcast_fusion.scal, ...), custom_call_target="tpu_custom_call" | custom-call | flops 1024 | bytes 1024 | tf_op jit(solution)/shard_map/pallas_call | solution.py:159
  47.4 0.2 collective-permute-start.16
  47.6 3.2 %collective-permute-start.14 = (bf16[256,1152]{1,0:T(8,128)(2,1)S(1)}, bf16[256,1152]{1,0:T(8,128)(2,1)S(1)}, u32[]{:S(2)}, u32[]{:S(2)}) collective-permute-start(bf16[256,1152]{1,0:T(8,128)(2,1)S(1)} %get-tuple-element.69), channel_id=1, source_target_pairs={{0,160},{64,67},{4,164},{68,71},{8,168},{72,75},{12,172},{76,79},{... | collective-permute-start | bytes 1769480 | tf_op jit(solution)/shard_map/ppermute | solution.py:25
  50.8 0.0 collective-permute-start.15
  50.8 2.0 %shard_map.89 = (bf16[256,1152]{1,0:T(8,128)(2,1)S(1)}, f32[64,1152]{1,0:T(8,128)S(1)}, bf16[64,1152]{1,0:T(8,128)(2,1)S(1)}, f32[256,1152]{1,0:T(8,128)S(1)}, bf16[256,1152]{1,0:T(8,128)(2,1)S(1)}) custom-call(f32[1,2]{1,0:T(1,128)S(1)} %maximum_bitcast_fusion.scal, bf16[128,1152]{1,0:T(8,128)(2,1)S(1)} %collective-permute-done.10.refs_3_.refs_0_, ...), custom_call_target="tpu_custom_call" | custom-call | flops 1024 | bytes 1024 | tf_op jit(solution)/shard_map/pallas_call | solution.py:159
  52.9 0.1 fusion.36
  53.0 0.2 collective-permute-start.17
  53.2 0.1 pad_maximum_fusion
  53.3 1.5 %collective-permute-start.22 = (bf16[320,1152]{1,0:T(8,128)(2,1)S(1)}, bf16[320,1152]{1,0:T(8,128)(2,1)S(1)}, u32[]{:S(2)}, u32[]{:S(2)}) collective-permute-start(bf16[320,1152]{1,0:T(8,128)(2,1)S(1)} %pad_maximum_fusion), channel_id=1, source_target_pairs={{0,64},{64,0},{4,68},{68,4},{8,72},{72,8},{12,76},{76,12},{16,80},... | collective-permute-start | bytes 2211848 | tf_op jit(solution)/shard_map/ppermute | solution.py:25
  54.7 4.6 %collective-permute-done.17 = bf16[64,1152]{1,0:T(8,128)(2,1)S(1)} collective-permute-done((bf16[64,1152]{1,0:T(8,128)(2,1)S(1)}, bf16[64,1152]{1,0:T(8,128)(2,1)S(1)}, u32[]{:S(2)}, u32[]{:S(2)}) %collective-permute-start.17) | collective-permute-done | bytes 147488 | tf_op jit(solution)/shard_map/ppermute | solution.py:25
  59.4 0.1 collective-permute-start.23
  59.5 2.4 %collective-permute-done.15 = bf16[256,1152]{1,0:T(8,128)(2,1)S(1)} collective-permute-done((bf16[256,1152]{1,0:T(8,128)(2,1)S(1)}, bf16[256,1152]{1,0:T(8,128)(2,1)S(1)}, u32[]{:S(2)}, u32[]{:S(2)}) %collective-permute-start.15) | collective-permute-done | bytes 589856 | tf_op jit(solution)/shard_map/ppermute | solution.py:25
  61.9 0.1 convert_element_type.88
  62.0 4.2 %collective-permute-done.23 = bf16[128,1152]{1,0:T(8,128)(2,1)S(1)} collective-permute-done((bf16[128,1152]{1,0:T(8,128)(2,1)S(1)}, bf16[128,1152]{1,0:T(8,128)(2,1)S(1)}, u32[]{:S(2)}, u32[]{:S(2)}) %collective-permute-start.23) | collective-permute-done | bytes 294944 | tf_op jit(solution)/shard_map/ppermute | solution.py:25
  66.2 0.1 fusion.1
  66.3 0.1 collective-permute-start.24
  66.4 6.9 %collective-permute-done.18 = bf16[256,1152]{1,0:T(8,128)(2,1)S(1)} collective-permute-done((bf16[256,1152]{1,0:T(8,128)(2,1)S(1)}, bf16[256,1152]{1,0:T(8,128)(2,1)S(1)}, u32[]{:S(2)}, u32[]{:S(2)}) %collective-permute-start.18) | collective-permute-done | bytes 589856 | tf_op jit(solution)/shard_map/ppermute | solution.py:25
  73.3 0.3 fusion.37
  73.6 0.7 collective-permute-start.19
  74.3 1.2 %collective-permute-start.21 = (bf16[64,1152]{1,0:T(8,128)(2,1)S(1)}, bf16[64,1152]{1,0:T(8,128)(2,1)S(1)}, u32[]{:S(2)}, u32[]{:S(2)}) collective-permute-start(bf16[64,1152]{1,0:T(8,128)(2,1)S(1)} %get-tuple-element.89), channel_id=1, source_target_pairs={{0,2},{64,96},{4,6},{68,100},{8,10},{72,104},{12,14},{76,108},{16,... | collective-permute-start | bytes 442376 | tf_op jit(solution)/shard_map/ppermute | solution.py:25
  75.5 0.4 collective-permute-start.20
  75.9 0.1 fusion.3
  76.0 0.8 collective-permute-start.25
  76.8 2.0 %collective-permute-done.19 = bf16[64,1152]{1,0:T(8,128)(2,1)S(1)} collective-permute-done((bf16[64,1152]{1,0:T(8,128)(2,1)S(1)}, bf16[64,1152]{1,0:T(8,128)(2,1)S(1)}, u32[]{:S(2)}, u32[]{:S(2)}) %collective-permute-start.19) | collective-permute-done | bytes 147488 | tf_op jit(solution)/shard_map/ppermute | solution.py:25
  78.8 2.2 %collective-permute-done.21 = bf16[64,1152]{1,0:T(8,128)(2,1)S(1)} collective-permute-done((bf16[64,1152]{1,0:T(8,128)(2,1)S(1)}, bf16[64,1152]{1,0:T(8,128)(2,1)S(1)}, u32[]{:S(2)}, u32[]{:S(2)}) %collective-permute-start.21) | collective-permute-done | bytes 147488 | tf_op jit(solution)/shard_map/ppermute | solution.py:25
  81.1 1.5 %collective-permute-done.20 = bf16[64,1152]{1,0:T(8,128)(2,1)S(1)} collective-permute-done((bf16[64,1152]{1,0:T(8,128)(2,1)S(1)}, bf16[64,1152]{1,0:T(8,128)(2,1)S(1)}, u32[]{:S(2)}, u32[]{:S(2)}) %collective-permute-start.20) | collective-permute-done | bytes 147488 | tf_op jit(solution)/shard_map/ppermute | solution.py:25
  82.6 0.2 multiply_reduce_fusion.1
  82.8 1.1 %fusion.34 = (f32[64]{0:T(128)S(1)}, f32[64]{0:T(128)S(1)}, f32[64,1152]{1,0:T(8,128)S(1)}) fusion(f32[64]{0:T(128)S(1)} %add_rsqrt_fusion, f32[64]{0:T(128)S(1)} %broadcast_multiply_fusion.2, bf16[64,1152]{1,0:T(8,128)(2,1)S(1)} %copy-done.2, f32[1152]{0:T(1024)S(1)} %copy-done.3, bf16[1152,1152]{1,0:T(8,128)(2,1)S(1)} %copy-done, ...), kind=kOutput, calls=%fused_computation.67 | convolution fusion | flops 171270016 | bytes 4139524 | tf_op jit(solution)/shard_map/dot_general | solution.py:77
  83.9 1.1 %collective-permute-done.25 = bf16[128,1152]{1,0:T(8,128)(2,1)S(1)} collective-permute-done((bf16[128,1152]{1,0:T(8,128)(2,1)S(1)}, bf16[128,1152]{1,0:T(8,128)(2,1)S(1)}, u32[]{:S(2)}, u32[]{:S(2)}) %collective-permute-start.25) | collective-permute-done | bytes 294944 | tf_op jit(solution)/shard_map/ppermute | solution.py:25
  85.0 0.1 collective-permute-start.26
  85.1 0.8 fusion.13
  86.0 0.5 collective-permute-done.26
  86.5 0.2 multiply_reduce_fusion
  86.7 1.6 %convolution_convert_fusion = bf16[64,1152]{1,0:T(8,128)(2,1)} fusion(bf16[1152,1152]{1,0:T(8,128)(2,1)S(1)} %copy-done.1, f32[64,1152]{1,0:T(8,128)S(1)} %get-tuple-element.83, f32[64]{0:T(128)S(1)} %get-tuple-element.82, f32[64]{0:T(128)S(1)} %add_sqrt_fusion.1, f32[64,1152]{1,0:T(8,128)S(1)} %get-tuple-element.94), kind=kOutput, calls=%fused_computation.1 | convolution fusion | flops 170311680 | bytes 3392000 | tf_op jit(solution)/shard_map/dot_general | solution.py:89
  (40 shorter events, 0.4 us)
Async XLA Ops:
  0.6 3.3 %copy-start = (bf16[1152,1152]{1,0:T(8,128)(2,1)S(1)}, bf16[1152,1152]{1,0:T(8,128)(2,1)}, u32[]{:S(2)}) copy-start(bf16[1152,1152]{1,0:T(8,128)(2,1)} %param.10) | copy-start | bytes 7962628
  0.6 3.0 %copy-start.2 = (bf16[64,1152]{1,0:T(8,128)(2,1)S(1)}, bf16[64,1152]{1,0:T(8,128)(2,1)}, u32[]{:S(2)}) copy-start(bf16[64,1152]{1,0:T(8,128)(2,1)} %param.7) | copy-start | bytes 442372
  0.7 3.3 %copy-start.3 = (f32[1152]{0:T(1024)S(1)}, f32[1152]{0:T(1024)}, u32[]{:S(2)}) copy-start(f32[1152]{0:T(1024)} %param.9) | copy-start | bytes 13828
  3.5 1.5 %collective-permute-start.5 = (bf16[64,1152]{1,0:T(8,128)(2,1)S(1)}, bf16[64,1152]{1,0:T(8,128)(2,1)S(1)}, u32[]{:S(2)}, u32[]{:S(2)}) collective-permute-start(bf16[64,1152]{1,0:T(8,128)(2,1)S(1)} %fusion.32), channel_id=1, source_target_pairs={{0,64},{64,0},{4,68},{68,4},{8,72},{72,8},{12,76},{76,12},{16,80},... | collective-permute-start | bytes 442376 | tf_op jit(solution)/shard_map/ppermute | solution.py:25
  5.0 7.4 %collective-permute-start.6 = (bf16[128,1152]{1,0:T(8,128)(2,1)S(1)}, bf16[128,1152]{1,0:T(8,128)(2,1)S(1)}, u32[]{:S(2)}, u32[]{:S(2)}) collective-permute-start(bf16[128,1152]{1,0:T(8,128)(2,1)S(1)} %constant_dynamic-update-slice_fusion.refs_1_.refs_2_), channel_id=1, source_target_pairs={{0,4},{64,92},{4,8},{68,64},{8,12},{72,68},{12,16},{76,72},{16,20}... | collective-permute-start | bytes 884744 | tf_op jit(solution)/shard_map/ppermute | solution.py:25
  7.1 7.2 %collective-permute-start.2 = (bf16[64,1152]{1,0:T(8,128)(2,1)S(1)}, bf16[64,1152]{1,0:T(8,128)(2,1)S(1)}, u32[]{:S(2)}, u32[]{:S(2)}) collective-permute-start(bf16[64,1152]{1,0:T(8,128)(2,1)S(1)} %fusion.33), channel_id=1, source_target_pairs={{0,2},{64,96},{4,6},{68,100},{8,10},{72,104},{12,14},{76,108},{16,... | collective-permute-start | bytes 442376 | tf_op jit(solution)/shard_map/ppermute | solution.py:25
  10.3 5.4 %collective-permute-start.1 = (bf16[64,1152]{1,0:T(8,128)(2,1)S(1)}, bf16[64,1152]{1,0:T(8,128)(2,1)S(1)}, u32[]{:S(2)}, u32[]{:S(2)}) collective-permute-start(bf16[64,1152]{1,0:T(8,128)(2,1)S(1)} %fusion.33), channel_id=1, source_target_pairs={{0,3},{64,224},{4,7},{68,228},{8,11},{72,232},{12,15},{76,236},{16... | collective-permute-start | bytes 442376 | tf_op jit(solution)/shard_map/ppermute | solution.py:25
  11.4 6.4 %collective-permute-start = (bf16[64,1152]{1,0:T(8,128)(2,1)S(1)}, bf16[64,1152]{1,0:T(8,128)(2,1)S(1)}, u32[]{:S(2)}, u32[]{:S(2)}) collective-permute-start(bf16[64,1152]{1,0:T(8,128)(2,1)S(1)} %fusion.33), channel_id=1, source_target_pairs={{0,1},{64,192},{4,5},{68,196},{8,9},{72,200},{12,13},{76,204},{16,... | collective-permute-start | bytes 442376 | tf_op jit(solution)/shard_map/ppermute | solution.py:25
  12.4 8.3 %collective-permute-start.7 = (bf16[128,1152]{1,0:T(8,128)(2,1)S(1)}, bf16[128,1152]{1,0:T(8,128)(2,1)S(1)}, u32[]{:S(2)}, u32[]{:S(2)}) collective-permute-start(bf16[128,1152]{1,0:T(8,128)(2,1)S(1)} %collective-permute-done.6), channel_id=1, source_target_pairs={{0,4},{64,92},{4,8},{68,64},{8,12},{72,68},{12,16},{76,72},{16,20}... | collective-permute-start | bytes 884744 | tf_op jit(solution)/shard_map/ppermute | solution.py:25
  17.8 10.2 %collective-permute-start.4 = (bf16[256,1152]{1,0:T(8,128)(2,1)S(1)}, bf16[256,1152]{1,0:T(8,128)(2,1)S(1)}, u32[]{:S(2)}, u32[]{:S(2)}) collective-permute-start(bf16[256,1152]{1,0:T(8,128)(2,1)S(1)} %pad_maximum_fusion.1.refs_0_), channel_id=1, source_target_pairs={{0,160},{64,67},{4,164},{68,71},{8,168},{72,75},{12,172},{76,79},{... | collective-permute-start | bytes 1769480 | tf_op jit(solution)/shard_map/ppermute | solution.py:25
  20.6 11.2 %collective-permute-start.3 = (bf16[256,1152]{1,0:T(8,128)(2,1)S(1)}, bf16[256,1152]{1,0:T(8,128)(2,1)S(1)}, u32[]{:S(2)}, u32[]{:S(2)}) collective-permute-start(bf16[256,1152]{1,0:T(8,128)(2,1)S(1)} %pad_maximum_fusion.1.refs_0_), channel_id=1, source_target_pairs={{0,128},{64,65},{4,132},{68,69},{8,136},{72,73},{12,140},{76,77},{... | collective-permute-start | bytes 1769480 | tf_op jit(solution)/shard_map/ppermute | solution.py:25
  20.7 14.9 %collective-permute-start.12 = (bf16[256,1152]{1,0:T(8,128)(2,1)S(1)}, bf16[256,1152]{1,0:T(8,128)(2,1)S(1)}, u32[]{:S(2)}, u32[]{:S(2)}) collective-permute-start(bf16[256,1152]{1,0:T(8,128)(2,1)S(1)} %constant_dynamic-update-slice_fusion.2.refs_2_.refs_3_), channel_id=1, source_target_pairs={{0,64},{64,0},{4,68},{68,4},{8,72},{72,8},{12,76},{76,12},{16,80},... | collective-permute-start | bytes 1769480 | tf_op jit(solution)/shard_map/ppermute | solution.py:25
  20.8 11.1 %collective-permute-start.8 = (bf16[128,1152]{1,0:T(8,128)(2,1)S(1)}, bf16[128,1152]{1,0:T(8,128)(2,1)S(1)}, u32[]{:S(2)}, u32[]{:S(2)}) collective-permute-start(bf16[128,1152]{1,0:T(8,128)(2,1)S(1)} %collective-permute-done.7), channel_id=1, source_target_pairs={{0,4},{64,92},{4,8},{68,64},{8,12},{72,68},{12,16},{76,72},{16,20}... | collective-permute-start | bytes 884744 | tf_op jit(solution)/shard_map/ppermute | solution.py:25
  28.1 13.3 %collective-permute-start.11 = (bf16[128,1152]{1,0:T(8,128)(2,1)S(1)}, bf16[128,1152]{1,0:T(8,128)(2,1)S(1)}, u32[]{:S(2)}, u32[]{:S(2)}) collective-permute-start(bf16[128,1152]{1,0:T(8,128)(2,1)S(1)} %slice.77), channel_id=1, source_target_pairs={{0,160},{64,67},{4,164},{68,71},{8,168},{72,75},{12,172},{76,79},{... | collective-permute-start | bytes 884744 | tf_op jit(solution)/shard_map/ppermute | solution.py:25
  31.9 9.5 %collective-permute-start.10 = (bf16[128,1152]{1,0:T(8,128)(2,1)S(1)}, bf16[128,1152]{1,0:T(8,128)(2,1)S(1)}, u32[]{:S(2)}, u32[]{:S(2)}) collective-permute-start(bf16[128,1152]{1,0:T(8,128)(2,1)S(1)} %slice.76), channel_id=1, source_target_pairs={{0,128},{64,65},{4,132},{68,69},{8,136},{72,73},{12,140},{76,77},{... | collective-permute-start | bytes 884744 | tf_op jit(solution)/shard_map/ppermute | solution.py:25
  32.0 9.4 %collective-permute-start.9 = (bf16[64,1152]{1,0:T(8,128)(2,1)S(1)}, bf16[64,1152]{1,0:T(8,128)(2,1)S(1)}, u32[]{:S(2)}, u32[]{:S(2)}) collective-permute-start(bf16[64,1152]{1,0:T(8,128)(2,1)S(1)} %slice.75), channel_id=1, source_target_pairs={{0,4},{64,92},{4,8},{68,64},{8,12},{72,68},{12,16},{76,72},{16,20}... | collective-permute-start | bytes 442376 | tf_op jit(solution)/shard_map/ppermute | solution.py:25
  41.4 1.9 %collective-permute-start.13 = (bf16[192,1152]{1,0:T(8,128)(2,1)S(1)}, bf16[192,1152]{1,0:T(8,128)(2,1)S(1)}, u32[]{:S(2)}, u32[]{:S(2)}) collective-permute-start(bf16[192,1152]{1,0:T(8,128)(2,1)S(1)} %constant_dynamic-update-slice_fusion.4.refs_5_), channel_id=1, source_target_pairs={{0,64},{64,0},{4,68},{68,4},{8,72},{72,8},{12,76},{76,12},{16,80},... | collective-permute-start | bytes 1327112 | tf_op jit(solution)/shard_map/ppermute | solution.py:25
  47.4 5.5 %collective-permute-start.16 = (bf16[192,1152]{1,0:T(8,128)(2,1)S(1)}, bf16[192,1152]{1,0:T(8,128)(2,1)S(1)}, u32[]{:S(2)}, u32[]{:S(2)}) collective-permute-start(bf16[192,1152]{1,0:T(8,128)(2,1)S(1)} %get-tuple-element.72), channel_id=1, source_target_pairs={{0,64},{64,0},{4,68},{68,4},{8,72},{72,8},{12,76},{76,12},{16,80},... | collective-permute-start | bytes 1327112 | tf_op jit(solution)/shard_map/ppermute | solution.py:25
  47.6 11.9 %collective-permute-start.14 = (bf16[256,1152]{1,0:T(8,128)(2,1)S(1)}, bf16[256,1152]{1,0:T(8,128)(2,1)S(1)}, u32[]{:S(2)}, u32[]{:S(2)}) collective-permute-start(bf16[256,1152]{1,0:T(8,128)(2,1)S(1)} %get-tuple-element.69), channel_id=1, source_target_pairs={{0,160},{64,67},{4,164},{68,71},{8,168},{72,75},{12,172},{76,79},{... | collective-permute-start | bytes 1769480 | tf_op jit(solution)/shard_map/ppermute | solution.py:25
  50.8 11.1 %collective-permute-start.15 = (bf16[256,1152]{1,0:T(8,128)(2,1)S(1)}, bf16[256,1152]{1,0:T(8,128)(2,1)S(1)}, u32[]{:S(2)}, u32[]{:S(2)}) collective-permute-start(bf16[256,1152]{1,0:T(8,128)(2,1)S(1)} %get-tuple-element.70), channel_id=1, source_target_pairs={{0,128},{64,65},{4,132},{68,69},{8,136},{72,73},{12,140},{76,77},{... | collective-permute-start | bytes 1769480 | tf_op jit(solution)/shard_map/ppermute | solution.py:25
  53.0 6.3 %collective-permute-start.17 = (bf16[64,1152]{1,0:T(8,128)(2,1)S(1)}, bf16[64,1152]{1,0:T(8,128)(2,1)S(1)}, u32[]{:S(2)}, u32[]{:S(2)}) collective-permute-start(bf16[64,1152]{1,0:T(8,128)(2,1)S(1)} %get-tuple-element.91), channel_id=1, source_target_pairs={{0,28},{64,68},{4,0},{68,72},{8,4},{72,76},{12,8},{76,80},{16,12},... | collective-permute-start | bytes 442376 | tf_op jit(solution)/shard_map/ppermute | solution.py:25
  53.3 8.7 %collective-permute-start.22 = (bf16[320,1152]{1,0:T(8,128)(2,1)S(1)}, bf16[320,1152]{1,0:T(8,128)(2,1)S(1)}, u32[]{:S(2)}, u32[]{:S(2)}) collective-permute-start(bf16[320,1152]{1,0:T(8,128)(2,1)S(1)} %pad_maximum_fusion), channel_id=1, source_target_pairs={{0,64},{64,0},{4,68},{68,4},{8,72},{72,8},{12,76},{76,12},{16,80},... | collective-permute-start | bytes 2211848 | tf_op jit(solution)/shard_map/ppermute | solution.py:25
  59.4 6.8 %collective-permute-start.23 = (bf16[128,1152]{1,0:T(8,128)(2,1)S(1)}, bf16[128,1152]{1,0:T(8,128)(2,1)S(1)}, u32[]{:S(2)}, u32[]{:S(2)}) collective-permute-start(bf16[128,1152]{1,0:T(8,128)(2,1)S(1)} %pad_maximum_fusion.2), channel_id=1, source_target_pairs={{0,28},{64,68},{4,0},{68,72},{8,4},{72,76},{12,8},{76,80},{16,12},... | collective-permute-start | bytes 884744 | tf_op jit(solution)/shard_map/ppermute | solution.py:25
  61.9 11.4 %collective-permute-start.18 = (bf16[256,1152]{1,0:T(8,128)(2,1)S(1)}, bf16[256,1152]{1,0:T(8,128)(2,1)S(1)}, u32[]{:S(2)}, u32[]{:S(2)}) collective-permute-start(bf16[256,1152]{1,0:T(8,128)(2,1)S(1)} %get-tuple-element.75), channel_id=1, source_target_pairs={{0,32},{64,66},{4,36},{68,70},{8,40},{72,74},{12,44},{76,78},{16,4... | collective-permute-start | bytes 1769480 | tf_op jit(solution)/shard_map/ppermute | solution.py:25
  66.3 9.7 %collective-permute-start.24 = (bf16[128,1152]{1,0:T(8,128)(2,1)S(1)}, bf16[128,1152]{1,0:T(8,128)(2,1)S(1)}, u32[]{:S(2)}, u32[]{:S(2)}) collective-permute-start(bf16[128,1152]{1,0:T(8,128)(2,1)S(1)} %fusion.1), channel_id=1, source_target_pairs={{0,28},{64,68},{4,0},{68,72},{8,4},{72,76},{12,8},{76,80},{16,12},... | collective-permute-start | bytes 884744 | tf_op jit(solution)/shard_map/ppermute | solution.py:25
  73.6 5.2 %collective-permute-start.19 = (bf16[64,1152]{1,0:T(8,128)(2,1)S(1)}, bf16[64,1152]{1,0:T(8,128)(2,1)S(1)}, u32[]{:S(2)}, u32[]{:S(2)}) collective-permute-start(bf16[64,1152]{1,0:T(8,128)(2,1)S(1)} %get-tuple-element.88), channel_id=1, source_target_pairs={{0,3},{64,224},{4,7},{68,228},{8,11},{72,232},{12,15},{76,236},{16... | collective-permute-start | bytes 442376 | tf_op jit(solution)/shard_map/ppermute | solution.py:25
  74.3 6.7 %collective-permute-start.21 = (bf16[64,1152]{1,0:T(8,128)(2,1)S(1)}, bf16[64,1152]{1,0:T(8,128)(2,1)S(1)}, u32[]{:S(2)}, u32[]{:S(2)}) collective-permute-start(bf16[64,1152]{1,0:T(8,128)(2,1)S(1)} %get-tuple-element.89), channel_id=1, source_target_pairs={{0,2},{64,96},{4,6},{68,100},{8,10},{72,104},{12,14},{76,108},{16,... | collective-permute-start | bytes 442376 | tf_op jit(solution)/shard_map/ppermute | solution.py:25
  75.5 7.0 %collective-permute-start.20 = (bf16[64,1152]{1,0:T(8,128)(2,1)S(1)}, bf16[64,1152]{1,0:T(8,128)(2,1)S(1)}, u32[]{:S(2)}, u32[]{:S(2)}) collective-permute-start(bf16[64,1152]{1,0:T(8,128)(2,1)S(1)} %get-tuple-element.90), channel_id=1, source_target_pairs={{0,1},{64,192},{4,5},{68,196},{8,9},{72,200},{12,13},{76,204},{16,... | collective-permute-start | bytes 442376 | tf_op jit(solution)/shard_map/ppermute | solution.py:25
  76.0 9.0 %collective-permute-start.25 = (bf16[128,1152]{1,0:T(8,128)(2,1)S(1)}, bf16[128,1152]{1,0:T(8,128)(2,1)S(1)}, u32[]{:S(2)}, u32[]{:S(2)}) collective-permute-start(bf16[128,1152]{1,0:T(8,128)(2,1)S(1)} %fusion.3), channel_id=1, source_target_pairs={{0,28},{64,68},{4,0},{68,72},{8,4},{72,76},{12,8},{76,80},{16,12},... | collective-permute-start | bytes 884744 | tf_op jit(solution)/shard_map/ppermute | solution.py:25
  82.8 3.9 %copy-start.1 = (bf16[1152,1152]{1,0:T(8,128)(2,1)S(1)}, bf16[1152,1152]{1,0:T(8,128)(2,1)}, u32[]{:S(2)}) copy-start(bf16[1152,1152]{1,0:T(8,128)(2,1)} %param.11) | copy-start | bytes 7962628
  85.0 1.5 %collective-permute-start.26 = (bf16[64,1152]{1,0:T(8,128)(2,1)S(1)}, bf16[64,1152]{1,0:T(8,128)(2,1)S(1)}, u32[]{:S(2)}, u32[]{:S(2)}) collective-permute-start(bf16[64,1152]{1,0:T(8,128)(2,1)S(1)} %slice.89), channel_id=1, source_target_pairs={{0,64},{64,0},{4,68},{68,4},{8,72},{72,8},{12,76},{76,12},{16,80},... | collective-permute-start | bytes 442376 | tf_op jit(solution)/shard_map/ppermute | solution.py:25
